TPU v7x, 32 devices: a whole 2x2x4 slice. The times are simulated.
32 devices in a mesh: dp: 4 (over x, core), seq: 8 (over z, y).
Axes of the slice: x: 2, y: 2, z: 4, core: 2. Of those that a mesh axis runs over, the one named last changes fastest.
Arguments:
- inputs: bfloat16 [4, 2048, 2048], P('dp', 'seq'), may hold values from -6 to 6
- reset: int32 [4, 2048], P('dp', 'seq'), may hold values 0 or 1
- initial_state: float32 [4, 2560], P('dp', 'seq'), may hold values from -6 to 6
- cotangent: bfloat16 [4, 2048, 2048], P('dp', 'seq'), may hold values from -6 to 6
- norm1_gain: bfloat16 [2048], P(('dp', 'seq')), may hold values from 0.5 to 1.5
- w_gate: bfloat16 [2048, 2560], P(('dp', 'seq')), may hold values from -0.125 to 0.125
- w_in: bfloat16 [2048, 2560], P(('dp', 'seq')), may hold values from -0.125 to 0.125
- conv_w: bfloat16 [4, 2560], P(None, ('dp', 'seq')), may hold values from -3 to 3
- conv_bias: bfloat16 [2560], P(('dp', 'seq')), may hold values from -2 to 2
- w_rgate: bfloat16 [2560, 256], P(('dp', 'seq')), may hold values from -0.375 to 0.375
- rgate_bias: bfloat16 [2560], P(('dp', 'seq')), may hold values from -3 to 3
- w_igate: bfloat16 [2560, 256], P(('dp', 'seq')), may hold values from -0.375 to 0.375
- igate_bias: bfloat16 [2560], P(('dp', 'seq')), may hold values from -3 to 3
- decay_param: bfloat16 [2560], P(('dp', 'seq')), may hold values from 4 to 9
- w_out: bfloat16 [2560, 2048], P(('dp', 'seq')), may hold values from -0.5 to 0.5
- norm2_gain: bfloat16 [2048], P(('dp', 'seq')), may hold values from 0.5 to 1.5
- w_ffgate: bfloat16 [2048, 6144], P('dp', 'seq'), may hold values from -0.125 to 0.125
- w_ffup: bfloat16 [2048, 6144], P('dp', 'seq'), may hold values from -0.125 to 0.125
- w_ffdown: bfloat16 [6144, 2048], P('seq', 'dp'), may hold values from -0.15625 to 0.15625
Outputs:
- output: bfloat16 [4, 2048, 2048], P('dp', 'seq')
- input_grad: float32 [4, 2048, 2048], P('dp', 'seq')
- final_state: float32 [4, 2560], P('dp', 'seq')
- grad_norm1: float32 [2048], P(('dp', 'seq'))
- grad_gate: float32 [2048, 2560], P(('dp', 'seq'))
- grad_in: float32 [2048, 2560], P(('dp', 'seq'))
- grad_conv: float32 [4, 2560], P(None, ('dp', 'seq'))
- grad_conv_bias: float32 [2560], P(('dp', 'seq'))
- grad_rgate: float32 [2560, 256], P(('dp', 'seq'))
- grad_rgate_bias: float32 [2560], P(('dp', 'seq'))
- grad_igate: float32 [2560, 256], P(('dp', 'seq'))
- grad_igate_bias: float32 [2560], P(('dp', 'seq'))
- grad_decay: float32 [2560], P(('dp', 'seq'))
- grad_out: float32 [2560, 2048], P(('dp', 'seq'))
- grad_norm2: float32 [2048], P(('dp', 'seq'))
- grad_ffgate: float32 [2048, 6144], P('dp', 'seq')
- grad_ffup: float32 [2048, 6144], P('dp', 'seq')
- grad_ffdown: float32 [6144, 2048], P('seq', 'dp')
Inputs may be any that keep to these rules, and one draw needn't show every extreme that they name: `reset`: 1 marks a token that begins a new document: the recurrence and the convolution read nothing before it.
All inputs are finite; a program needn't handle non-finite values. No bound on the sum of `reset` on one device may be relied on, other than what follows from the above.
Results may differ from a plain program's by a relative error of at most 0.0177.
Values may be sent and summed in bfloat16 or wider, within the bound.
A program may use at most 320 MiB of HBM per device.

v0:
```python
import jax
import jax.numpy as jnp
from jax import lax
from jax.sharding import PartitionSpec as P

HW = 256


epsilon = 1e-06
floor_value = 0.0001


def passed_along(value, axis, steps):
    count = lax.axis_size(axis)
    first, last = (max(0, -steps), min(count, count - steps))
    return lax.ppermute(value, axis, [(source, source + steps) for source in range(first, last)])


def gelu_tanh(values):
    return jax.nn.gelu(values, approximate=True)


def rms_parts(values, norm_gain):
    root_scale = lax.rsqrt(jnp.mean(values * values, axis=-1, keepdims=True) + epsilon)
    unit_rows = values * root_scale
    return (unit_rows * norm_gain, root_scale, unit_rows)


def norm_back(d_normed, norm_gain, root_scale, unit_rows):
    weighted = d_normed * norm_gain
    grad_gain = jnp.sum(d_normed * unit_rows, axis=0)
    d_values = root_scale * (
        weighted - unit_rows * jnp.mean(weighted * unit_rows, axis=-1, keepdims=True)
    )
    return (grad_gain, d_values)


def rows_of(values, first_row, row_count):
    return lax.slice_in_dim(values, first_row, first_row + row_count, axis=values.ndim - 2)


def gate_math(rate_pre, input_pre, conv_vals, decay_param, reset_col):
    rate = jax.nn.sigmoid(rate_pre)
    in_gate = jax.nn.sigmoid(input_pre)
    log_decay = -8.0 * jax.nn.softplus(-decay_param) * rate
    keep_mask = 1.0 - reset_col
    decay_rows = jnp.exp(log_decay) * keep_mask
    root_term = jnp.sqrt(jnp.maximum(-jnp.expm1(2.0 * log_decay), floor_value))
    drive_rows = (reset_col + keep_mask * root_term) * in_gate * conv_vals
    return (decay_rows, drive_rows)


def combine_linear(earlier, later):
    return (earlier[0] * later[0], later[0] * earlier[1] + later[1])


def feed_forward(normed_rows, cotan_rows, gate_slab, up_slab, down_slab):
    f32 = jnp.float32
    ff_gate = jnp.dot(normed_rows, gate_slab, preferred_element_type=f32)
    ff_up = jnp.dot(normed_rows, up_slab, preferred_element_type=f32)
    ff_act, ff_back = jax.vjp(gelu_tanh, ff_gate)
    hidden = (ff_act * ff_up).astype(jnp.bfloat16)
    out_part = jnp.dot(hidden, down_slab, preferred_element_type=f32)
    d_hidden = jnp.dot(cotan_rows, down_slab.T, preferred_element_type=f32)
    d_ffgate = ff_back(d_hidden * ff_up)[0].astype(jnp.bfloat16)
    d_ffup = (d_hidden * ff_act).astype(jnp.bfloat16)
    grad_gate_part = jnp.dot(normed_rows.T, d_ffgate, preferred_element_type=f32)
    grad_up_part = jnp.dot(normed_rows.T, d_ffup, preferred_element_type=f32)
    grad_down_part = jnp.dot(hidden.T, cotan_rows, preferred_element_type=f32)
    d_normed_part = jnp.dot(d_ffgate, gate_slab.T, preferred_element_type=f32) + jnp.dot(
        d_ffup, up_slab.T, preferred_element_type=f32
    )
    return (out_part, d_normed_part, grad_gate_part, grad_up_part, grad_down_part)


def per_device(
    inputs,
    reset,
    initial_state,
    cotangent,
    norm1_gain,
    w_gate,
    w_in,
    conv_w,
    conv_bias,
    w_rgate,
    rgate_bias,
    w_igate,
    igate_bias,
    decay_param,
    w_out,
    norm2_gain,
    w_ffgate,
    w_ffup,
    w_ffdown,
):
    gathered = (
        lax.all_gather(norm1_gain, ("dp", "seq"), axis=0, tiled=True),
        lax.all_gather(w_gate, ("dp", "seq"), axis=0, tiled=True),
        lax.all_gather(w_in, ("dp", "seq"), axis=0, tiled=True),
        lax.all_gather(conv_w, ("dp", "seq"), axis=1, tiled=True),
        lax.all_gather(conv_bias, ("dp", "seq"), axis=0, tiled=True),
        lax.all_gather(w_rgate, ("dp", "seq"), axis=0, tiled=True),
        lax.all_gather(rgate_bias, ("dp", "seq"), axis=0, tiled=True),
        lax.all_gather(w_igate, ("dp", "seq"), axis=0, tiled=True),
        lax.all_gather(igate_bias, ("dp", "seq"), axis=0, tiled=True),
        lax.all_gather(decay_param, ("dp", "seq"), axis=0, tiled=True),
        lax.all_gather(w_out, ("dp", "seq"), axis=0, tiled=True),
        lax.all_gather(norm2_gain, ("dp", "seq"), axis=0, tiled=True),
    )
    (
        full_norm1,
        full_gate,
        full_in,
        full_conv,
        full_cbias,
        full_rgate,
        full_rbias,
        full_igate,
        full_ibias,
        full_decay,
        full_out,
        full_norm2,
    ) = gathered
    slab_gate, slab_up, slab_down = (
        lax.all_gather(w_ffgate, "dp", axis=0, tiled=True),
        lax.all_gather(w_ffup, "dp", axis=0, tiled=True),
        lax.all_gather(w_ffdown, "dp", axis=1, tiled=True),
    )
    seqs_here, len_here, width = inputs.shape
    rows_here = seqs_here * len_here
    channels = full_rgate.shape[0]
    head_count = channels // HW
    rim_rows = full_conv.shape[0] - 1
    f32 = jnp.float32
    bf16 = jnp.bfloat16
    token_rows = inputs.reshape(rows_here, width).astype(f32)
    normed_f, scale_one, unit_one = rms_parts(token_rows, full_norm1.astype(f32))
    normed = normed_f.astype(bf16)
    gate_pre = jnp.dot(normed, full_gate, preferred_element_type=f32)
    branch = (
        jnp.dot(normed, full_in, preferred_element_type=f32)
        .astype(bf16)
        .reshape(seqs_here, len_here, channels)
    )
    reset_flags = reset.astype(bf16)
    rim_branch, rim_flags = passed_along(
        (branch[:, len_here - rim_rows :], reset_flags[:, len_here - rim_rows :]), "seq", 1
    )
    padded = jnp.concatenate([rim_branch, branch], 1).astype(f32)
    open_pad = (1.0 - jnp.concatenate([rim_flags, reset_flags], 1).astype(f32))[..., None]
    conv_wf = full_conv.astype(f32)
    open_masks = [None]
    conv_total = full_cbias.astype(f32) + conv_wf[0] * rows_of(padded, rim_rows, len_here)
    running = rows_of(open_pad, rim_rows, len_here)
    for offset in range(1, rim_rows + 1):
        if offset > 1:
            running = running * rows_of(open_pad, rim_rows + 1 - offset, len_here)
        open_masks.append(running)
        conv_total = conv_total + running * conv_wf[offset] * rows_of(
            padded, rim_rows - offset, len_here
        )
    conv_low = conv_total.astype(bf16).reshape(rows_here, channels)
    conv_f = conv_low.astype(f32)
    head_view = conv_low.reshape(rows_here, head_count, HW)
    rgate_blocks = full_rgate.reshape(head_count, HW, HW)
    igate_blocks = full_igate.reshape(head_count, HW, HW)
    rate_pre = jnp.einsum(
        "nhi,hij->nhj", head_view, rgate_blocks, preferred_element_type=f32
    ).reshape(rows_here, channels) + full_rbias.astype(f32)
    input_pre = jnp.einsum(
        "nhi,hij->nhj", head_view, igate_blocks, preferred_element_type=f32
    ).reshape(rows_here, channels) + full_ibias.astype(f32)
    reset_col = reset.astype(f32).reshape(rows_here, 1)
    decay_f = full_decay.astype(f32)

    def gate_local(rate_in, input_in, conv_in, decay_in):
        return gate_math(rate_in, input_in, conv_in, decay_in, reset_col)

    (decay_rows, drive_rows), gate_grad_fn = jax.vjp(
        gate_local, rate_pre, input_pre, conv_f, decay_f
    )
    decay_ch, drive_ch = (
        lax.all_to_all(
            decay_rows.reshape(seqs_here, len_here, channels),
            "seq",
            split_axis=2,
            concat_axis=1,
            tiled=True,
        ),
        lax.all_to_all(
            drive_rows.reshape(seqs_here, len_here, channels),
            "seq",
            split_axis=2,
            concat_axis=1,
            tiled=True,
        ),
    )
    drive_ch = drive_ch.at[:, 0].add(decay_ch[:, 0] * initial_state)
    states = lax.associative_scan(combine_linear, (decay_ch, drive_ch), axis=1)[1]
    final_state = states[:, -1]
    prev_states = jnp.concatenate([initial_state[:, None, :], states[:, :-1]], 1)
    back_states = lax.all_to_all(
        states.astype(bf16), "seq", split_axis=1, concat_axis=2, tiled=True
    ).reshape(rows_here, channels)
    state_f = back_states.astype(f32)
    gate_act, gate_back = jax.vjp(gelu_tanh, gate_pre)
    mixed_rows = (state_f * gate_act).astype(bf16)
    residual = token_rows + jnp.dot(mixed_rows, full_out, preferred_element_type=f32)
    normed_two_f, scale_two, unit_two = rms_parts(residual, full_norm2.astype(f32))
    normed_two = normed_two_f.astype(bf16)
    cotan_rows = cotangent.reshape(rows_here, width)
    group_normed, group_cotan = (
        lax.all_gather(normed_two.reshape(seqs_here, len_here, width), "seq", axis=1, tiled=True),
        lax.all_gather(cotangent, "seq", axis=1, tiled=True),
    )
    group_len = group_normed.shape[1]
    group_rows = seqs_here * group_len
    out_part, d_normed_part, gate_part, up_part, down_part = feed_forward(
        group_normed.reshape(group_rows, width),
        group_cotan.reshape(group_rows, width),
        slab_gate,
        slab_up,
        slab_down,
    )
    ff_out, d_normed_two = (
        lax.psum_scatter(
            out_part.reshape(seqs_here, group_len, width).astype(jnp.bfloat16),
            "seq",
            scatter_dimension=1,
            tiled=True,
        ).astype(jnp.float32),
        lax.psum_scatter(
            d_normed_part.reshape(seqs_here, group_len, width).astype(jnp.bfloat16),
            "seq",
            scatter_dimension=1,
            tiled=True,
        ).astype(jnp.float32),
    )
    ff_out = ff_out.reshape(rows_here, width)
    d_normed_two = d_normed_two.reshape(rows_here, width)
    ff_grad_parts = (gate_part, up_part, down_part)
    result = residual + ff_out
    output = result.astype(bf16).reshape(seqs_here, len_here, width)
    grad_ffgate, grad_ffup, grad_ffdown = (
        lax.psum_scatter(
            ff_grad_parts[0].astype(jnp.bfloat16), "dp", scatter_dimension=0, tiled=True
        ).astype(jnp.float32),
        lax.psum_scatter(
            ff_grad_parts[1].astype(jnp.bfloat16), "dp", scatter_dimension=0, tiled=True
        ).astype(jnp.float32),
        lax.psum_scatter(
            ff_grad_parts[2].astype(jnp.bfloat16), "dp", scatter_dimension=1, tiled=True
        ).astype(jnp.float32),
    )
    grad_norm2, d_resid_norm = norm_back(d_normed_two, full_norm2.astype(f32), scale_two, unit_two)
    d_residual = cotan_rows.astype(f32) + d_resid_norm
    d_residual_low = d_residual.astype(bf16)
    grad_out = jnp.dot(mixed_rows.T, d_residual_low, preferred_element_type=f32)
    d_mixed = jnp.dot(d_residual_low, full_out.T, preferred_element_type=f32)
    d_state = (d_mixed * gate_act).astype(bf16).reshape(seqs_here, len_here, channels)
    d_gate_pre = gate_back(d_mixed * state_f)[0].astype(bf16)
    d_state_ch = lax.all_to_all(d_state, "seq", split_axis=2, concat_axis=1, tiled=True).astype(f32)
    next_decay = jnp.concatenate([decay_ch[:, 1:], jnp.zeros_like(decay_ch[:, :1])], 1)
    flipped = lax.associative_scan(
        combine_linear, (jnp.flip(next_decay, 1), jnp.flip(d_state_ch, 1)), axis=1
    )[1]
    carry_back = jnp.flip(flipped, 1)
    d_decay_ch = carry_back * prev_states
    d_decay_tok, d_drive_tok = (
        lax.all_to_all(
            d_decay_ch.astype(jnp.bfloat16), "seq", split_axis=1, concat_axis=2, tiled=True
        ).astype(d_decay_ch.dtype),
        lax.all_to_all(
            carry_back.astype(jnp.bfloat16), "seq", split_axis=1, concat_axis=2, tiled=True
        ).astype(carry_back.dtype),
    )
    d_rate_pre, d_input_pre, d_conv_direct, grad_decay = gate_grad_fn(
        (d_decay_tok.reshape(rows_here, channels), d_drive_tok.reshape(rows_here, channels))
    )
    d_rate_low = d_rate_pre.astype(bf16)
    d_input_low = d_input_pre.astype(bf16)
    d_rate_heads = d_rate_low.reshape(rows_here, head_count, HW)
    d_input_heads = d_input_low.reshape(rows_here, head_count, HW)
    grad_rgate = jnp.einsum(
        "nhi,nhj->hij", head_view, d_rate_heads, preferred_element_type=f32
    ).reshape(channels, HW)
    grad_igate = jnp.einsum(
        "nhi,nhj->hij", head_view, d_input_heads, preferred_element_type=f32
    ).reshape(channels, HW)
    grad_rbias = jnp.sum(d_rate_low.astype(f32), axis=0)
    grad_ibias = jnp.sum(d_input_low.astype(f32), axis=0)
    d_conv = d_conv_direct + jnp.einsum(
        "nhj,hij->nhi", d_rate_heads, rgate_blocks, preferred_element_type=f32
    ).reshape(rows_here, channels)
    d_conv = d_conv + jnp.einsum(
        "nhj,hij->nhi", d_input_heads, igate_blocks, preferred_element_type=f32
    ).reshape(rows_here, channels)
    d_conv_low = d_conv.astype(bf16).reshape(seqs_here, len_here, channels)
    rim_grad, rim_next = passed_along(
        (d_conv_low[:, :rim_rows], reset_flags[:, :rim_rows]), "seq", -1
    )
    grad_ext = jnp.concatenate([d_conv_low, rim_grad], 1).astype(f32)
    open_next = (1.0 - jnp.concatenate([reset_flags, rim_next], 1).astype(f32))[..., None]
    d_conv_f = rows_of(grad_ext, 0, len_here)
    d_branch = conv_wf[0] * d_conv_f
    ahead = None
    conv_grads = [jnp.sum(rows_of(padded, rim_rows, len_here) * d_conv_f, axis=(0, 1))]
    for offset in range(1, rim_rows + 1):
        ahead = (
            rows_of(open_next, offset, len_here)
            if offset == 1
            else ahead * rows_of(open_next, offset, len_here)
        )
        d_branch = d_branch + ahead * conv_wf[offset] * rows_of(grad_ext, offset, len_here)
        conv_grads.append(
            jnp.sum(
                open_masks[offset] * rows_of(padded, rim_rows - offset, len_here) * d_conv_f,
                axis=(0, 1),
            )
        )
    grad_conv = jnp.stack(conv_grads, 0)
    grad_cbias = jnp.sum(d_conv_f, axis=(0, 1))
    d_branch_low = d_branch.astype(bf16).reshape(rows_here, channels)
    grad_in = jnp.dot(normed.T, d_branch_low, preferred_element_type=f32)
    grad_gate = jnp.dot(normed.T, d_gate_pre, preferred_element_type=f32)
    d_normed_one = jnp.dot(d_branch_low, full_in.T, preferred_element_type=f32) + jnp.dot(
        d_gate_pre, full_gate.T, preferred_element_type=f32
    )
    grad_norm1, d_token_norm = norm_back(d_normed_one, full_norm1.astype(f32), scale_one, unit_one)
    input_grad = (d_residual + d_token_norm).reshape(seqs_here, len_here, width)
    branch_parts = (
        lax.psum_scatter(grad_norm1, ("dp", "seq"), scatter_dimension=0, tiled=True),
        lax.psum_scatter(grad_gate, ("dp", "seq"), scatter_dimension=0, tiled=True),
        lax.psum_scatter(grad_in, ("dp", "seq"), scatter_dimension=0, tiled=True),
        lax.psum_scatter(grad_conv, ("dp", "seq"), scatter_dimension=1, tiled=True),
        lax.psum_scatter(grad_cbias, ("dp", "seq"), scatter_dimension=0, tiled=True),
        lax.psum_scatter(grad_rgate, ("dp", "seq"), scatter_dimension=0, tiled=True),
        lax.psum_scatter(grad_rbias, ("dp", "seq"), scatter_dimension=0, tiled=True),
        lax.psum_scatter(grad_igate, ("dp", "seq"), scatter_dimension=0, tiled=True),
        lax.psum_scatter(grad_ibias, ("dp", "seq"), scatter_dimension=0, tiled=True),
        lax.psum_scatter(grad_decay, ("dp", "seq"), scatter_dimension=0, tiled=True),
        lax.psum_scatter(grad_out, ("dp", "seq"), scatter_dimension=0, tiled=True),
        lax.psum_scatter(grad_norm2, ("dp", "seq"), scatter_dimension=0, tiled=True),
    )
    return (
        (output, input_grad, final_state)
        + tuple(branch_parts)
        + (grad_ffgate, grad_ffup, grad_ffdown)
    )


def solution(mesh):
    return jax.shard_map(
        per_device,
        mesh=mesh,
        in_specs=(
            P("dp", "seq", None),
            P("dp", "seq"),
            P("dp", "seq"),
            P("dp", "seq", None),
            P(("dp", "seq")),
            P(("dp", "seq"), None),
            P(("dp", "seq"), None),
            P(None, ("dp", "seq")),
            P(("dp", "seq")),
            P(("dp", "seq"), None),
            P(("dp", "seq")),
            P(("dp", "seq"), None),
            P(("dp", "seq")),
            P(("dp", "seq")),
            P(("dp", "seq"), None),
            P(("dp", "seq")),
            P("dp", "seq"),
            P("dp", "seq"),
            P("seq", "dp"),
        ),
        out_specs=(
            P("dp", "seq", None),
            P("dp", "seq", None),
            P("dp", "seq"),
            P(("dp", "seq")),
            P(("dp", "seq"), None),
            P(("dp", "seq"), None),
            P(None, ("dp", "seq")),
            P(("dp", "seq")),
            P(("dp", "seq"), None),
            P(("dp", "seq")),
            P(("dp", "seq"), None),
            P(("dp", "seq")),
            P(("dp", "seq")),
            P(("dp", "seq"), None),
            P(("dp", "seq")),
            P("dp", "seq"),
            P("dp", "seq"),
            P("seq", "dp"),
        ),
        check_vma=False,
    )
```

profile of v0, /device:TPU:0, one launch (start us, length us, event | category | flops | bytes accessed | tf_op | source)
XLA Modules:
  0.0 5050.6 jit_solution(15601937087589803221)
XLA Ops:
  68.7 66.3 %all-gather.1 = bf16[32,80,4]{1,2,0:T(4,128)(2,1)S(1)} all-gather(bf16[1,80,4]{1,2,0:T(4,128)(2,1)} %bitcast.357), channel_id=1, replica_groups=mesh['dp'=4,'seq'=8] {'dp','seq'}, dimensions={0}, use_global_device_ids=true | all-gather | bytes 21120 | tf_op jit(solution)/shard_map/all_gather | solution.py:101
  163.9 49.1 all-gather.17.cloned.1.call-done
  244.1 98.3 %all-to-all-done = f32[1,256,2560]{1,0,2:T(1,128)} async-done(((f32[1,256,2560]{1,0,2:T(1,128)}), f32[1,256,2560]{1,0,2:T(1,128)}, u32[]{:S(2)}, u32[]{:S(2)}) %all-to-all-start) | async-done | bytes 2621472 | tf_op jit(solution)/shard_map/all_to_all | solution.py:191
  349.9 75.9 %all-to-all-done.1 = f32[1,256,2560]{1,0,2:T(1,128)S(1)} async-done(((f32[1,256,2560]{1,0,2:T(1,128)}), f32[1,256,2560]{1,0,2:T(1,128)S(1)}, u32[]{:S(2)}, u32[]{:S(2)}) %all-to-all-start.1) | async-done | bytes 2621472 | tf_op jit(solution)/shard_map/all_to_all | solution.py:184
  429.6 45.1 slice.731
  474.8 45.1 slice.653
  519.9 45.2 slice.652
  565.1 44.6 slice.655
  990.4 44.7 slice.650
  1134.9 47.9 pad.158
  1188.4 52.3 %pad.157 = f32[1,2048,320]{1,2,0:T(8,128)} pad(f32[1,1024,320]{1,2,0:T(8,128)} %pad_maximum_fusion, f32[]{:T(128)} %constant.57.clone.1), padding=0_0_0x0_1_1x0_0_0 | pad | bytes 3932164 | tf_op jit(solution)/shard_map/pad | solution.py:200
  1365.7 122.0 %all-gather.31.cloned.1.call-done = bf16[2048,2048]{1,0:T(8,128)(2,1)} async-done(((bf16[256,2048]{1,0:T(8,128)(2,1)}), bf16[2048,2048]{1,0:T(8,128)(2,1)}) %all-gather.31.cloned.1.call-update) | async-done | bytes 8388624 | tf_op jit(solution)/shard_map/all_gather | solution.py:214
  1546.2 126.9 %all-gather.29.cloned.1.call-done = bf16[1,2048,2048]{2,1,0:T(8,128)(2,1)} async-done(((bf16[1,256,2048]{2,1,0:T(8,128)(2,1)}), bf16[1,2048,2048]{2,1,0:T(8,128)(2,1)}) %all-gather.29.cloned.1.call-update) | async-done | bytes 8388624 | tf_op jit(solution)/shard_map/all_gather | solution.py:215
  1740.1 122.2 %reduce-scatter.16.cloned.1.call-done = bf16[1,256,2048]{2,1,0:T(8,128)(2,1)} async-done(((bf16[1,2048,2048]{2,1,0:T(8,128)(2,1)}), bf16[1,256,2048]{2,1,0:T(8,128)(2,1)}) %reduce-scatter.16.cloned.1.call-update) | async-done | bytes 1048592 | tf_op jit(solution)/shard_map/reduce_scatter | solution.py:233
  1864.9 149.4 %reduce-scatter.14.cloned.1.call-done = bf16[1,256,2048]{2,1,0:T(8,128)(2,1)} async-done(((bf16[1,2048,2048]{2,1,0:T(8,128)(2,1)}), bf16[1,256,2048]{2,1,0:T(8,128)(2,1)}) %reduce-scatter.14.cloned.1.call-update) | async-done | bytes 1048592 | tf_op jit(solution)/shard_map/reduce_scatter | solution.py:227
  2244.8 44.4 slice.740
  2729.1 44.8 slice.820
  2941.5 47.5 pad.179
  2989.0 52.5 %pad.180 = f32[1,2048,320]{1,2,0:T(8,128)} pad(f32[1,1024,320]{1,2,0:T(8,128)} %add.789, f32[]{:T(128)} %constant.57.clone.1), padding=0_0_0x1_0_1x0_0_0 | pad | bytes 3932164 | tf_op jit(solution)/shard_map/pad | solution.py:265
  3430.6 135.0 %reduce-scatter.22.cloned.1.call-done = f32[80,256]{1,0:T(8,128)} async-done(((f32[2560,256]{1,0:T(8,128)}), f32[80,256]{1,0:T(8,128)}) %reduce-scatter.22.cloned.1.call-update) | async-done | bytes 81936 | tf_op jit(solution)/shard_map/reduce_scatter | solution.py:338
  3565.6 139.3 %reduce-scatter.24.cloned.1.call-done = f32[80,256]{1,0:T(8,128)} async-done(((f32[2560,256]{1,0:T(8,128)}), f32[80,256]{1,0:T(8,128)}) %reduce-scatter.24.cloned.1.call-update) | async-done | bytes 81936 | tf_op jit(solution)/shard_map/reduce_scatter | solution.py:340
  3704.9 444.1 %reduce-scatter.26.cloned.1.call-done = f32[80,2048]{1,0:T(8,128)} async-done(((f32[2560,2048]{1,0:T(8,128)}), f32[80,2048]{1,0:T(8,128)}) %reduce-scatter.26.cloned.1.call-update) | async-done | bytes 655376 | tf_op jit(solution)/shard_map/reduce_scatter | solution.py:343
  4149.0 447.2 %reduce-scatter.18.cloned.1.call-done = f32[64,2560]{1,0:T(8,128)} async-done(((f32[2048,2560]{1,0:T(8,128)}), f32[64,2560]{1,0:T(8,128)}) %reduce-scatter.18.cloned.1.call-update) | async-done | bytes 655376 | tf_op jit(solution)/shard_map/reduce_scatter | solution.py:334
  4596.2 447.4 %reduce-scatter.20.cloned.1.call-done = f32[64,2560]{1,0:T(8,128)} async-done(((f32[2048,2560]{1,0:T(8,128)}), f32[64,2560]{1,0:T(8,128)}) %reduce-scatter.20.cloned.1.call-update) | async-done | bytes 655376 | tf_op jit(solution)/shard_map/reduce_scatter | solution.py:335
  (734 shorter events, 2096.5 us)
Async XLA Ops:
  7.2 128.2 %all-gather.13.cloned.1.call-start = ((), (), s32[]{:S(2)}) async-start(), calls=%async_computation.17 | async-start | bytes 10813440 | tf_op jit(solution)/shard_map/all_gather | solution.py:100
  7.9 149.0 %all-gather.15.cloned.1.call-start = ((), (), s32[]{:S(2)}) async-start(), calls=%async_computation.18 | async-start | bytes 1351680 | tf_op jit(solution)/shard_map/all_gather | solution.py:103
  8.7 204.3 %all-gather.17.cloned.1.call-start = ((), (), s32[]{:S(2)}) async-start(), calls=%async_computation.19 | async-start | bytes 1351680 | tf_op jit(solution)/shard_map/all_gather | solution.py:105
  9.4 1337.2 %all-gather.19.cloned.1.call-start = ((), (), s32[]{:S(2)}) async-start(), calls=%async_computation.20 | async-start | bytes 10813440 | tf_op jit(solution)/shard_map/all_gather | solution.py:99
  10.0 1346.2 %all-gather.21.cloned.1.call-start = ((), (), s32[]{:S(2)}) async-start(), calls=%async_computation.21 | async-start | bytes 10813440 | tf_op jit(solution)/shard_map/all_gather | solution.py:108
  10.9 124.4 %collective-permute-start.3 = (bf16[1,3]{1,0:T(2,128)(2,1)S(1)}, bf16[1,3]{1,0:T(2,128)(2,1)S(1)}, u32[]{:S(2)}, u32[]{:S(2)}) collective-permute-start(bf16[1,3]{1,0:T(2,128)(2,1)S(1)} %get-tuple-element.125), channel_id=1, source_target_pairs={{1,0},{2,1},{3,2},{4,3},{5,4},{6,5},{7,6},{9,8},{10,9},{11,10},{12... | collective-permute-start | bytes 26 | tf_op jit(solution)/shard_map/ppermute | solution.py:16
  12.2 123.2 %collective-permute-start.1 = (bf16[1,3]{1,0:T(2,128)(2,1)S(1)}, bf16[1,3]{1,0:T(2,128)(2,1)S(1)}, u32[]{:S(2)}, u32[]{:S(2)}) collective-permute-start(bf16[1,3]{1,0:T(2,128)(2,1)S(1)} %get-tuple-element.126), channel_id=1, source_target_pairs={{0,1},{1,2},{2,3},{3,4},{4,5},{5,6},{6,7},{8,9},{9,10},{10,11},{11... | collective-permute-start | bytes 26 | tf_op jit(solution)/shard_map/ppermute | solution.py:16
  235.3 107.1 %all-to-all-start = ((f32[1,256,2560]{1,0,2:T(1,128)}), f32[1,256,2560]{1,0,2:T(1,128)}, u32[]{:S(2)}, u32[]{:S(2)}) async-start(f32[1,256,2560]{1,0,2:T(1,128)} %copy.396), calls=%async_computation | async-start | bytes 5242880 | tf_op jit(solution)/shard_map/all_to_all | solution.py:191
  1296.0 191.7 %all-gather.31.cloned.1.call-start = ((), (), s32[]{:S(2)}) async-start(), calls=%async_computation.36 | async-start | bytes 9437184 | tf_op jit(solution)/shard_map/all_gather | solution.py:214
  1363.6 152.4 %all-gather.23.cloned.1.call-start = ((), (), s32[]{:S(2)}) async-start(), calls=%async_computation.22 | async-start | bytes 3932160 | tf_op jit(solution)/shard_map/all_gather | solution.py:126
  1364.4 181.8 %all-gather.27.cloned.1.call-start = ((), (), s32[]{:S(2)}) async-start(), calls=%async_computation.24 | async-start | bytes 3932160 | tf_op jit(solution)/shard_map/all_gather | solution.py:128
  1365.1 308.0 %all-gather.29.cloned.1.call-start = ((), (), s32[]{:S(2)}) async-start(), calls=%async_computation.26 | async-start | bytes 9437184 | tf_op jit(solution)/shard_map/all_gather | solution.py:215
  1365.7 496.7 %reduce-scatter.16.cloned.1.call-start = ((), (), s32[]{:S(2)}) async-start(), calls=%async_computation.27 | async-start | bytes 9437184 | tf_op jit(solution)/shard_map/reduce_scatter | solution.py:233
  1715.0 299.3 %reduce-scatter.14.cloned.1.call-start = ((), (), s32[]{:S(2)}) async-start(), calls=%async_computation.25 | async-start | bytes 9437184 | tf_op jit(solution)/shard_map/reduce_scatter | solution.py:227
  1726.5 1611.9 %reduce-scatter.32.cloned.1.call-start = ((), (), s32[]{:S(2)}) async-start(), calls=%async_computation.35 | async-start | bytes 3932160 | tf_op jit(solution)/shard_map/reduce_scatter | solution.py:252
  2053.8 185.6 %all-to-all-start.3 = ((bf16[8,2,40960]{2,1,0:T(2,128)(2,1)}), bf16[8,2,40960]{2,1,0:T(2,128)(2,1)}, u32[]{:S(2)}, u32[]{:S(2)}) async-start(bf16[8,2,40960]{2,1,0:T(2,128)(2,1)} %reshape.1657), calls=%async_computation.5 | async-start | bytes 2621440 | tf_op jit(solution)/shard_map/all_to_all | solution.py:263
  2058.1 1282.7 %reduce-scatter.30.cloned.1.call-start = ((), (), s32[]{:S(2)}) async-start(), calls=%async_computation.34 | async-start | bytes 3932160 | tf_op jit(solution)/shard_map/reduce_scatter | solution.py:249
  3177.3 165.9 %reduce-scatter.28.cloned.1.call-start = ((), (), s32[]{:S(2)}) async-start(), calls=%async_computation.33 | async-start | bytes 3932160 | tf_op jit(solution)/shard_map/reduce_scatter | solution.py:246
  3187.8 241.4 %reduce-scatter.34.cloned.1.call-start = ((), (), s32[]{:S(2)}) async-start(), calls=%async_computation.37 | async-start | bytes 1351680
  3289.0 276.6 %reduce-scatter.22.cloned.1.call-start = ((), (), s32[]{:S(2)}) async-start(), calls=%async_computation.30 | async-start | bytes 2703360 | tf_op jit(solution)/shard_map/reduce_scatter | solution.py:338
  3292.8 412.1 %reduce-scatter.24.cloned.1.call-start = ((), (), s32[]{:S(2)}) async-start(), calls=%async_computation.31 | async-start | bytes 2703360 | tf_op jit(solution)/shard_map/reduce_scatter | solution.py:340
  3296.7 852.3 %reduce-scatter.26.cloned.1.call-start = ((), (), s32[]{:S(2)}) async-start(), calls=%async_computation.32 | async-start | bytes 21626880 | tf_op jit(solution)/shard_map/reduce_scatter | solution.py:343
  3308.8 1287.4 %reduce-scatter.18.cloned.1.call-start = ((), (), s32[]{:S(2)}) async-start(), calls=%async_computation.28 | async-start | bytes 21626880 | tf_op jit(solution)/shard_map/reduce_scatter | solution.py:334
  3321.1 1722.5 %reduce-scatter.20.cloned.1.call-start = ((), (), s32[]{:S(2)}) async-start(), calls=%async_computation.29 | async-start | bytes 21626880 | tf_op jit(solution)/shard_map/reduce_scatter | solution.py:335
  (116 other events, 6305.0 us)
Sparse Core Ops, SparseCore 0:
  11.0 89.6 all-gather.12
  103.5 53.3 all-gather.14
  159.8 53.2 all-gather.16
  215.8 130.6 all-gather.18
  349.3 110.6 all-gather.20
  1297.5 29.8 all-gather.24
  1363.7 123.9 all-gather.30
  1489.3 26.6 all-gather.22
  1517.6 28.5 all-gather.26
  1548.1 124.9 all-gather.28
  1715.1 147.1 reduce-scatter.15
  1866.2 147.9 reduce-scatter.13
  2016.8 36.9 reduce-scatter.31
  2239.6 39.1 reduce-scatter.29
  3187.9 39.3 reduce-scatter.27
  3289.1 138.7 reduce-scatter.33
  3430.5 135.0 reduce-scatter.21
  3568.3 136.5 reduce-scatter.23
  3707.8 441.1 reduce-scatter.25
  4151.7 444.4 reduce-scatter.17
  4599.1 444.4 reduce-scatter.19
where the time goes:
time: 5070 us; the launch traced here: 5050 us
  waiting for transfers between devices  2430 us (48%)
  local copies, waits for them, and re-layouts  1900 us (37%)
  other arithmetic  293 us (6%)
  matrix products  213 us (4%)
  blocking collectives  153 us (3%)
    slice x67, local copies, waits for them, and re-layouts, per_device(): lax.associative_scan(combine_linear, (jnp.flip(next_decay, 1), jnp.flip(d...  667 us
    slice x62, local copies, waits for them, and re-layouts, per_device(): lax.associative_scan(combine_linear, (decay_ch, drive_ch), axis=1)[1]  589 us
    reduce_scatter x1, waiting for transfers between devices, per_device(): lax.psum_scatter(grad_in, ('dp', 'seq'), scatter_dimension=0, tiled=True)  447 us
    reduce_scatter x1, waiting for transfers between devices, per_device(): lax.psum_scatter(grad_gate, ('dp', 'seq'), scatter_dimension=0, tiled=True)  447 us
    reduce_scatter x1, waiting for transfers between devices, per_device(): lax.psum_scatter(grad_out, ('dp', 'seq'), scatter_dimension=0, tiled=True)  444 us
    pad x20, local copies, waits for them, and re-layouts, per_device(): lax.associative_scan(combine_linear, (jnp.flip(next_decay, 1), jnp.flip(d...  209 us
    pad x20, local copies, waits for them, and re-layouts, per_device(): lax.associative_scan(combine_linear, (decay_ch, drive_ch), axis=1)[1]  188 us
    reduce_scatter x1, waiting for transfers between devices, per_device(): lax.psum_scatter(out_part.reshape(seqs_here, group_len, width).astype(jnp...  149 us
  transfers between devices with their start and end apart: 31, of which 17 were waited for; matrix products, arithmetic and copies ran while one was open for 46% of the time, Pallas kernels for 0%

commit v1 on v0

v1 whole, which is shorter than its diff:
```python
import functools

import jax
import jax.numpy as jnp
from jax import lax
from jax.experimental import pallas as pl
from jax.experimental.pallas import tpu as pltpu
from jax.sharding import PartitionSpec as P

HW = 256
LANES = 8


epsilon = 1e-06
floor_value = 0.0001
f32 = jnp.float32
bf16 = jnp.bfloat16


def seq_order(count):
    if count % 8:
        return list(range(count))
    wide = count // 4
    path = []
    for z in range(4):
        ys = range(1, wide) if z % 2 == 0 else range(wide - 1, 0, -1)
        path += [z * wide + y for y in ys]
    return path + [z * wide for z in (3, 2, 1, 0)]


class Ring:
    def __init__(self, axis, cycles):
        self.axis = axis
        self.cycles = cycles
        self.count = len(cycles[0])

    def shift(self, value, step):
        pairs = [
            (cycle[i], cycle[(i + step) % self.count])
            for cycle in self.cycles
            for i in range(self.count)
        ]
        return lax.ppermute(value, self.axis, pairs)

    def place(self):
        table = [0] * (self.count * len(self.cycles))
        for cycle in self.cycles:
            for i, device in enumerate(cycle):
                table[device] = i
        return jnp.asarray(table, jnp.int32)[lax.axis_index(self.axis)]

    def gather(self, value):
        count, half = self.count, self.count // 2
        blocks = [value] * count
        if count == 1:
            return blocks
        ahead = behind = value
        for step in range(1, half):
            behind = self.shift(behind, 1)
            ahead = self.shift(ahead, -1)
            blocks[count - step] = behind
            blocks[step] = ahead
        rows = value.shape[0]
        if half > 1 and rows % 32 == 0:
            top = self.shift(behind[: rows // 2], 1)
            bottom = self.shift(ahead[rows // 2 :], -1)
            blocks[half] = jnp.concatenate([top, bottom], 0)
        else:
            blocks[half] = self.shift(behind, 1)
        return blocks

    def scatter(self, part):
        count, half = self.count, self.count // 2
        if count == 1:
            return part(0).astype(f32)
        far = part(half).astype(bf16)
        if half == 1:
            return part(0).astype(f32) + self.shift(far, 1).astype(f32)
        rows = far.shape[0]
        cut = rows // 2 if rows % 32 == 0 else rows
        ahead, behind = far[:cut], far[cut:]
        for k in range(half - 1, 0, -1):
            got_ahead = self.shift(ahead, 1).astype(f32)
            mine_ahead = part(k).astype(f32)
            mine_behind = part(count - k).astype(f32)
            if k == half - 1 and cut == rows:
                ahead = (mine_ahead + got_ahead).astype(bf16)
                behind = mine_behind.astype(bf16)
                continue
            got_behind = self.shift(behind, -1).astype(f32)
            if k == half - 1:
                ahead = jnp.concatenate([mine_ahead[:cut] + got_ahead, mine_ahead[cut:]], 0)
                behind = jnp.concatenate([mine_behind[:cut], mine_behind[cut:] + got_behind], 0)
            else:
                ahead = mine_ahead + got_ahead
                behind = mine_behind + got_behind
            ahead, behind = ahead.astype(bf16), behind.astype(bf16)
        return (
            part(0).astype(f32)
            + self.shift(ahead, 1).astype(f32)
            + self.shift(behind, -1).astype(f32)
        )


class Net:
    def __init__(self):
        self.seq_count = lax.axis_size("seq")
        self.dp_count = lax.axis_size("dp")
        self.order = seq_order(self.seq_count)
        self.seq = Ring("seq", [self.order])
        self.cores = 2 if self.dp_count % 2 == 0 else 1
        self.chips = self.dp_count // self.cores
        cores, chips = self.cores, self.chips
        self.chip = Ring("dp", [[o * cores + c for o in range(chips)] for c in range(cores)])
        self.core = Ring("dp", [[o * cores + c for c in range(cores)] for o in range(chips)])
        self.place = self.seq.place()
        dp = lax.axis_index("dp")
        self.my_chip, self.my_core = dp // cores, dp % cores

    def seq_at(self, k):
        return jnp.asarray(self.order, jnp.int32)[(self.place + k) % self.seq_count]

    def rel(self):
        return [(c, k) for c in range(self.cores) for k in range(self.chips)]

    def dp_at(self, c, k):
        return ((self.my_chip + k) % self.chips) * self.cores + (self.my_core + c) % self.cores

    def columns_out(self, values):
        chunk = values.shape[1] // self.dp_count
        return jnp.concatenate(
            [lax.dynamic_slice_in_dim(values, self.dp_at(c, k) * chunk, chunk, 1) for c, k in self.rel()],
            1,
        )

    def columns_back(self, values):
        chunk = values.shape[1] // self.dp_count
        pieces = []
        for dp in range(self.dp_count):
            chip, core = dp // self.cores, dp % self.cores
            at = ((core - self.my_core) % self.cores) * self.chips + (chip - self.my_chip) % self.chips
            pieces.append(lax.dynamic_slice_in_dim(values, at * chunk, chunk, 1))
        return jnp.concatenate(pieces, 1)

    def gather_dp(self, value):
        blocks = self.chip.gather(value)
        if self.cores == 1:
            return blocks
        return blocks + [self.core.shift(block, 1) for block in blocks]

    def scatter_dp(self, part):
        sums = [part(0, k) for k in range(self.chips)]
        if self.cores > 1:
            sums = [
                mine.astype(f32) + self.core.shift(part(1, k).astype(bf16), 1).astype(f32)
                for k, mine in enumerate(sums)
            ]
        return self.chip.scatter(lambda k: sums[k])

    def gather_seq_placed(self, value):
        blocks = self.seq.gather(value)
        whole = jnp.zeros((self.seq_count,) + value.shape, value.dtype)
        for k, block in enumerate(blocks):
            whole = lax.dynamic_update_index_in_dim(whole, block, self.seq_at(k), 0)
        return whole

    def gather_all(self, value):
        return self.gather_dp(self.gather_seq_placed(value))

    def scatter_seq_placed(self, whole):
        return self.seq.scatter(
            lambda k: lax.dynamic_index_in_dim(whole, self.seq_at(k), 0, keepdims=False)
        )

    def scatter_all(self, part):
        return self.scatter_seq_placed(self.scatter_dp(part).astype(bf16))


def exchange(totals, everyone, send_sem, recv_sem, count):
    me = lax.axis_index("seq")
    everyone[me] = totals[...]
    copies = []
    for step in range(1, count):
        peer = lax.rem(me + step, count)
        copy = pltpu.make_async_remote_copy(
            src_ref=totals,
            dst_ref=everyone.at[me],
            send_sem=send_sem.at[step],
            recv_sem=recv_sem.at[step],
            device_id={"seq": peer},
            device_id_type=pl.DeviceIdType.MESH,
        )
        copy.start()
    for step in range(1, count):
        source = lax.rem(me + count - step, count)
        copy = pltpu.make_async_remote_copy(
            src_ref=totals,
            dst_ref=everyone.at[source],
            send_sem=send_sem.at[step],
            recv_sem=recv_sem.at[step],
            device_id={"seq": source},
            device_id_type=pl.DeviceIdType.MESH,
        )
        copy.wait()


def greet(count):
    me = lax.axis_index("seq")
    barrier = pltpu.get_barrier_semaphore()
    for step in range(1, count):
        pl.semaphore_signal(
            barrier,
            inc=1,
            device_id={"seq": lax.rem(me + step, count)},
            device_id_type=pl.DeviceIdType.MESH,
        )
    pl.semaphore_wait(barrier, count - 1)


def tiles(channels):
    wide = 512 if channels % 512 == 0 else 128
    return [pl.ds(at, wide) for at in range(0, channels, wide)]


def tile_prefix(product, total, step):
    row = lax.broadcasted_iota(jnp.int32, product.shape, 0)
    reach = 1
    while reach < LANES:
        turn = reach if step > 0 else LANES - reach
        inside = row >= reach if step > 0 else row < LANES - reach
        total = total + product * jnp.where(inside, pltpu.roll(total, turn, 0), 0.0)
        product = product * jnp.where(inside, pltpu.roll(product, turn, 0), 1.0)
        reach *= 2
    return (product, total)


def scan_kernel(
    count, decay_ref, drive_ref, start_ref, state_ref, prev_ref, last_ref,
    totals, everyone, send_sem, recv_sem,
):
    greet(count)
    rows, channels = decay_ref.shape
    end = LANES - 1
    for cols in tiles(channels):

        def first_pass(t, carry):
            run_product, run_sum = carry
            at = pl.ds(pl.multiple_of(t * LANES, LANES), LANES)
            product, total = tile_prefix(decay_ref[at, cols], drive_ref[at, cols], 1)
            prev_ref[at, cols] = product
            state_ref[at, cols] = total
            last = product[end:]
            return (last * run_product, last * run_sum + total[end:])

        zero = jnp.zeros((1, cols.size), f32)
        run_product, run_sum = lax.fori_loop(
            0, rows // LANES, first_pass, (zero + 1.0, zero), unroll=4
        )
        totals[0:1, cols] = run_product
        totals[1:2, cols] = run_sum
    exchange(totals, everyone, send_sem, recv_sem, count)
    me = lax.axis_index("seq")
    for cols in tiles(channels):
        state = start_ref[0:1, cols]
        entering = state
        for device in range(count):
            entering = jnp.where(me == device, state, entering)
            state = everyone[device, 0:1, cols] * state + everyone[device, 1:2, cols]
        last_ref[0:1, cols] = state

        def second_pass(t, entry):
            at = pl.ds(pl.multiple_of(t * LANES, LANES), LANES)
            state = prev_ref[at, cols] * entry + state_ref[at, cols]
            row = lax.broadcasted_iota(jnp.int32, state.shape, 0)
            state_ref[at, cols] = state
            prev_ref[at, cols] = jnp.where(row == 0, entry, pltpu.roll(state, 1, 0))
            return state[end:]

        lax.fori_loop(0, rows // LANES, second_pass, entering, unroll=4)


def scan_back_kernel(
    count, decay_ref, d_state_ref, prev_ref, d_drive_ref, d_decay_ref,
    totals, everyone, send_sem, recv_sem,
):
    greet(count)
    rows, channels = decay_ref.shape
    last_tile = rows // LANES - 1
    end = LANES - 1
    for cols in tiles(channels):

        def first_pass(i, carry):
            run_product, run_sum = carry
            at = pl.ds(pl.multiple_of((last_tile - i) * LANES, LANES), LANES)
            decay = decay_ref[at, cols]
            product, total = tile_prefix(decay, decay * d_state_ref[at, cols], -1)
            d_decay_ref[at, cols] = product
            d_drive_ref[at, cols] = total
            first = product[:1]
            return (first * run_product, first * run_sum + total[:1])

        zero = jnp.zeros((1, cols.size), f32)
        run_product, run_sum = lax.fori_loop(
            0, rows // LANES, first_pass, (zero + 1.0, zero), unroll=4
        )
        totals[0:1, cols] = run_product
        totals[1:2, cols] = run_sum
    exchange(totals, everyone, send_sem, recv_sem, count)
    me = lax.axis_index("seq")
    for cols in tiles(channels):
        state = jnp.zeros((1, cols.size), f32)
        entering = state
        for device in reversed(range(count)):
            entering = jnp.where(me == device, state, entering)
            state = everyone[device, 0:1, cols] * state + everyone[device, 1:2, cols]

        def second_pass(i, entry):
            at = pl.ds(pl.multiple_of((last_tile - i) * LANES, LANES), LANES)
            outgoing = d_decay_ref[at, cols] * entry + d_drive_ref[at, cols]
            row = lax.broadcasted_iota(jnp.int32, outgoing.shape, 0)
            incoming = jnp.where(row == end, entry, pltpu.roll(outgoing, end, 0))
            carry = d_state_ref[at, cols] + incoming
            d_drive_ref[at, cols] = carry
            d_decay_ref[at, cols] = carry * prev_ref[at, cols]
            return outgoing[:1]

        lax.fori_loop(0, rows // LANES, second_pass, entering, unroll=4)


def scan_call(kernel, collective_id, count, operands, out_shapes):
    channels = operands[0].shape[1]
    vmem = pl.BlockSpec(memory_space=pltpu.VMEM)
    return pl.pallas_call(
        functools.partial(kernel, count),
        out_shape=out_shapes,
        in_specs=[vmem] * len(operands),
        out_specs=[vmem] * len(out_shapes),
        scratch_shapes=[
            pltpu.VMEM((2, channels), f32),
            pltpu.VMEM((count, 2, channels), f32),
            pltpu.SemaphoreType.DMA((count,)),
            pltpu.SemaphoreType.DMA((count,)),
        ],
        compiler_params=pltpu.CompilerParams(
            collective_id=collective_id, has_side_effects=True, vmem_limit_bytes=40 * 2**20
        ),
        cost_estimate=pl.CostEstimate(
            flops=8 * operands[0].size, bytes_accessed=20 * operands[0].size, transcendentals=0
        ),
    )(*operands)


def passed_along(value, axis, steps):
    count = lax.axis_size(axis)
    first, last = (max(0, -steps), min(count, count - steps))
    return lax.ppermute(value, axis, [(source, source + steps) for source in range(first, last)])


def gelu_tanh(values):
    return jax.nn.gelu(values, approximate=True)


def rms_parts(values, norm_gain):
    root_scale = lax.rsqrt(jnp.mean(values * values, axis=-1, keepdims=True) + epsilon)
    unit_rows = values * root_scale
    return (unit_rows * norm_gain, root_scale, unit_rows)


def norm_back(d_normed, norm_gain, root_scale, unit_rows):
    weighted = d_normed * norm_gain
    grad_gain = jnp.sum(d_normed * unit_rows, axis=0)
    d_values = root_scale * (
        weighted - unit_rows * jnp.mean(weighted * unit_rows, axis=-1, keepdims=True)
    )
    return (grad_gain, d_values)


def rows_of(values, first_row, row_count):
    return lax.slice_in_dim(values, first_row, first_row + row_count, axis=values.ndim - 2)


def gate_math(rate_pre, input_pre, conv_vals, decay_param, reset_col):
    rate = jax.nn.sigmoid(rate_pre)
    in_gate = jax.nn.sigmoid(input_pre)
    log_decay = -8.0 * jax.nn.softplus(-decay_param) * rate
    keep_mask = 1.0 - reset_col
    decay_rows = jnp.exp(log_decay) * keep_mask
    root_term = jnp.sqrt(jnp.maximum(-jnp.expm1(2.0 * log_decay), floor_value))
    drive_rows = (reset_col + keep_mask * root_term) * in_gate * conv_vals
    return (decay_rows, drive_rows)


def dot(left, right):
    return jnp.dot(left, right, preferred_element_type=f32)


def dot_t(left, right):
    return lax.dot_general(left, right, (((1,), (1,)), ((), ())), preferred_element_type=f32)


def t_dot(left, right):
    return lax.dot_general(left, right, (((0,), (0,)), ((), ())), preferred_element_type=f32)


def total(terms):
    result = terms[0]
    for term in terms[1:]:
        result = result + term
    return result


def per_device(
    inputs,
    reset,
    initial_state,
    cotangent,
    norm1_gain,
    w_gate,
    w_in,
    conv_w,
    conv_bias,
    w_rgate,
    rgate_bias,
    w_igate,
    igate_bias,
    decay_param,
    w_out,
    norm2_gain,
    w_ffgate,
    w_ffup,
    w_ffdown,
):
    net = Net()
    seqs_here, len_here, width = inputs.shape
    assert seqs_here == 1
    rows_here = len_here
    dp_count, seq_count = net.dp_count, net.seq_count
    devices = dp_count * seq_count
    chan_here, channels = w_rgate.shape[0], w_rgate.shape[0] * devices
    wide_here = norm1_gain.shape[0]
    head_count = channels // HW
    taps = conv_w.shape[0]
    rim_rows = taps - 1
    rel = net.rel()

    vectors = [norm1_gain, norm2_gain, conv_w.reshape(-1), conv_bias, rgate_bias, igate_bias, decay_param]
    lengths = [v.shape[0] for v in vectors]
    flat = jnp.concatenate(vectors)
    small_rows = -(-flat.shape[0] // HW)
    flat = jnp.pad(flat, (0, small_rows * HW - flat.shape[0]))
    packed = jnp.concatenate([w_rgate, w_igate, flat.reshape(small_rows, HW)], 0)
    pack_blocks = net.gather_all(packed)
    pack_all = jnp.zeros((dp_count,) + pack_blocks[0].shape, bf16)
    for (c, k), block in zip(rel, pack_blocks):
        pack_all = lax.dynamic_update_index_in_dim(pack_all, block, net.dp_at(c, k), 0)
    pack_all = pack_all.reshape((devices,) + packed.shape)
    full_rgate = pack_all[:, :chan_here].reshape(channels, HW)
    full_igate = pack_all[:, chan_here : 2 * chan_here].reshape(channels, HW)
    flat_all = pack_all[:, 2 * chan_here :].reshape(devices, small_rows * HW)
    pieces, at = [], 0
    for length in lengths:
        pieces.append(flat_all[:, at : at + length])
        at += length
    full_norm1 = pieces[0].reshape(-1).astype(f32)
    full_norm2 = pieces[1].reshape(-1).astype(f32)
    conv_wf = pieces[2].reshape(devices, taps, chan_here).transpose(1, 0, 2).reshape(taps, channels).astype(f32)
    full_cbias, full_rbias, full_ibias, decay_f = (p.reshape(-1).astype(f32) for p in pieces[3:])
    start_state = net.gather_seq_placed(initial_state).reshape(1, channels)

    in_blocks = [
        b.reshape(seq_count * wide_here, 2 * channels)
        for b in net.gather_all(jnp.concatenate([w_in, w_gate], 1))
    ]
    out_blocks = [b.reshape(seq_count * chan_here, width) for b in net.gather_all(w_out)]
    slab_gate = jnp.concatenate(net.gather_dp(w_ffgate), 0)
    slab_up = jnp.concatenate(net.gather_dp(w_ffup), 0)
    slab_down = jnp.concatenate(net.gather_dp(w_ffdown), 1)
    cotan_rows = cotangent.reshape(rows_here, width)
    group_cotan = jnp.concatenate(net.seq.gather(net.columns_out(cotan_rows)), 0)

    token_rows = inputs.reshape(rows_here, width).astype(f32)
    normed_f, scale_one, unit_one = rms_parts(token_rows, full_norm1)
    normed = net.columns_out(normed_f.astype(bf16))
    step_cols = width // dp_count
    normed_parts = [normed[:, i * step_cols : (i + 1) * step_cols] for i in range(dp_count)]
    both = total([dot(n, w) for n, w in zip(normed_parts, in_blocks)])
    branch = both[:, :channels].astype(bf16)
    gate_pre = both[:, channels:]
    reset_flags = reset.reshape(rows_here).astype(bf16)
    rim_branch, rim_flags = passed_along(
        (branch[len_here - rim_rows :], reset_flags[len_here - rim_rows :]), "seq", 1
    )
    padded = jnp.concatenate([rim_branch, branch], 0).astype(f32)
    open_pad = (1.0 - jnp.concatenate([rim_flags, reset_flags], 0).astype(f32))[:, None]
    open_masks = [None]
    conv_total = full_cbias + conv_wf[0] * rows_of(padded, rim_rows, len_here)
    running = rows_of(open_pad, rim_rows, len_here)
    for offset in range(1, rim_rows + 1):
        if offset > 1:
            running = running * rows_of(open_pad, rim_rows + 1 - offset, len_here)
        open_masks.append(running)
        conv_total = conv_total + running * conv_wf[offset] * rows_of(
            padded, rim_rows - offset, len_here
        )
    conv_low = conv_total.astype(bf16)
    conv_f = conv_low.astype(f32)
    head_view = conv_low.reshape(rows_here, head_count, HW)
    rgate_blocks = full_rgate.reshape(head_count, HW, HW)
    igate_blocks = full_igate.reshape(head_count, HW, HW)
    rate_pre = (
        jnp.einsum("nhi,hij->nhj", head_view, rgate_blocks, preferred_element_type=f32).reshape(
            rows_here, channels
        )
        + full_rbias
    )
    input_pre = (
        jnp.einsum("nhi,hij->nhj", head_view, igate_blocks, preferred_element_type=f32).reshape(
            rows_here, channels
        )
        + full_ibias
    )
    reset_col = reset.astype(f32).reshape(rows_here, 1)

    def gate_local(rate_in, input_in, conv_in, decay_in):
        return gate_math(rate_in, input_in, conv_in, decay_in, reset_col)

    (decay_rows, drive_rows), gate_grad_fn = jax.vjp(
        gate_local, rate_pre, input_pre, conv_f, decay_f
    )
    row_shape = jax.ShapeDtypeStruct((rows_here, channels), f32)
    states, prev_states, last_state = scan_call(
        scan_kernel,
        0,
        seq_count,
        (decay_rows, drive_rows, start_state),
        [row_shape, row_shape, jax.ShapeDtypeStruct((1, channels), f32)],
    )
    final_here = initial_state.shape[1]
    final_state = lax.dynamic_slice_in_dim(
        last_state, lax.axis_index("seq") * final_here, final_here, 1
    )
    state_f = states.astype(bf16).astype(f32)
    gate_act, gate_back = jax.vjp(gelu_tanh, gate_pre)
    mixed_rows = net.columns_out((state_f * gate_act).astype(bf16))
    step_chan = channels // dp_count
    mixed_parts = [mixed_rows[:, i * step_chan : (i + 1) * step_chan] for i in range(dp_count)]
    residual = token_rows + total([dot(m, w) for m, w in zip(mixed_parts, out_blocks)])

    normed_two_f, scale_two, unit_two = rms_parts(residual, full_norm2)
    normed_two = net.columns_out(normed_two_f.astype(bf16))
    group_normed = jnp.concatenate(net.seq.gather(normed_two), 0)
    ff_gate = dot(group_normed, slab_gate)
    ff_up = dot(group_normed, slab_up)
    ff_act, ff_back = jax.vjp(gelu_tanh, ff_gate)
    hidden = (ff_act * ff_up).astype(bf16)
    d_hidden = dot_t(group_cotan, slab_down)
    d_ffgate = ff_back(d_hidden * ff_up)[0].astype(bf16)
    d_ffup = (d_hidden * ff_act).astype(bf16)
    d_normed_part = (dot_t(d_ffgate, slab_gate) + dot_t(d_ffup, slab_up)).astype(bf16)
    out_part = dot(hidden, slab_down).astype(bf16)

    def block_rows(whole):
        return lambda k: whole[k * rows_here : (k + 1) * rows_here]

    d_normed_two = net.columns_back(net.seq.scatter(block_rows(d_normed_part)))
    ff_out = net.columns_back(net.seq.scatter(block_rows(out_part)))
    gate_part = t_dot(group_normed, d_ffgate).astype(bf16)
    up_part = t_dot(group_normed, d_ffup).astype(bf16)
    down_part = t_dot(hidden, group_cotan).astype(bf16)

    def dp_chunk(whole, axis):
        size = whole.shape[axis] // dp_count
        return lambda c, k: lax.slice_in_dim(
            whole, (c * net.chips + k) * size, (c * net.chips + k + 1) * size, axis=axis
        )

    grad_ffgate = net.scatter_dp(dp_chunk(gate_part, 0))
    grad_ffup = net.scatter_dp(dp_chunk(up_part, 0))
    grad_ffdown = net.scatter_dp(dp_chunk(down_part, 1))
    output = (residual + ff_out).astype(bf16).reshape(seqs_here, len_here, width)

    grad_norm2, d_resid_norm = norm_back(d_normed_two, full_norm2, scale_two, unit_two)
    d_residual = cotan_rows.astype(f32) + d_resid_norm
    d_residual_low = d_residual.astype(bf16)
    d_mixed = net.columns_back(jnp.concatenate([dot_t(d_residual_low, w) for w in out_blocks], 1))
    d_state = (d_mixed * gate_act).astype(bf16)
    d_gate_pre = gate_back(d_mixed * state_f)[0].astype(bf16)
    d_drive, d_decay = scan_call(
        scan_back_kernel,
        1,
        seq_count,
        (decay_rows, d_state.astype(f32), prev_states),
        [row_shape, row_shape],
    )

    def grad_all(parts, right):
        return net.scatter_all(
            lambda c, k: t_dot(parts[c * net.chips + k], right)
            .astype(bf16)
            .reshape(seq_count, -1, right.shape[1])
        )

    grad_out = grad_all(mixed_parts, d_residual_low)
    grad_gate = grad_all(normed_parts, d_gate_pre)
    d_rate_pre, d_input_pre, d_conv_direct, grad_decay = gate_grad_fn((d_decay, d_drive))
    d_rate_low = d_rate_pre.astype(bf16)
    d_input_low = d_input_pre.astype(bf16)
    d_rate_heads = d_rate_low.reshape(rows_here, head_count, HW)
    d_input_heads = d_input_low.reshape(rows_here, head_count, HW)
    grad_rgate = jnp.einsum("nhi,nhj->hij", head_view, d_rate_heads, preferred_element_type=f32)
    grad_igate = jnp.einsum("nhi,nhj->hij", head_view, d_input_heads, preferred_element_type=f32)
    grad_rbias = jnp.sum(d_rate_low.astype(f32), axis=0)
    grad_ibias = jnp.sum(d_input_low.astype(f32), axis=0)
    d_conv = (
        d_conv_direct
        + jnp.einsum("nhj,hij->nhi", d_rate_heads, rgate_blocks, preferred_element_type=f32).reshape(
            rows_here, channels
        )
        + jnp.einsum("nhj,hij->nhi", d_input_heads, igate_blocks, preferred_element_type=f32).reshape(
            rows_here, channels
        )
    )
    d_conv_low = d_conv.astype(bf16)
    rim_grad, rim_next = passed_along((d_conv_low[:rim_rows], reset_flags[:rim_rows]), "seq", -1)
    grad_ext = jnp.concatenate([d_conv_low, rim_grad], 0).astype(f32)
    open_next = (1.0 - jnp.concatenate([reset_flags, rim_next], 0).astype(f32))[:, None]
    d_conv_f = rows_of(grad_ext, 0, len_here)
    d_branch = conv_wf[0] * d_conv_f
    ahead = None
    conv_grads = [jnp.sum(rows_of(padded, rim_rows, len_here) * d_conv_f, axis=0)]
    for offset in range(1, rim_rows + 1):
        step_open = rows_of(open_next, offset, len_here)
        ahead = step_open if offset == 1 else ahead * step_open
        d_branch = d_branch + ahead * conv_wf[offset] * rows_of(grad_ext, offset, len_here)
        conv_grads.append(
            jnp.sum(
                open_masks[offset] * rows_of(padded, rim_rows - offset, len_here) * d_conv_f,
                axis=0,
            )
        )
    grad_conv = jnp.stack(conv_grads, 0)
    grad_cbias = jnp.sum(d_conv_f, axis=0)
    d_branch_low = d_branch.astype(bf16)
    grad_in = grad_all(normed_parts, d_branch_low)
    d_both = jnp.concatenate([d_branch_low, d_gate_pre], 1)
    d_normed_one = net.columns_back(jnp.concatenate([dot_t(d_both, w) for w in in_blocks], 1))
    grad_norm1, d_token_norm = norm_back(d_normed_one, full_norm1, scale_one, unit_one)
    input_grad = (d_residual + d_token_norm).reshape(seqs_here, len_here, width)

    conv_flat = grad_conv.reshape(taps, devices, chan_here).transpose(1, 0, 2)
    flat_grads = jnp.concatenate(
        [
            v.reshape(devices, -1)
            for v in (grad_norm1, grad_norm2, conv_flat, grad_cbias, grad_rbias, grad_ibias, grad_decay)
        ],
        1,
    )
    flat_grads = jnp.pad(flat_grads, ((0, 0), (0, small_rows * HW - flat_grads.shape[1])))
    pack_grads = jnp.concatenate(
        [
            grad_rgate.astype(bf16).reshape(devices, chan_here, HW),
            grad_igate.astype(bf16).reshape(devices, chan_here, HW),
            flat_grads.astype(bf16).reshape(devices, small_rows, HW),
        ],
        1,
    ).reshape(dp_count, seq_count, 2 * chan_here + small_rows, HW)
    pack_mine = net.scatter_all(
        lambda c, k: lax.dynamic_index_in_dim(pack_grads, net.dp_at(c, k), 0, keepdims=False)
    )
    flat_mine = pack_mine[2 * chan_here :].reshape(-1)
    mine, at = [], 0
    for length in lengths:
        mine.append(flat_mine[at : at + length])
        at += length
    return (
        output,
        input_grad,
        final_state,
        mine[0],
        grad_gate,
        grad_in,
        mine[2].reshape(taps, chan_here),
        mine[3],
        pack_mine[:chan_here],
        mine[4],
        pack_mine[chan_here : 2 * chan_here],
        mine[5],
        mine[6],
        grad_out,
        mine[1],
        grad_ffgate,
        grad_ffup,
        grad_ffdown,
    )


def solution(mesh):
    split = ("dp", "seq")
    return jax.shard_map(
        per_device,
        mesh=mesh,
        in_specs=(
            P("dp", "seq", None),
            P("dp", "seq"),
            P("dp", "seq"),
            P("dp", "seq", None),
            P(split),
            P(split, None),
            P(split, None),
            P(None, split),
            P(split),
            P(split, None),
            P(split),
            P(split, None),
            P(split),
            P(split),
            P(split, None),
            P(split),
            P("dp", "seq"),
            P("dp", "seq"),
            P("seq", "dp"),
        ),
        out_specs=(
            P("dp", "seq", None),
            P("dp", "seq", None),
            P("dp", "seq"),
            P(split),
            P(split, None),
            P(split, None),
            P(None, split),
            P(split),
            P(split, None),
            P(split),
            P(split, None),
            P(split),
            P(split),
            P(split, None),
            P(split),
            P("dp", "seq"),
            P("dp", "seq"),
            P("seq", "dp"),
        ),
        check_vma=False,
    )
```

time: 5070 us -> 1270 us (0.25)
  waiting for transfers between devices: 2430 us -> 586 us
  local copies, waits for them, and re-layouts: 1900 us -> 169 us
  other arithmetic: 293 us -> 109 us
  blocking collectives: 153 us -> 0 us
  starting transfers between devices: 39.9 us -> 135 us
    reduce_scatter x10 -> x0, waiting for transfers between devices: 1880 us -> none  [the longest x1 447 us: per_device(): lax.psum_scatter(grad_in, ('dp', 'seq'), scatter_dimension=0, tiled=True)]
    slice x137 -> x25, local copies, waits for them, and re-layouts: 1260 us -> 14 us  [the longest x3 3.69 us: dp_chunk(): lax.slice_in_dim(whole, (c * net.chips + k) * size, (c * net.chips + k +...]
    ppermute x0 -> x130, waiting for transfers between devices: none -> 586 us  [shift(): return lax.ppermute(value, self.axis, pairs)]
    pad x40 -> x0, local copies, waits for them, and re-layouts: 397 us -> none  [the longest x20 209 us: per_device(): lax.associative_scan(combine_linear, (jnp.flip(next_decay, 1), jnp.flip(d...]
    all_gather x10 -> x0, waiting for transfers between devices: 339 us -> none  [the longest x1 127 us: per_device(): lax.all_gather(cotangent, 'seq', axis=1, tiled=True)]
    all_to_all x6 -> x0, waiting for transfers between devices: 205 us -> none  [the longest x1 98.3 us: per_device(): lax.all_to_all(drive_rows.reshape(seqs_here, len_here, channels), 'seq',...]
    ppermute x0 -> x130, starting transfers between devices: none -> 125 us  [shift(): return lax.ppermute(value, self.axis, pairs)]
    unnamed x5 -> x1, other arithmetic: 118 us -> 0.01 us
  transfers between devices with their start and end apart: 31 -> 134, of which waited for: 17 -> 56; matrix products, arithmetic and copies ran while one was open for 46% -> 23% of each run, Pallas kernels for 0% -> 1%
where the time goes in v1:
time: 1270 us; the launch traced here: 1260 us
  waiting for transfers between devices  586 us (46%)
  matrix products  209 us (16%)
  local copies, waits for them, and re-layouts  169 us (13%)
  starting transfers between devices  135 us (11%)
  other arithmetic  109 us (9%)
  between operations  25.3 us (2%)
  Pallas kernels  24.4 us (2%)
    ppermute x130, waiting for transfers between devices, shift(): return lax.ppermute(value, self.axis, pairs)  586 us
    ppermute x130, starting transfers between devices, shift(): return lax.ppermute(value, self.axis, pairs)  125 us
    dot_general x11, matrix products, dot(): return jnp.dot(left, right, preferred_element_type=f32)  69.4 us
    dot_general x11, matrix products, dot_t(): lax.dot_general(left, right, (((1,), (1,)), ((), ())), preferred_element_...  62.1 us
    dot_general x15, matrix products, t_dot(): lax.dot_general(left, right, (((0,), (0,)), ((), ())), preferred_element_...  58.5 us
    dynamic_update_slice x31, local copies, waits for them, and re-layouts, gather_seq_placed(): whole = lax.dynamic_update_index_in_dim(whole, block, self.seq_at(k), 0)  54 us
    unnamed x247, local copies, waits for them, and re-layouts  45.5 us
  transfers between devices with their start and end apart: 134, of which 56 were waited for; matrix products, arithmetic and copies ran while one was open for 23% of the time, Pallas kernels for 1%

profile of v1, /device:TPU:0, one launch (start us, length us, event | category | flops | bytes accessed | tf_op | source)
XLA Modules:
  0.0 1256.7 jit_solution(16591825338285619048)
XLA Ops:
  55.8 11.3 collective-permute-done.14
  70.1 11.9 collective-permute-done.15
  171.4 57.6 %collective-permute-done.48 = bf16[512,768]{1,0:T(8,128)(2,1)} collective-permute-done((bf16[512,768]{1,0:T(8,128)(2,1)S(1)}, bf16[512,768]{1,0:T(8,128)(2,1)}, u32[]{:S(2)}, u32[]{:S(2)}) %collective-permute-start.48) | collective-permute-done | bytes 786464 | tf_op jit(solution)/shard_map/ppermute | solution.py:43
  325.6 23.4 %collective-permute-done.37 = bf16[8,80,2048]{2,1,0:T(8,128)(2,1)} collective-permute-done((bf16[8,80,2048]{2,1,0:T(8,128)(2,1)}, bf16[8,80,2048]{2,1,0:T(8,128)(2,1)}, u32[]{:S(2)}, u32[]{:S(2)}) %collective-permute-start.37) | collective-permute-done | bytes 2621472 | tf_op jit(solution)/shard_map/ppermute | solution.py:43
  377.1 12.1 shard_map.907
  403.5 15.2 %collective-permute-done.66 = bf16[256,2048]{1,0:T(8,128)(2,1)S(1)} collective-permute-done((bf16[256,2048]{1,0:T(8,128)(2,1)}, bf16[256,2048]{1,0:T(8,128)(2,1)S(1)}, u32[]{:S(2)}, u32[]{:S(2)}) %collective-permute-start.66) | collective-permute-done | bytes 1048608 | tf_op jit(solution)/shard_map/ppermute | solution.py:43
  431.7 15.2 %collective-permute-done.70 = bf16[256,2048]{1,0:T(8,128)(2,1)S(1)} collective-permute-done((bf16[256,2048]{1,0:T(8,128)(2,1)S(1)}, bf16[256,2048]{1,0:T(8,128)(2,1)S(1)}, u32[]{:S(2)}, u32[]{:S(2)}) %collective-permute-start.70) | collective-permute-done | bytes 1048608 | tf_op jit(solution)/shard_map/ppermute | solution.py:43
  451.4 16.7 %collective-permute-done.40 = bf16[256,2048]{1,0:T(8,128)(2,1)S(1)} collective-permute-done((bf16[256,2048]{1,0:T(8,128)(2,1)S(1)}, bf16[256,2048]{1,0:T(8,128)(2,1)S(1)}, u32[]{:S(2)}, u32[]{:S(2)}) %collective-permute-start.40) | collective-permute-done | bytes 1048608 | tf_op jit(solution)/shard_map/ppermute | solution.py:43
  486.8 13.8 %collective-permute-done.41 = bf16[256,2048]{1,0:T(8,128)(2,1)S(1)} collective-permute-done((bf16[256,2048]{1,0:T(8,128)(2,1)S(1)}, bf16[256,2048]{1,0:T(8,128)(2,1)S(1)}, u32[]{:S(2)}, u32[]{:S(2)}) %collective-permute-start.41) | collective-permute-done | bytes 1048608 | tf_op jit(solution)/shard_map/ppermute | solution.py:43
  502.6 10.9 fusion.154
  514.1 11.0 collective-permute-done.45
  543.4 10.7 fusion.153
  554.1 17.9 %fusion.7 = (bf16[2048,768]{1,0:T(8,128)(2,1)}, bf16[2048,768]{1,0:T(8,128)(2,1)}, bf16[2048,768]{1,0:T(8,128)(2,1)S(1)}) fusion(f32[2048,768]{1,0:T(8,128)} %fusion.154, f32[2048,768]{1,0:T(8,128)} %fusion.153, bf16[2048,2048]{1,0:T(8,128)(2,1)} %constant_dynamic-update-slice_fusion.5, bf16[2048,768]{1,0:T(8,128)(2,1)S(1)} %constant_dynamic-update-slice_fusion.14), kind=kOutput, calls=%fused_computation.13 | convolution fusion | flops 6483345408 | bytes 33554432 | tf_op jit(solution)/shard_map/dot_general | solution.py:394
  630.9 13.7 %add_convert_fusion = bf16[2048,2048]{1,0:T(8,128)(2,1)} fusion(f32[2048,2048]{1,0:T(8,128)} %fusion.155, bf16[2048,768]{1,0:T(8,128)(2,1)} %get-tuple-element.53, bf16[2048,768]{1,0:T(8,128)(2,1)} %copy-done.76), kind=kOutput, calls=%fused_computation | convolution fusion | flops 6450839552 | bytes 31457280 | tf_op jit(solution)/shard_map/dot_general | solution.py:398
  664.0 22.1 %collective-permute-done.58 = bf16[256,2048]{1,0:T(8,128)(2,1)S(1)} collective-permute-done((bf16[256,2048]{1,0:T(8,128)(2,1)S(1)}, bf16[256,2048]{1,0:T(8,128)(2,1)S(1)}, u32[]{:S(2)}, u32[]{:S(2)}) %collective-permute-start.58) | collective-permute-done | bytes 1048608 | tf_op jit(solution)/shard_map/ppermute | solution.py:43
  691.1 17.4 %collective-permute-done.74 = bf16[256,2048]{1,0:T(8,128)(2,1)S(1)} collective-permute-done((bf16[256,2048]{1,0:T(8,128)(2,1)S(1)}, bf16[256,2048]{1,0:T(8,128)(2,1)S(1)}, u32[]{:S(2)}, u32[]{:S(2)}) %collective-permute-start.74) | collective-permute-done | bytes 1048608 | tf_op jit(solution)/shard_map/ppermute | solution.py:43
  713.3 17.7 %collective-permute-done.59 = bf16[256,2048]{1,0:T(8,128)(2,1)S(1)} collective-permute-done((bf16[256,2048]{1,0:T(8,128)(2,1)S(1)}, bf16[256,2048]{1,0:T(8,128)(2,1)S(1)}, u32[]{:S(2)}, u32[]{:S(2)}) %collective-permute-start.59) | collective-permute-done | bytes 1048608 | tf_op jit(solution)/shard_map/ppermute | solution.py:43
  735.4 16.1 %collective-permute-done.75 = bf16[256,2048]{1,0:T(8,128)(2,1)S(1)} collective-permute-done((bf16[256,2048]{1,0:T(8,128)(2,1)S(1)}, bf16[256,2048]{1,0:T(8,128)(2,1)S(1)}, u32[]{:S(2)}, u32[]{:S(2)}) %collective-permute-start.75) | collective-permute-done | bytes 1048608 | tf_op jit(solution)/shard_map/ppermute | solution.py:43
  760.1 13.0 %collective-permute-done.130 = bf16[512,768]{1,0:T(8,128)(2,1)S(1)} collective-permute-done((bf16[512,768]{1,0:T(8,128)(2,1)S(1)}, bf16[512,768]{1,0:T(8,128)(2,1)S(1)}, u32[]{:S(2)}, u32[]{:S(2)}) %collective-permute-start.130) | collective-permute-done | bytes 786464 | tf_op jit(solution)/shard_map/ppermute | solution.py:43
  806.8 16.5 %collective-permute-done.80 = bf16[256,2048]{1,0:T(8,128)(2,1)S(1)} collective-permute-done((bf16[256,2048]{1,0:T(8,128)(2,1)S(1)}, bf16[256,2048]{1,0:T(8,128)(2,1)S(1)}, u32[]{:S(2)}, u32[]{:S(2)}) %collective-permute-start.80) | collective-permute-done | bytes 1048608 | tf_op jit(solution)/shard_map/ppermute | solution.py:43
  862.1 12.3 shard_map.908
  1030.3 41.5 %collective-permute-done.95 = bf16[8,64,2560]{2,1,0:T(8,128)(2,1)} collective-permute-done((bf16[8,64,2560]{2,1,0:T(8,128)(2,1)}, bf16[8,64,2560]{2,1,0:T(8,128)(2,1)}, u32[]{:S(2)}, u32[]{:S(2)}) %collective-permute-start.95) | collective-permute-done | bytes 2621472 | tf_op jit(solution)/shard_map/ppermute | solution.py:43
  1077.7 50.3 %collective-permute-done.117 = bf16[8,80,2048]{2,1,0:T(8,128)(2,1)} collective-permute-done((bf16[8,80,2048]{2,1,0:T(8,128)(2,1)}, bf16[8,80,2048]{2,1,0:T(8,128)(2,1)}, u32[]{:S(2)}, u32[]{:S(2)}) %collective-permute-start.117) | collective-permute-done | bytes 2621472 | tf_op jit(solution)/shard_map/ppermute | solution.py:43
  1134.5 42.2 %collective-permute-done.106 = bf16[8,64,2560]{2,1,0:T(8,128)(2,1)} collective-permute-done((bf16[8,64,2560]{2,1,0:T(8,128)(2,1)}, bf16[8,64,2560]{2,1,0:T(8,128)(2,1)}, u32[]{:S(2)}, u32[]{:S(2)}) %collective-permute-start.106) | collective-permute-done | bytes 2621472 | tf_op jit(solution)/shard_map/ppermute | solution.py:43
  (762 shorter events, 741.1 us)
Async XLA Ops:
  8.9 109.0 %collective-permute-start.3 = (bf16[163,256]{1,0:T(8,128)(2,1)}, bf16[163,256]{1,0:T(8,128)(2,1)}, u32[]{:S(2)}, u32[]{:S(2)}) collective-permute-start(bf16[163,256]{1,0:T(8,128)(2,1)} %constant_dynamic-update-slice_fusion), channel_id=1, source_target_pairs={{1,3},{3,5},{5,7},{7,6},{6,4},{4,2},{2,0},{0,1},{9,11},{11,13},{13... | collective-permute-start | bytes 250376 | tf_op jit(solution)/shard_map/ppermute | solution.py:43
  11.9 108.0 %collective-permute-start = (bf16[163,256]{1,0:T(8,128)(2,1)}, bf16[163,256]{1,0:T(8,128)(2,1)}, u32[]{:S(2)}, u32[]{:S(2)}) collective-permute-start(bf16[163,256]{1,0:T(8,128)(2,1)} %constant_dynamic-update-slice_fusion), channel_id=1, source_target_pairs={{1,0},{3,1},{5,3},{7,5},{6,7},{4,6},{2,4},{0,2},{9,8},{11,9},{13,1... | collective-permute-start | bytes 250376 | tf_op jit(solution)/shard_map/ppermute | solution.py:43
  16.9 87.5 %collective-permute-start.82 = (bf16[3]{0:T(256)(128)(2,1)S(1)}, bf16[3]{0:T(256)(128)(2,1)}, u32[]{:S(2)}, u32[]{:S(2)}) collective-permute-start(bf16[3]{0:T(256)(128)(2,1)S(1)} %get-tuple-element.161), channel_id=1, source_target_pairs={{1,0},{2,1},{3,2},{4,3},{5,4},{6,5},{7,6},{9,8},{10,9},{11,10},{12... | collective-permute-start | bytes 26 | tf_op jit(solution)/shard_map/ppermute | solution.py:356
  95.9 190.2 %collective-permute-start.18 = (bf16[8,64,5120]{2,1,0:T(8,128)(2,1)}, bf16[8,64,5120]{2,1,0:T(8,128)(2,1)}, u32[]{:S(2)}, u32[]{:S(2)}) collective-permute-start(bf16[8,64,5120]{2,1,0:T(8,128)(2,1)} %bitcast_dynamic-update-slice_fusion), channel_id=1, source_target_pairs={{0,16},{16,0},{8,24},{24,8},{1,17},{17,1},{9,25},{25,9},{2,18},{18... | collective-permute-start | bytes 15728648 | tf_op jit(solution)/shard_map/ppermute | solution.py:43
  125.6 103.4 %collective-permute-start.48 = (bf16[512,768]{1,0:T(8,128)(2,1)S(1)}, bf16[512,768]{1,0:T(8,128)(2,1)}, u32[]{:S(2)}, u32[]{:S(2)}) collective-permute-start(bf16[512,768]{1,0:T(8,128)(2,1)S(1)} %copy-done.50), channel_id=1, source_target_pairs={{0,16},{16,0},{8,24},{24,8},{1,17},{17,1},{9,25},{25,9},{2,18},{18... | collective-permute-start | bytes 2359304 | tf_op jit(solution)/shard_map/ppermute | solution.py:43
  127.5 103.1 %collective-permute-start.49 = (bf16[512,768]{1,0:T(8,128)(2,1)S(1)}, bf16[512,768]{1,0:T(8,128)(2,1)}, u32[]{:S(2)}, u32[]{:S(2)}) collective-permute-start(bf16[512,768]{1,0:T(8,128)(2,1)S(1)} %copy-done.50), channel_id=1, source_target_pairs={{0,8},{8,0},{16,24},{24,16},{1,9},{9,1},{17,25},{25,17},{2,10},{10... | collective-permute-start | bytes 2359304 | tf_op jit(solution)/shard_map/ppermute | solution.py:43
  170.3 75.4 %collective-permute-start.51 = (bf16[512,768]{1,0:T(8,128)(2,1)}, bf16[512,768]{1,0:T(8,128)(2,1)S(1)}, u32[]{:S(2)}, u32[]{:S(2)}) collective-permute-start(bf16[512,768]{1,0:T(8,128)(2,1)} %param.101), channel_id=1, source_target_pairs={{0,16},{16,0},{8,24},{24,8},{1,17},{17,1},{9,25},{25,9},{2,18},{18... | collective-permute-start | bytes 2359304 | tf_op jit(solution)/shard_map/ppermute | solution.py:43
  171.3 77.4 %collective-permute-start.52 = (bf16[512,768]{1,0:T(8,128)(2,1)}, bf16[512,768]{1,0:T(8,128)(2,1)S(1)}, u32[]{:S(2)}, u32[]{:S(2)}) collective-permute-start(bf16[512,768]{1,0:T(8,128)(2,1)} %param.101), channel_id=1, source_target_pairs={{0,8},{8,0},{16,24},{24,16},{1,9},{9,1},{17,25},{25,17},{2,10},{10... | collective-permute-start | bytes 2359304 | tf_op jit(solution)/shard_map/ppermute | solution.py:43
  273.5 119.4 %collective-permute-start.65 = (bf16[256,2048]{1,0:T(8,128)(2,1)}, bf16[256,2048]{1,0:T(8,128)(2,1)}, u32[]{:S(2)}, u32[]{:S(2)}) collective-permute-start(bf16[256,2048]{1,0:T(8,128)(2,1)} %get-tuple-element.126), channel_id=1, source_target_pairs={{1,0},{3,1},{5,3},{7,5},{6,7},{4,6},{2,4},{0,2},{9,8},{11,9},{13,1... | collective-permute-start | bytes 3145736 | tf_op jit(solution)/shard_map/ppermute | solution.py:43
  275.7 117.3 %collective-permute-start.68 = (bf16[256,2048]{1,0:T(8,128)(2,1)}, bf16[256,2048]{1,0:T(8,128)(2,1)}, u32[]{:S(2)}, u32[]{:S(2)}) collective-permute-start(bf16[256,2048]{1,0:T(8,128)(2,1)} %get-tuple-element.126), channel_id=1, source_target_pairs={{1,3},{3,5},{5,7},{7,6},{6,4},{4,2},{2,0},{0,1},{9,11},{11,13},{13... | collective-permute-start | bytes 3145736 | tf_op jit(solution)/shard_map/ppermute | solution.py:43
  297.3 129.9 %collective-permute-start.50 = (bf16[512,768]{1,0:T(8,128)(2,1)}, bf16[512,768]{1,0:T(8,128)(2,1)S(1)}, u32[]{:S(2)}, u32[]{:S(2)}) collective-permute-start(bf16[512,768]{1,0:T(8,128)(2,1)} %collective-permute-done.48), channel_id=1, source_target_pairs={{0,8},{8,0},{16,24},{24,16},{1,9},{9,1},{17,25},{25,17},{2,10},{10... | collective-permute-start | bytes 2359304 | tf_op jit(solution)/shard_map/ppermute | solution.py:43
  349.6 71.1 %collective-permute-start.39 = (bf16[8,80,2048]{2,1,0:T(8,128)(2,1)}, bf16[8,80,2048]{2,1,0:T(8,128)(2,1)}, u32[]{:S(2)}, u32[]{:S(2)}) collective-permute-start(bf16[8,80,2048]{2,1,0:T(8,128)(2,1)} %collective-permute-done.37), channel_id=1, source_target_pairs={{0,8},{8,0},{16,24},{24,16},{1,9},{9,1},{17,25},{25,17},{2,10},{10... | collective-permute-start | bytes 7864328 | tf_op jit(solution)/shard_map/ppermute | solution.py:43
  614.1 73.9 %collective-permute-start.132 = (bf16[768,512]{1,0:T(8,128)(2,1)}, bf16[768,512]{1,0:T(8,128)(2,1)}, u32[]{:S(2)}, u32[]{:S(2)}) collective-permute-start(bf16[768,512]{1,0:T(8,128)(2,1)} %get-tuple-element.75), channel_id=1, source_target_pairs={{0,8},{8,0},{16,24},{24,16},{1,9},{9,1},{17,25},{25,17},{2,10},{10... | collective-permute-start | bytes 2359304 | tf_op jit(solution)/shard_map/ppermute | solution.py:43
  626.2 84.3 %collective-permute-start.129 = (bf16[512,768]{1,0:T(8,128)(2,1)}, bf16[512,768]{1,0:T(8,128)(2,1)}, u32[]{:S(2)}, u32[]{:S(2)}) collective-permute-start(bf16[512,768]{1,0:T(8,128)(2,1)} %get-tuple-element.77), channel_id=1, source_target_pairs={{0,8},{8,0},{16,24},{24,16},{1,9},{9,1},{17,25},{25,17},{2,10},{10... | collective-permute-start | bytes 2359304 | tf_op jit(solution)/shard_map/ppermute | solution.py:43
  627.3 105.0 %collective-permute-start.126 = (bf16[512,768]{1,0:T(8,128)(2,1)}, bf16[512,768]{1,0:T(8,128)(2,1)}, u32[]{:S(2)}, u32[]{:S(2)}) collective-permute-start(bf16[512,768]{1,0:T(8,128)(2,1)} %get-tuple-element.79), channel_id=1, source_target_pairs={{0,8},{8,0},{16,24},{24,16},{1,9},{9,1},{17,25},{25,17},{2,10},{10... | collective-permute-start | bytes 2359304 | tf_op jit(solution)/shard_map/ppermute | solution.py:43
  957.1 69.8 %collective-permute-start.93 = (bf16[8,64,2560]{2,1,0:T(8,128)(2,1)}, bf16[8,64,2560]{2,1,0:T(8,128)(2,1)}, u32[]{:S(2)}, u32[]{:S(2)}) collective-permute-start(bf16[8,64,2560]{2,1,0:T(8,128)(2,1)} %bitcast.94), channel_id=1, source_target_pairs={{0,8},{8,0},{16,24},{24,16},{1,9},{9,1},{17,25},{25,17},{2,10},{10... | collective-permute-start | bytes 7864328 | tf_op jit(solution)/shard_map/ppermute | solution.py:43
  1011.8 60.1 %collective-permute-start.95 = (bf16[8,64,2560]{2,1,0:T(8,128)(2,1)}, bf16[8,64,2560]{2,1,0:T(8,128)(2,1)}, u32[]{:S(2)}, u32[]{:S(2)}) collective-permute-start(bf16[8,64,2560]{2,1,0:T(8,128)(2,1)} %fusion.14), channel_id=1, source_target_pairs={{0,16},{16,0},{8,24},{24,8},{1,17},{17,1},{9,25},{25,9},{2,18},{18... | collective-permute-start | bytes 7864328 | tf_op jit(solution)/shard_map/ppermute | solution.py:43
  1015.7 60.6 %collective-permute-start.115 = (bf16[8,80,2048]{2,1,0:T(8,128)(2,1)}, bf16[8,80,2048]{2,1,0:T(8,128)(2,1)}, u32[]{:S(2)}, u32[]{:S(2)}) collective-permute-start(bf16[8,80,2048]{2,1,0:T(8,128)(2,1)} %bitcast.124), channel_id=1, source_target_pairs={{0,8},{8,0},{16,24},{24,16},{1,9},{9,1},{17,25},{25,17},{2,10},{10... | collective-permute-start | bytes 7864328 | tf_op jit(solution)/shard_map/ppermute | solution.py:43
  1016.3 116.7 %collective-permute-start.104 = (bf16[8,64,2560]{2,1,0:T(8,128)(2,1)}, bf16[8,64,2560]{2,1,0:T(8,128)(2,1)}, u32[]{:S(2)}, u32[]{:S(2)}) collective-permute-start(bf16[8,64,2560]{2,1,0:T(8,128)(2,1)} %bitcast.368), channel_id=1, source_target_pairs={{0,8},{8,0},{16,24},{24,16},{1,9},{9,1},{17,25},{25,17},{2,10},{10... | collective-permute-start | bytes 7864328 | tf_op jit(solution)/shard_map/ppermute | solution.py:43
  1022.3 105.7 %collective-permute-start.117 = (bf16[8,80,2048]{2,1,0:T(8,128)(2,1)}, bf16[8,80,2048]{2,1,0:T(8,128)(2,1)}, u32[]{:S(2)}, u32[]{:S(2)}) collective-permute-start(bf16[8,80,2048]{2,1,0:T(8,128)(2,1)} %fusion.8), channel_id=1, source_target_pairs={{0,16},{16,0},{8,24},{24,8},{1,17},{17,1},{9,25},{25,9},{2,18},{18... | collective-permute-start | bytes 7864328 | tf_op jit(solution)/shard_map/ppermute | solution.py:43
  1027.0 149.8 %collective-permute-start.106 = (bf16[8,64,2560]{2,1,0:T(8,128)(2,1)}, bf16[8,64,2560]{2,1,0:T(8,128)(2,1)}, u32[]{:S(2)}, u32[]{:S(2)}) collective-permute-start(bf16[8,64,2560]{2,1,0:T(8,128)(2,1)} %fusion.11), channel_id=1, source_target_pairs={{0,16},{16,0},{8,24},{24,8},{1,17},{17,1},{9,25},{25,9},{2,18},{18... | collective-permute-start | bytes 7864328 | tf_op jit(solution)/shard_map/ppermute | solution.py:43
  1075.6 106.1 %collective-permute-start.96 = (bf16[32,2560]{1,0:T(8,128)(2,1)S(1)}, bf16[32,2560]{1,0:T(8,128)(2,1)S(1)}, u32[]{:S(2)}, u32[]{:S(2)}) collective-permute-start(bf16[32,2560]{1,0:T(8,128)(2,1)S(1)} %get-tuple-element.105), channel_id=1, source_target_pairs={{1,3},{3,5},{5,7},{7,6},{6,4},{4,2},{2,0},{0,1},{9,11},{11,13},{13... | collective-permute-start | bytes 491528 | tf_op jit(solution)/shard_map/ppermute | solution.py:43
  1076.3 106.2 %collective-permute-start.100 = (bf16[32,2560]{1,0:T(8,128)(2,1)S(1)}, bf16[32,2560]{1,0:T(8,128)(2,1)S(1)}, u32[]{:S(2)}, u32[]{:S(2)}) collective-permute-start(bf16[32,2560]{1,0:T(8,128)(2,1)S(1)} %get-tuple-element.107), channel_id=1, source_target_pairs={{1,0},{3,1},{5,3},{7,5},{6,7},{4,6},{2,4},{0,2},{9,8},{11,9},{13,1... | collective-permute-start | bytes 491528 | tf_op jit(solution)/shard_map/ppermute | solution.py:43
  1133.1 94.8 %collective-permute-start.122 = (bf16[80,2048]{1,0:T(8,128)(2,1)S(1)}, bf16[80,2048]{1,0:T(8,128)(2,1)S(1)}, u32[]{:S(2)}, u32[]{:S(2)}) collective-permute-start(bf16[80,2048]{1,0:T(8,128)(2,1)S(1)} %get-tuple-element.92), channel_id=1, source_target_pairs={{1,0},{3,1},{5,3},{7,5},{6,7},{4,6},{2,4},{0,2},{9,8},{11,9},{13,1... | collective-permute-start | bytes 983048 | tf_op jit(solution)/shard_map/ppermute | solution.py:43
  (219 other events, 4028.0 us)

commit v2 on v1

--- a/solution.py
+++ b/solution.py
@@ -176,6 +176,250 @@
         return self.scatter_seq_placed(self.scatter_dp(part).astype(bf16))
 
 
+def lookup(table, index):
+    value = jnp.int32(table[0])
+    for i, entry in enumerate(table):
+        value = jnp.where(index == i, jnp.int32(entry), value)
+    return value
+
+
+class Links:
+    def __init__(self, order, chips, cores):
+        self.count, self.chips, self.cores = len(order), chips, cores
+        me, dp = lax.axis_index("seq"), lax.axis_index("dp")
+        count = self.count
+        place = [0] * count
+        for i, device in enumerate(order):
+            place[device] = i
+        self.seq_at = [
+            lookup([order[(place[d] + k) % count] for d in range(count)], me) for k in range(count)
+        ]
+        self.ring = ({"seq": self.seq_at[1]}, {"seq": self.seq_at[count - 1]})
+        chip, core = dp // cores, dp % cores
+        self.chip = [
+            {"dp": lax.rem(chip + step, chips) * cores + core} for step in range(1, chips)
+        ]
+        self.core = {"dp": chip * cores + (1 - core)} if cores == 2 else None
+
+    def greet(self):
+        barrier = pltpu.get_barrier_semaphore()
+        peers = list(self.ring) + self.chip + ([self.core] if self.cores == 2 else [])
+        for peer in peers:
+            pl.semaphore_signal(
+                barrier, inc=1, device_id=peer, device_id_type=pl.DeviceIdType.MESH
+            )
+        pl.semaphore_wait(barrier, len(peers))
+
+
+def remote(source, target, send_sem, recv_sem, peer):
+    return pltpu.make_async_remote_copy(
+        src_ref=source,
+        dst_ref=target,
+        send_sem=send_sem,
+        recv_sem=recv_sem,
+        device_id=peer,
+        device_id_type=pl.DeviceIdType.MESH,
+    )
+
+
+RING_FIRST, CHIP_FIRST, RING_ONLY = 0, 1, 2
+
+
+def gather_kernel(order, chips, cores, pieces, arrays, *refs):
+    ins, outs = refs[:arrays], refs[arrays : 2 * arrays]
+    own_sem, recv_sem, ring_sem, chip_sem, core_sem = refs[2 * arrays :]
+    links = Links(order, chips, cores)
+    count, half = links.count, links.count // 2
+    links.greet()
+
+    owns = [
+        pltpu.make_async_copy(ins[i], outs[i].at[0, links.seq_at[0]], own_sem.at[i])
+        for i in range(arrays)
+    ]
+    for copy in owns:
+        copy.start()
+    sent = []
+
+    def whole(p, r, k):
+        array, first, rows, _ = pieces[p]
+        place = outs[array].at[r, links.seq_at[k]]
+        return place if rows == ins[array].shape[0] else place.at[pl.ds(first, rows)]
+
+    def rows_in(p, r, k, first, rows):
+        return outs[pieces[p][0]].at[r, links.seq_at[k], pl.ds(pieces[p][1] + first, rows)]
+
+    def held(p, r, k):
+        array, first, rows, _ = pieces[p]
+        if r == 0 and k == 0:
+            return ins[array] if rows == ins[array].shape[0] else ins[array].at[pl.ds(first, rows)]
+        return whole(p, r, k)
+
+    def cut_of(p):
+        return pieces[p][2] // 32 * 16
+
+    def start(copy):
+        copy.start()
+        sent.append(copy)
+
+    def ring_copies(p, r, s):
+        cut, rows = cut_of(p), pieces[p][2]
+        if s < half - 1:
+            return [
+                remote(
+                    held(p, r, (count - s) % count), whole(p, r, (count - s) % count),
+                    ring_sem.at[p, r, 0, s], recv_sem.at[p, r, count - s - 1], links.ring[0],
+                ),
+                remote(
+                    held(p, r, s), whole(p, r, s),
+                    ring_sem.at[p, r, 1, s], recv_sem.at[p, r, s + 1], links.ring[1],
+                ),
+            ]
+        back = count - s
+        if not cut:
+            return [
+                remote(
+                    whole(p, r, back), whole(p, r, back),
+                    ring_sem.at[p, r, 0, s], recv_sem.at[p, r, half], links.ring[0],
+                )
+            ]
+        top, bottom = rows_in(p, r, back, 0, cut), rows_in(p, r, s, cut, rows - cut)
+        return [
+            remote(top, top, ring_sem.at[p, r, 0, s], recv_sem.at[p, r, half], links.ring[0]),
+            remote(
+                bottom, bottom, ring_sem.at[p, r, 1, s], recv_sem.at[p, r, count], links.ring[1]
+            ),
+        ]
+
+    def arrived(p, r, k):
+        cut, rows = cut_of(p), pieces[p][2]
+        if k == half and cut:
+            for part, sem in (((0, cut), half), ((cut, rows - cut), count)):
+                ref = rows_in(p, r, k, *part)
+                remote(ref, ref, ring_sem.at[p, r, 0, 0], recv_sem.at[p, r, sem], links.ring[0]).wait_recv()
+        else:
+            ref = whole(p, r, k)
+            remote(ref, ref, ring_sem.at[p, r, 0, 0], recv_sem.at[p, r, k], links.ring[0]).wait_recv()
+
+    def to_chips(p, k):
+        for step in range(1, chips):
+            start(
+                remote(
+                    held(p, 0, k), whole(p, chips - step, k),
+                    chip_sem.at[p, step - 1, k], recv_sem.at[p, chips - step, k], links.chip[step - 1],
+                )
+            )
+
+    def to_core(p, r, k):
+        if cores == 2:
+            start(
+                remote(
+                    held(p, r, k), whole(p, chips + r, k),
+                    core_sem.at[p, r, k], recv_sem.at[p, chips + r, k], links.core,
+                )
+            )
+
+    method = [piece[3] for piece in pieces]
+    everyone = range(len(pieces))
+
+    def planes(p):
+        return range(chips) if method[p] == CHIP_FIRST else range(1)
+
+    for p in everyone:
+        if method[p] != RING_ONLY:
+            to_chips(p, 0)
+        for copy in ring_copies(p, 0, 0):
+            start(copy)
+    for p in everyone:
+        if method[p] != RING_ONLY:
+            to_core(p, 0, 0)
+    for s in range(1, half + 1):
+        steps = sorted({count - s, s})
+        before = sorted({(count - s + 1) % count, s - 1})
+        for p in everyone:
+            for r in planes(p):
+                if r == 0 or s > 1:
+                    for k in steps:
+                        arrived(p, r, k)
+                    if s < half:
+                        for copy in ring_copies(p, r, s):
+                            start(copy)
+                    if method[p] == RING_FIRST:
+                        for k in steps:
+                            to_chips(p, k)
+                    if method[p] != RING_ONLY:
+                        for k in steps:
+                            to_core(p, r, k)
+        for p in everyone:
+            if method[p] == RING_FIRST:
+                for r in range(1, chips):
+                    for k in before:
+                        arrived_from_chip(links, whole(p, r, k), chip_sem.at[p, 0, 0], recv_sem.at[p, r, k])
+                        to_core(p, r, k)
+            if method[p] == CHIP_FIRST and s == 1:
+                for r in range(1, chips):
+                    arrived_from_chip(links, whole(p, r, 0), chip_sem.at[p, 0, 0], recv_sem.at[p, r, 0])
+                    for copy in ring_copies(p, r, 0):
+                        start(copy)
+                    to_core(p, r, 0)
+                for r in range(1, chips):
+                    for k in steps:
+                        arrived(p, r, k)
+                    if s < half:
+                        for copy in ring_copies(p, r, s):
+                            start(copy)
+                    for k in steps:
+                        to_core(p, r, k)
+    for p in everyone:
+        if method[p] == RING_FIRST:
+            for r in range(1, chips):
+                arrived_from_chip(links, whole(p, r, half), chip_sem.at[p, 0, 0], recv_sem.at[p, r, half])
+                to_core(p, r, half)
+    for p in everyone:
+        if method[p] != RING_ONLY and cores == 2:
+            for r in range(chips):
+                for k in range(count):
+                    arrived_from_chip(
+                        links, whole(p, chips + r, k), core_sem.at[p, r, k], recv_sem.at[p, chips + r, k]
+                    )
+    for copy in sent:
+        copy.wait_send()
+    for copy in owns:
+        copy.wait()
+
+
+def arrived_from_chip(links, ref, send_sem, recv_sem):
+    remote(ref, ref, send_sem, recv_sem, links.ring[0]).wait_recv()
+
+
+def gather_call(net, arrays, pieces):
+    chips, cores, count = net.chips, net.cores, net.seq_count
+    slots = chips * cores
+    only_ring = {piece[0] for piece in pieces if piece[3] == RING_ONLY}
+    anywhere = pl.BlockSpec(memory_space=pl.ANY)
+    return pl.pallas_call(
+        functools.partial(gather_kernel, net.order, chips, cores, pieces, len(arrays)),
+        out_shape=[
+            jax.ShapeDtypeStruct((1 if i in only_ring else slots, count) + v.shape, v.dtype)
+            for i, v in enumerate(arrays)
+        ],
+        in_specs=[anywhere] * len(arrays),
+        out_specs=[anywhere] * len(arrays),
+        scratch_shapes=[
+            pltpu.SemaphoreType.DMA((len(arrays),)),
+            pltpu.SemaphoreType.DMA((len(pieces), slots, count + 1)),
+            pltpu.SemaphoreType.DMA((len(pieces), chips, 2, count // 2)),
+            pltpu.SemaphoreType.DMA((len(pieces), max(chips - 1, 1), count)),
+            pltpu.SemaphoreType.DMA((len(pieces), chips, count)),
+        ],
+        compiler_params=pltpu.CompilerParams(
+            collective_id=3, has_side_effects=True, vmem_limit_bytes=32 * 2**20
+        ),
+        cost_estimate=pl.CostEstimate(
+            flops=0, bytes_accessed=slots * count * sum(v.size for v in arrays) * 4, transcendentals=0
+        ),
+    )(*arrays)
+
+
 def exchange(totals, everyone, send_sem, recv_sem, count):
     me = lax.axis_index("seq")
     everyone[me] = totals[...]
@@ -348,6 +592,222 @@
             flops=8 * operands[0].size, bytes_accessed=20 * operands[0].size, transcendentals=0
         ),
     )(*operands)
+
+
+def pair_slots(count):
+    half = count // 2
+    return [k for s in range(1, half) for k in (count - s, s)] + [half, 0]
+
+
+def gelu_parts(v):
+    root, cubic = 0.7978845608028654, 0.044715
+    curve = jnp.tanh(root * (v + cubic * v * v * v))
+    act = 0.5 * v * (1.0 + curve)
+    slope = 0.5 * (1.0 + curve) + 0.5 * v * (1.0 - curve * curve) * root * (
+        1.0 + 3.0 * cubic * v * v
+    )
+    return (act, slope)
+
+
+def contract(left, right, left_dim, right_dim):
+    return lax.dot_general(
+        left, right, (((left_dim,), (right_dim,)), ((), ())), preferred_element_type=f32
+    )
+
+
+def ff_kernel(
+    order, own_ref, cot_ref, gate_hbm, up_hbm, down_hbm,
+    blocks_ref, hidden_ref, d_gate_ref, d_up_ref, out_ref, d_in_ref,
+    gate_ref, up_ref, down_ref, rows_ref, cots_ref, h_ref, g_ref, u_ref, o_ref, d_ref,
+    send_sem, recv_sem, load_sem, store_sem,
+):
+    count = len(order)
+    half = count // 2
+    rows, width = own_ref.shape
+    hidden_here = gate_ref.shape[1]
+    cut = rows // 2
+    me = lax.axis_index("seq")
+    ahead_of, behind_of = [0] * count, [0] * count
+    for i, device in enumerate(order):
+        ahead_of[device] = order[(i + 1) % count]
+        behind_of[device] = order[(i - 1) % count]
+    sides = (lookup(ahead_of, me), lookup(behind_of, me))
+
+    barrier = pltpu.get_barrier_semaphore()
+    for side in sides:
+        pl.semaphore_signal(
+            barrier, inc=1, device_id={"seq": side}, device_id_type=pl.DeviceIdType.MESH
+        )
+    weights = [
+        pltpu.make_async_copy(hbm, vmem, load_sem.at[i])
+        for i, (hbm, vmem) in enumerate(
+            ((gate_hbm, gate_ref), (up_hbm, up_ref), (down_hbm, down_ref))
+        )
+    ]
+    for copy in weights:
+        copy.start()
+    keep = pltpu.make_async_copy(own_ref, blocks_ref.at[count - 1], load_sem.at[3])
+    keep.start()
+    pl.semaphore_wait(barrier, 2)
+
+    def full(side, source, slot, s):
+        return pltpu.make_async_remote_copy(
+            src_ref=source,
+            dst_ref=blocks_ref.at[slot],
+            send_sem=send_sem.at[side, s],
+            recv_sem=recv_sem.at[slot],
+            device_id={"seq": sides[side]},
+            device_id_type=pl.DeviceIdType.MESH,
+        )
+
+    def part(side):
+        at = pl.ds(0, cut) if side == 0 else pl.ds(cut, rows - cut)
+        return pltpu.make_async_remote_copy(
+            src_ref=blocks_ref.at[2 * (half - 2) + side, at],
+            dst_ref=blocks_ref.at[count - 2, at],
+            send_sem=send_sem.at[side, half - 1],
+            recv_sem=recv_sem.at[count - 2 + side],
+            device_id={"seq": sides[side]},
+            device_id_type=pl.DeviceIdType.MESH,
+        )
+
+    for side in range(2):
+        full(side, own_ref, side, 0).start()
+    keep.wait()
+    for copy in weights:
+        copy.wait()
+
+    def loads(s):
+        return [
+            pltpu.make_async_copy(blocks_ref.at[pl.ds(2 * (s - 1), 2)], rows_ref, load_sem.at[4]),
+            pltpu.make_async_copy(cot_ref.at[pl.ds(2 * (s - 1), 2)], cots_ref, load_sem.at[5]),
+        ]
+
+    def stores(s):
+        return [
+            pltpu.make_async_copy(vmem, hbm.at[s - 1], store_sem.at[i])
+            for i, (vmem, hbm) in enumerate(
+                (
+                    (h_ref, hidden_ref),
+                    (g_ref, d_gate_ref),
+                    (u_ref, d_up_ref),
+                    (o_ref, out_ref),
+                    (d_ref, d_in_ref),
+                )
+            )
+        ]
+
+    def step(s, carry):
+        @pl.when(s < half)
+        def _():
+            for side in range(2):
+                full(side, own_ref, 2 * (s - 1) + side, s).wait_recv()
+
+            @pl.when(s < half - 1)
+            def _():
+                for side in range(2):
+                    slot = 2 * (s - 1) + side
+                    full(side, blocks_ref.at[slot], slot + 2, s).start()
+
+            @pl.when(s == half - 1)
+            def _():
+                for side in range(2):
+                    part(side).start()
+
+        @pl.when(s == half)
+        def _():
+            for side in range(2):
+                part(side).wait_recv()
+
+        for copy in loads(s):
+            copy.start()
+
+        @pl.when(s > 1)
+        def _():
+            for copy in stores(s - 1):
+                copy.wait()
+
+        for copy in loads(s):
+            copy.wait()
+        wide = 256 if hidden_here % 256 == 0 else 128
+
+        def inner(j, carry):
+            at = pl.ds(pl.multiple_of(j * wide, wide), wide)
+            x = rows_ref[...].reshape(2 * rows, width)
+            c = cots_ref[...].reshape(2 * rows, width)
+            ff_gate = contract(x, gate_ref[:, at], 1, 0)
+            ff_up = contract(x, up_ref[:, at], 1, 0)
+            d_hidden = contract(c, down_ref[at, :], 1, 1)
+            act, slope = gelu_parts(ff_gate)
+            h_ref[:, at] = (act * ff_up).astype(bf16)
+            g_ref[:, at] = (d_hidden * ff_up * slope).astype(bf16)
+            u_ref[:, at] = (d_hidden * act).astype(bf16)
+            return carry
+
+        lax.fori_loop(0, hidden_here // wide, inner, 0)
+        out_wide = 512
+
+        def outer(j, carry):
+            at = pl.ds(pl.multiple_of(j * out_wide, out_wide), out_wide)
+            o_ref[:, at] = contract(h_ref[...], down_ref[:, at], 1, 0).astype(bf16)
+            d_ref[:, at] = (
+                contract(g_ref[...], gate_ref[at, :], 1, 1)
+                + contract(u_ref[...], up_ref[at, :], 1, 1)
+            ).astype(bf16)
+            return carry
+
+        lax.fori_loop(0, width // out_wide, outer, 0)
+        for copy in stores(s):
+            copy.start()
+        return carry
+
+    lax.fori_loop(1, half + 1, step, 0)
+    for copy in stores(half):
+        copy.wait()
+    for side in range(2):
+        for s in range(half - 1):
+            full(side, own_ref, side, s).wait_send()
+        part(side).wait_send()
+
+
+def ff_call(order, own, cot, slab_gate, slab_up, slab_down):
+    rows, width = own.shape
+    count, half = len(order), len(order) // 2
+    hidden_here = slab_gate.shape[1]
+    anywhere = pl.BlockSpec(memory_space=pl.ANY)
+    pair = 2 * rows
+    shape = jax.ShapeDtypeStruct
+    flops = 12 * count * rows * width * hidden_here
+    return pl.pallas_call(
+        functools.partial(ff_kernel, order),
+        out_shape=[shape((count, rows, width), bf16)]
+        + [shape((half, pair, hidden_here), bf16)] * 3
+        + [shape((half, pair, width), bf16)] * 2,
+        in_specs=[anywhere] * 5,
+        out_specs=[anywhere] * 6,
+        scratch_shapes=[
+            pltpu.VMEM((width, hidden_here), bf16),
+            pltpu.VMEM((width, hidden_here), bf16),
+            pltpu.VMEM((hidden_here, width), bf16),
+            pltpu.VMEM((2, rows, width), bf16),
+            pltpu.VMEM((2, rows, width), bf16),
+            pltpu.VMEM((pair, hidden_here), bf16),
+            pltpu.VMEM((pair, hidden_here), bf16),
+            pltpu.VMEM((pair, hidden_here), bf16),
+            pltpu.VMEM((pair, width), bf16),
+            pltpu.VMEM((pair, width), bf16),
+            pltpu.SemaphoreType.DMA((2, half)),
+            pltpu.SemaphoreType.DMA((count,)),
+            pltpu.SemaphoreType.DMA((6,)),
+            pltpu.SemaphoreType.DMA((5,)),
+        ],
+        compiler_params=pltpu.CompilerParams(
+            collective_id=2, has_side_effects=True, vmem_limit_bytes=48 * 2**20
+        ),
+        cost_estimate=pl.CostEstimate(
+            flops=flops, bytes_accessed=60 * 2**20, transcendentals=count * rows * hidden_here
+        ),
+    )(own, cot, slab_gate, slab_up, slab_down)
 
 
 def passed_along(value, axis, steps):
@@ -447,9 +907,25 @@
     lengths = [v.shape[0] for v in vectors]
     flat = jnp.concatenate(vectors)
     small_rows = -(-flat.shape[0] // HW)
+    small_rows += -(2 * chan_here + small_rows) % 16
     flat = jnp.pad(flat, (0, small_rows * HW - flat.shape[0]))
     packed = jnp.concatenate([w_rgate, w_igate, flat.reshape(small_rows, HW)], 0)
-    pack_blocks = net.gather_all(packed)
+    half_rows = chan_here * 3 // 5 // 16 * 16
+    out_pieces = [(3, 0, half_rows, RING_FIRST), (3, half_rows, chan_here - half_rows, CHIP_FIRST)]
+    if half_rows == 0 or chan_here % 16:
+        out_pieces = [(3, 0, chan_here, RING_FIRST)]
+    pack_got, in_got, gate_got, out_got, start_got = gather_call(
+        net,
+        (packed, w_in, w_gate, w_out, initial_state),
+        [
+            (0, 0, packed.shape[0], RING_FIRST),
+            (1, 0, wide_here, RING_FIRST),
+            (2, 0, wide_here, CHIP_FIRST),
+        ]
+        + out_pieces
+        + [(4, 0, 1, RING_ONLY)],
+    )
+    pack_blocks = [pack_got[i] for i in range(dp_count)]
     pack_all = jnp.zeros((dp_count,) + pack_blocks[0].shape, bf16)
     for (c, k), block in zip(rel, pack_blocks):
         pack_all = lax.dynamic_update_index_in_dim(pack_all, block, net.dp_at(c, k), 0)
@@ -465,27 +941,31 @@
     full_norm2 = pieces[1].reshape(-1).astype(f32)
     conv_wf = pieces[2].reshape(devices, taps, chan_here).transpose(1, 0, 2).reshape(taps, channels).astype(f32)
     full_cbias, full_rbias, full_ibias, decay_f = (p.reshape(-1).astype(f32) for p in pieces[3:])
-    start_state = net.gather_seq_placed(initial_state).reshape(1, channels)
-
-    in_blocks = [
-        b.reshape(seq_count * wide_here, 2 * channels)
-        for b in net.gather_all(jnp.concatenate([w_in, w_gate], 1))
-    ]
-    out_blocks = [b.reshape(seq_count * chan_here, width) for b in net.gather_all(w_out)]
+    start_state = start_got.reshape(1, channels)
+
+    in_blocks, gate_blocks = (
+        [got[i].reshape(seq_count * wide_here, channels) for i in range(dp_count)]
+        for got in (in_got, gate_got)
+    )
+    out_blocks = [out_got[i].reshape(seq_count * chan_here, width) for i in range(dp_count)]
+    w_ffgate, w_ffup, w_ffdown, cotangent, in_blocks[0] = lax.optimization_barrier(
+        (w_ffgate, w_ffup, w_ffdown, cotangent, in_blocks[0])
+    )
     slab_gate = jnp.concatenate(net.gather_dp(w_ffgate), 0)
     slab_up = jnp.concatenate(net.gather_dp(w_ffup), 0)
     slab_down = jnp.concatenate(net.gather_dp(w_ffdown), 1)
     cotan_rows = cotangent.reshape(rows_here, width)
-    group_cotan = jnp.concatenate(net.seq.gather(net.columns_out(cotan_rows)), 0)
+    cot_blocks = net.seq.gather(net.columns_out(cotan_rows))
+    slots = pair_slots(seq_count)
+    group_cotan = jnp.stack([cot_blocks[k] for k in slots], 0)
 
     token_rows = inputs.reshape(rows_here, width).astype(f32)
     normed_f, scale_one, unit_one = rms_parts(token_rows, full_norm1)
     normed = net.columns_out(normed_f.astype(bf16))
     step_cols = width // dp_count
     normed_parts = [normed[:, i * step_cols : (i + 1) * step_cols] for i in range(dp_count)]
-    both = total([dot(n, w) for n, w in zip(normed_parts, in_blocks)])
-    branch = both[:, :channels].astype(bf16)
-    gate_pre = both[:, channels:]
+    branch = total([dot(n, w) for n, w in zip(normed_parts, in_blocks)]).astype(bf16)
+    gate_pre = total([dot(n, w) for n, w in zip(normed_parts, gate_blocks)])
     reset_flags = reset.reshape(rows_here).astype(bf16)
     rim_branch, rim_flags = passed_along(
         (branch[len_here - rim_rows :], reset_flags[len_here - rim_rows :]), "seq", 1
@@ -548,21 +1028,21 @@
 
     normed_two_f, scale_two, unit_two = rms_parts(residual, full_norm2)
     normed_two = net.columns_out(normed_two_f.astype(bf16))
-    group_normed = jnp.concatenate(net.seq.gather(normed_two), 0)
-    ff_gate = dot(group_normed, slab_gate)
-    ff_up = dot(group_normed, slab_up)
-    ff_act, ff_back = jax.vjp(gelu_tanh, ff_gate)
-    hidden = (ff_act * ff_up).astype(bf16)
-    d_hidden = dot_t(group_cotan, slab_down)
-    d_ffgate = ff_back(d_hidden * ff_up)[0].astype(bf16)
-    d_ffup = (d_hidden * ff_act).astype(bf16)
-    d_normed_part = (dot_t(d_ffgate, slab_gate) + dot_t(d_ffup, slab_up)).astype(bf16)
-    out_part = dot(hidden, slab_down).astype(bf16)
+    group_normed, hidden, d_ffgate, d_ffup, out_part, d_normed_part = ff_call(
+        net.order, normed_two, group_cotan, slab_gate, slab_up, slab_down
+    )
+    group_rows = seq_count * rows_here
+    group_normed = group_normed.reshape(group_rows, width)
+    group_cotan = group_cotan.reshape(group_rows, width)
+    hidden, d_ffgate, d_ffup = (v.reshape(group_rows, -1) for v in (hidden, d_ffgate, d_ffup))
 
     def block_rows(whole):
-        return lambda k: whole[k * rows_here : (k + 1) * rows_here]
-
-    d_normed_two = net.columns_back(net.seq.scatter(block_rows(d_normed_part)))
+        whole = whole.reshape(seq_count, rows_here, width)
+        return lambda k: whole[slots.index(k)]
+
+    d_normed_sum = net.seq.scatter(block_rows(d_normed_part))
+    d_normed_sum, out_part = lax.optimization_barrier((d_normed_sum, out_part))
+    d_normed_two = net.columns_back(d_normed_sum)
     ff_out = net.columns_back(net.seq.scatter(block_rows(out_part)))
     gate_part = t_dot(group_normed, d_ffgate).astype(bf16)
     up_part = t_dot(group_normed, d_ffup).astype(bf16)
@@ -642,8 +1122,15 @@
     grad_cbias = jnp.sum(d_conv_f, axis=0)
     d_branch_low = d_branch.astype(bf16)
     grad_in = grad_all(normed_parts, d_branch_low)
-    d_both = jnp.concatenate([d_branch_low, d_gate_pre], 1)
-    d_normed_one = net.columns_back(jnp.concatenate([dot_t(d_both, w) for w in in_blocks], 1))
+    d_normed_one = net.columns_back(
+        jnp.concatenate(
+            [
+                dot_t(d_branch_low, left) + dot_t(d_gate_pre, right)
+                for left, right in zip(in_blocks, gate_blocks)
+            ],
+            1,
+        )
+    )
     grad_norm1, d_token_norm = norm_back(d_normed_one, full_norm1, scale_one, unit_one)
     input_grad = (d_residual + d_token_norm).reshape(seqs_here, len_here, width)
 

time: 1270 us -> 1160 us (0.913)
  Pallas kernels: 24.4 us -> 271 us
  waiting for transfers between devices: 586 us -> 435 us
  matrix products: 209 us -> 108 us
  local copies, waits for them, and re-layouts: 169 us -> 96.2 us
  starting transfers between devices: 135 us -> 87.6 us
  other arithmetic: 109 us -> 127 us
    pallas_call x0 -> x2, Pallas kernels: none -> 246 us  [the longest x1 142 us: gather_call(): pl.pallas_call(functools.partial(gather_kernel, net.order, chips, cores,...]
    ppermute x130 -> x84, waiting for transfers between devices: 586 us -> 429 us  [shift(): return lax.ppermute(value, self.axis, pairs)]
    dynamic_update_slice x31 -> x0, local copies, waits for them, and re-layouts: 54 us -> none  [gather_seq_placed(): whole = lax.dynamic_update_index_in_dim(whole, block, self.seq_at(k), 0)]
    ppermute x130 -> x84, starting transfers between devices: 125 us -> 76.2 us  [shift(): return lax.ppermute(value, self.axis, pairs)]
    dot_general x11 -> x12, matrix products: 62.1 us -> 13.4 us  [dot_t(): lax.dot_general(left, right, (((1,), (1,)), ((), ())), preferred_element_...]
    dot_general x11 -> x12, matrix products: 69.4 us -> 22.3 us  [dot(): return jnp.dot(left, right, preferred_element_type=f32)]
    slice x2, local copies, waits for them, and re-layouts: 1.4 us -> 17.3 us  [the longest x1 9.7 us: per_device(): got[i].reshape(seq_count * wide_here, channels)]
    unnamed x247 -> x263, local copies, waits for them, and re-layouts: 45.5 us -> 38 us
  transfers between devices with their start and end apart: 134 -> 88, of which waited for: 56 -> 44; matrix products, arithmetic and copies ran while one was open for 23% -> 15% of each run, Pallas kernels for 1% -> 1%
where the time goes in v2:
time: 1160 us; the launch traced here: 1150 us
  waiting for transfers between devices  435 us (38%)
  Pallas kernels  271 us (23%)
  other arithmetic  127 us (11%)
  matrix products  108 us (9%)
  local copies, waits for them, and re-layouts  96.2 us (8%)
  starting transfers between devices  87.6 us (8%)
  between operations  25.2 us (2%)
    ppermute x84, waiting for transfers between devices, shift(): return lax.ppermute(value, self.axis, pairs)  429 us
    pallas_call x1, Pallas kernels, gather_call(): pl.pallas_call(functools.partial(gather_kernel, net.order, chips, cores,...  142 us
    pallas_call x1, Pallas kernels, ff_call(): pl.pallas_call(functools.partial(ff_kernel, order), out_shape=[shape((cou...  104 us
    ppermute x84, starting transfers between devices, shift(): return lax.ppermute(value, self.axis, pairs)  76.2 us
    dot_general x15, matrix products, t_dot(): lax.dot_general(left, right, (((0,), (0,)), ((), ())), preferred_element_...  54 us
    unnamed x263, local copies, waits for them, and re-layouts  38 us
    pallas_call x2, Pallas kernels, scan_call(): pl.pallas_call(functools.partial(kernel, count), out_shape=out_shapes, in...  25.5 us
  transfers between devices with their start and end apart: 88, of which 44 were waited for; matrix products, arithmetic and copies ran while one was open for 15% of the time, Pallas kernels for 1%

profile of v2, /device:TPU:0, one launch (start us, length us, event | category | flops | bytes accessed | tf_op | source)
XLA Modules:
  0.0 1149.5 jit_solution(2085330046366080550)
XLA Ops:
  9.9 142.1 %shard_map.619 = (bf16[4,8,176,256]{3,2,1,0:T(8,128)(2,1)S(1)}, bf16[4,8,64,2560]{3,2,1,0:T(8,128)(2,1)S(1)}, bf16[4,8,64,2560]{3,2,1,0:T(8,128)(2,1)}, bf16[4,8...) custom-call(bf16[176,256]{1,0:T(8,128)(2,1)S(1)} %pad_maximum_fusion.19.refs_0_, bf16[64,2560]{1,0:T(8,128)(2,1)S(1)} %copy-done.6, ...), custom_call_target="tpu_custom_call" | custom-call | bytes 68722688 | tf_op jit(solution)/shard_map/pallas_call | solution.py:399
  153.6 9.7 fusion.149
  235.0 10.4 convert_multiply_fusion.3
  245.4 14.1 %shard_map.620 = (f32[256,2560]{1,0:T(8,128)S(1)}, f32[256,2560]{1,0:T(8,128)S(1)}, f32[1,2560]{1,0:T(1,128)S(1)}) custom-call(f32[256,2560]{1,0:T(8,128)S(1)} %get-tuple-element.131.decay_ref, f32[256,2560]{1,0:T(8,128)S(1)} %get-tuple-element.130.drive_ref, f32[1,2560]{1,0:T(1,128)S(1)} %reshape.455.start_ref), custom_call_target="tpu_custom_call" | custom-call | flops 5242880 | bytes 13107200 | tf_op jit(solution)/shard_map/pallas_call | solution.py:577
  277.9 14.1 %collective-permute-done.13 = bf16[512,768]{1,0:T(8,128)(2,1)S(1)} collective-permute-done((bf16[512,768]{1,0:T(8,128)(2,1)}, bf16[512,768]{1,0:T(8,128)(2,1)S(1)}, u32[]{:S(2)}, u32[]{:S(2)}) %collective-permute-start.13) | collective-permute-done | bytes 786464 | tf_op jit(solution)/shard_map/ppermute | solution.py:43
  292.0 16.0 %collective-permute-done.16 = bf16[768,512]{1,0:T(8,128)(2,1)S(1)} collective-permute-done((bf16[768,512]{1,0:T(8,128)(2,1)S(1)}, bf16[768,512]{1,0:T(8,128)(2,1)S(1)}, u32[]{:S(2)}, u32[]{:S(2)}) %collective-permute-start.16) | collective-permute-done | bytes 786464 | tf_op jit(solution)/shard_map/ppermute | solution.py:43
  318.3 16.4 %collective-permute-done.5 = bf16[256,2048]{1,0:T(8,128)(2,1)S(1)} collective-permute-done((bf16[256,2048]{1,0:T(8,128)(2,1)}, bf16[256,2048]{1,0:T(8,128)(2,1)S(1)}, u32[]{:S(2)}, u32[]{:S(2)}) %collective-permute-start.5) | collective-permute-done | bytes 1048608 | tf_op jit(solution)/shard_map/ppermute | solution.py:43
  341.2 18.0 %collective-permute-done.7 = bf16[256,2048]{1,0:T(8,128)(2,1)S(1)} collective-permute-done((bf16[256,2048]{1,0:T(8,128)(2,1)S(1)}, bf16[256,2048]{1,0:T(8,128)(2,1)S(1)}, u32[]{:S(2)}, u32[]{:S(2)}) %collective-permute-start.7) | collective-permute-done | bytes 1048608 | tf_op jit(solution)/shard_map/ppermute | solution.py:43
  374.4 103.6 %shard_map.621 = (bf16[8,256,2048]{2,1,0:T(8,128)(2,1)}, bf16[4,512,768]{2,1,0:T(8,128)(2,1)S(1)}, bf16[4,512,768]{2,1,0:T(8,128)(2,1)}, bf16[4,512,768]{2,1,0:T...) custom-call(bf16[256,2048]{1,0:T(8,128)(2,1)S(1)} %pad_maximum_fusion.9.own_ref, ...), custom_call_target="tpu_custom_call" | custom-call | flops 38654705664 | bytes 62914560 | tf_op jit(solution)/shard_map/pallas_call | solution.py:781
  483.0 9.5 collective-permute-done.19
  498.9 20.6 %collective-permute-done.20 = bf16[256,2048]{1,0:T(8,128)(2,1)S(1)} collective-permute-done((bf16[256,2048]{1,0:T(8,128)(2,1)S(1)}, bf16[256,2048]{1,0:T(8,128)(2,1)S(1)}, u32[]{:S(2)}, u32[]{:S(2)}) %collective-permute-start.20) | collective-permute-done | bytes 1048608 | tf_op jit(solution)/shard_map/ppermute | solution.py:43
  520.1 19.9 %collective-permute-done.21 = bf16[256,2048]{1,0:T(8,128)(2,1)S(1)} collective-permute-done((bf16[256,2048]{1,0:T(8,128)(2,1)S(1)}, bf16[256,2048]{1,0:T(8,128)(2,1)S(1)}, u32[]{:S(2)}, u32[]{:S(2)}) %collective-permute-start.21) | collective-permute-done | bytes 1048608 | tf_op jit(solution)/shard_map/ppermute | solution.py:43
  543.7 23.4 %collective-permute-done.25 = bf16[256,2048]{1,0:T(8,128)(2,1)S(1)} collective-permute-done((bf16[256,2048]{1,0:T(8,128)(2,1)S(1)}, bf16[256,2048]{1,0:T(8,128)(2,1)S(1)}, u32[]{:S(2)}, u32[]{:S(2)}) %collective-permute-start.25) | collective-permute-done | bytes 1048608 | tf_op jit(solution)/shard_map/ppermute | solution.py:43
  610.9 9.5 convolution_convert_fusion.9
  621.1 13.3 %collective-permute-done.28 = bf16[256,2048]{1,0:T(8,128)(2,1)S(1)} collective-permute-done((bf16[256,2048]{1,0:T(8,128)(2,1)S(1)}, bf16[256,2048]{1,0:T(8,128)(2,1)S(1)}, u32[]{:S(2)}, u32[]{:S(2)}) %collective-permute-start.28) | collective-permute-done | bytes 1048608 | tf_op jit(solution)/shard_map/ppermute | solution.py:43
  648.9 10.4 collective-permute-done.29
  669.8 14.6 %collective-permute-done.33 = bf16[256,2048]{1,0:T(8,128)(2,1)S(1)} collective-permute-done((bf16[256,2048]{1,0:T(8,128)(2,1)S(1)}, bf16[256,2048]{1,0:T(8,128)(2,1)S(1)}, u32[]{:S(2)}, u32[]{:S(2)}) %collective-permute-start.33) | collective-permute-done | bytes 1048608 | tf_op jit(solution)/shard_map/ppermute | solution.py:43
  689.4 11.5 %collective-permute-done.84 = bf16[512,768]{1,0:T(8,128)(2,1)S(1)} collective-permute-done((bf16[512,768]{1,0:T(8,128)(2,1)S(1)}, bf16[512,768]{1,0:T(8,128)(2,1)S(1)}, u32[]{:S(2)}, u32[]{:S(2)}) %collective-permute-start.84) | collective-permute-done | bytes 786464 | tf_op jit(solution)/shard_map/ppermute | solution.py:43
  748.0 11.4 shard_map.622
  759.6 10.8 multiply_reduce_fusion
  770.4 11.3 fusion.145
  907.3 47.2 %collective-permute-done.49 = bf16[8,64,2560]{2,1,0:T(8,128)(2,1)} collective-permute-done((bf16[8,64,2560]{2,1,0:T(8,128)(2,1)}, bf16[8,64,2560]{2,1,0:T(8,128)(2,1)}, u32[]{:S(2)}, u32[]{:S(2)}) %collective-permute-start.49) | collective-permute-done | bytes 2621472 | tf_op jit(solution)/shard_map/ppermute | solution.py:43
  960.3 50.3 %collective-permute-done.71 = bf16[8,80,2048]{2,1,0:T(8,128)(2,1)} collective-permute-done((bf16[8,80,2048]{2,1,0:T(8,128)(2,1)}, bf16[8,80,2048]{2,1,0:T(8,128)(2,1)}, u32[]{:S(2)}, u32[]{:S(2)}) %collective-permute-start.71) | collective-permute-done | bytes 2621472 | tf_op jit(solution)/shard_map/ppermute | solution.py:43
  1017.1 47.5 %collective-permute-done.60 = bf16[8,64,2560]{2,1,0:T(8,128)(2,1)} collective-permute-done((bf16[8,64,2560]{2,1,0:T(8,128)(2,1)}, bf16[8,64,2560]{2,1,0:T(8,128)(2,1)}, u32[]{:S(2)}, u32[]{:S(2)}) %collective-permute-start.60) | collective-permute-done | bytes 2621472 | tf_op jit(solution)/shard_map/ppermute | solution.py:43
  (640 shorter events, 468.6 us)
Async XLA Ops:
  163.3 108.0 %collective-permute-start.11 = (bf16[512,768]{1,0:T(8,128)(2,1)}, bf16[512,768]{1,0:T(8,128)(2,1)}, u32[]{:S(2)}, u32[]{:S(2)}) collective-permute-start(bf16[512,768]{1,0:T(8,128)(2,1)} %param.68), channel_id=1, source_target_pairs={{0,8},{8,0},{16,24},{24,16},{1,9},{9,1},{17,25},{25,17},{2,10},{10... | collective-permute-start | bytes 2359304 | tf_op jit(solution)/shard_map/ppermute | solution.py:43
  164.1 109.2 %collective-permute-start.10 = (bf16[512,768]{1,0:T(8,128)(2,1)}, bf16[512,768]{1,0:T(8,128)(2,1)}, u32[]{:S(2)}, u32[]{:S(2)}) collective-permute-start(bf16[512,768]{1,0:T(8,128)(2,1)} %param.68), channel_id=1, source_target_pairs={{0,16},{16,0},{8,24},{24,8},{1,17},{17,1},{9,25},{25,9},{2,18},{18... | collective-permute-start | bytes 2359304 | tf_op jit(solution)/shard_map/ppermute | solution.py:43
  167.7 140.3 %collective-permute-start.3 = (bf16[256,2048]{1,0:T(8,128)(2,1)}, bf16[256,2048]{1,0:T(8,128)(2,1)}, u32[]{:S(2)}, u32[]{:S(2)}) collective-permute-start(bf16[256,2048]{1,0:T(8,128)(2,1)} %pad_maximum_fusion.10), channel_id=1, source_target_pairs={{1,0},{3,1},{5,3},{7,5},{6,7},{4,6},{2,4},{0,2},{9,8},{11,9},{13,1... | collective-permute-start | bytes 3145736 | tf_op jit(solution)/shard_map/ppermute | solution.py:43
  169.2 105.5 %collective-permute-start.2 = (bf16[256,2048]{1,0:T(8,128)(2,1)}, bf16[256,2048]{1,0:T(8,128)(2,1)}, u32[]{:S(2)}, u32[]{:S(2)}) collective-permute-start(bf16[256,2048]{1,0:T(8,128)(2,1)} %pad_maximum_fusion.10), channel_id=1, source_target_pairs={{1,3},{3,5},{5,7},{7,6},{6,4},{4,2},{2,0},{0,1},{9,11},{11,13},{13... | collective-permute-start | bytes 3145736 | tf_op jit(solution)/shard_map/ppermute | solution.py:43
  211.3 66.0 %collective-permute-start.14 = (bf16[512,768]{1,0:T(8,128)(2,1)}, bf16[512,768]{1,0:T(8,128)(2,1)}, u32[]{:S(2)}, u32[]{:S(2)}) collective-permute-start(bf16[512,768]{1,0:T(8,128)(2,1)} %param.69), channel_id=1, source_target_pairs={{0,8},{8,0},{16,24},{24,16},{1,9},{9,1},{17,25},{25,17},{2,10},{10... | collective-permute-start | bytes 2359304 | tf_op jit(solution)/shard_map/ppermute | solution.py:43
  273.3 34.7 %collective-permute-start.16 = (bf16[768,512]{1,0:T(8,128)(2,1)S(1)}, bf16[768,512]{1,0:T(8,128)(2,1)S(1)}, u32[]{:S(2)}, u32[]{:S(2)}) collective-permute-start(bf16[768,512]{1,0:T(8,128)(2,1)S(1)} %copy-done.85), channel_id=1, source_target_pairs={{0,16},{16,0},{8,24},{24,8},{1,17},{17,1},{9,25},{25,9},{2,18},{18... | collective-permute-start | bytes 2359304 | tf_op jit(solution)/shard_map/ppermute | solution.py:43
  274.7 34.6 %collective-permute-start.12 = (bf16[512,768]{1,0:T(8,128)(2,1)}, bf16[512,768]{1,0:T(8,128)(2,1)S(1)}, u32[]{:S(2)}, u32[]{:S(2)}) collective-permute-start(bf16[512,768]{1,0:T(8,128)(2,1)} %collective-permute-done.10), channel_id=1, source_target_pairs={{0,8},{8,0},{16,24},{24,16},{1,9},{9,1},{17,25},{25,17},{2,10},{10... | collective-permute-start | bytes 2359304 | tf_op jit(solution)/shard_map/ppermute | solution.py:43
  277.4 59.4 %collective-permute-start.17 = (bf16[768,512]{1,0:T(8,128)(2,1)S(1)}, bf16[768,512]{1,0:T(8,128)(2,1)S(1)}, u32[]{:S(2)}, u32[]{:S(2)}) collective-permute-start(bf16[768,512]{1,0:T(8,128)(2,1)S(1)} %copy-done.85), channel_id=1, source_target_pairs={{0,8},{8,0},{16,24},{24,16},{1,9},{9,1},{17,25},{25,17},{2,10},{10... | collective-permute-start | bytes 2359304 | tf_op jit(solution)/shard_map/ppermute | solution.py:43
  541.7 50.6 %collective-permute-start.22 = (bf16[256,2048]{1,0:T(8,128)(2,1)}, bf16[256,2048]{1,0:T(8,128)(2,1)}, u32[]{:S(2)}, u32[]{:S(2)}) collective-permute-start(bf16[256,2048]{1,0:T(8,128)(2,1)} %get-tuple-element.109), channel_id=1, source_target_pairs={{1,3},{3,5},{5,7},{7,6},{6,4},{4,2},{2,0},{0,1},{9,11},{11,13},{13... | collective-permute-start | bytes 3145736 | tf_op jit(solution)/shard_map/ppermute | solution.py:43
  608.1 56.3 %collective-permute-start.85 = (bf16[768,512]{1,0:T(8,128)(2,1)S(1)}, bf16[768,512]{1,0:T(8,128)(2,1)S(1)}, u32[]{:S(2)}, u32[]{:S(2)}) collective-permute-start(bf16[768,512]{1,0:T(8,128)(2,1)S(1)} %get-tuple-element.119), channel_id=1, source_target_pairs={{0,8},{8,0},{16,24},{24,16},{1,9},{9,1},{17,25},{25,17},{2,10},{10... | collective-permute-start | bytes 2359304 | tf_op jit(solution)/shard_map/ppermute | solution.py:43
  608.2 38.0 %collective-permute-start.86 = (bf16[768,512]{1,0:T(8,128)(2,1)S(1)}, bf16[768,512]{1,0:T(8,128)(2,1)S(1)}, u32[]{:S(2)}, u32[]{:S(2)}) collective-permute-start(bf16[768,512]{1,0:T(8,128)(2,1)S(1)} %get-tuple-element.120), channel_id=1, source_target_pairs={{0,8},{8,0},{16,24},{24,16},{1,9},{9,1},{17,25},{25,17},{2,10},{10... | collective-permute-start | bytes 2359304 | tf_op jit(solution)/shard_map/ppermute | solution.py:43
  666.6 34.3 %collective-permute-start.84 = (bf16[512,768]{1,0:T(8,128)(2,1)S(1)}, bf16[512,768]{1,0:T(8,128)(2,1)S(1)}, u32[]{:S(2)}, u32[]{:S(2)}) collective-permute-start(bf16[512,768]{1,0:T(8,128)(2,1)S(1)} %add_convert_fusion.3), channel_id=1, source_target_pairs={{0,16},{16,0},{8,24},{24,8},{1,17},{17,1},{9,25},{25,9},{2,18},{18... | collective-permute-start | bytes 2359304 | tf_op jit(solution)/shard_map/ppermute | solution.py:43
  845.2 57.0 %collective-permute-start.47 = (bf16[8,64,2560]{2,1,0:T(8,128)(2,1)S(1)}, bf16[8,64,2560]{2,1,0:T(8,128)(2,1)S(1)}, u32[]{:S(2)}, u32[]{:S(2)}) collective-permute-start(bf16[8,64,2560]{2,1,0:T(8,128)(2,1)S(1)} %bitcast.458), channel_id=1, source_target_pairs={{0,8},{8,0},{16,24},{24,16},{1,9},{9,1},{17,25},{25,17},{2,10},{10... | collective-permute-start | bytes 7864328 | tf_op jit(solution)/shard_map/ppermute | solution.py:43
  845.2 44.6 %collective-permute-start.48 = (bf16[8,64,2560]{2,1,0:T(8,128)(2,1)S(1)}, bf16[8,64,2560]{2,1,0:T(8,128)(2,1)S(1)}, u32[]{:S(2)}, u32[]{:S(2)}) collective-permute-start(bf16[8,64,2560]{2,1,0:T(8,128)(2,1)S(1)} %bitcast.459), channel_id=1, source_target_pairs={{0,8},{8,0},{16,24},{24,16},{1,9},{9,1},{17,25},{25,17},{2,10},{10... | collective-permute-start | bytes 7864328 | tf_op jit(solution)/shard_map/ppermute | solution.py:43
  845.7 51.1 %collective-permute-start.70 = (bf16[8,80,2048]{2,1,0:T(8,128)(2,1)S(1)}, bf16[8,80,2048]{2,1,0:T(8,128)(2,1)S(1)}, u32[]{:S(2)}, u32[]{:S(2)}) collective-permute-start(bf16[8,80,2048]{2,1,0:T(8,128)(2,1)S(1)} %bitcast.457), channel_id=1, source_target_pairs={{0,8},{8,0},{16,24},{24,16},{1,9},{9,1},{17,25},{25,17},{2,10},{10... | collective-permute-start | bytes 7864328 | tf_op jit(solution)/shard_map/ppermute | solution.py:43
  892.7 66.6 %collective-permute-start.69 = (bf16[8,80,2048]{2,1,0:T(8,128)(2,1)}, bf16[8,80,2048]{2,1,0:T(8,128)(2,1)}, u32[]{:S(2)}, u32[]{:S(2)}) collective-permute-start(bf16[8,80,2048]{2,1,0:T(8,128)(2,1)} %bitcast.127), channel_id=1, source_target_pairs={{0,8},{8,0},{16,24},{24,16},{1,9},{9,1},{17,25},{25,17},{2,10},{10... | collective-permute-start | bytes 7864328 | tf_op jit(solution)/shard_map/ppermute | solution.py:43
  894.4 60.1 %collective-permute-start.49 = (bf16[8,64,2560]{2,1,0:T(8,128)(2,1)}, bf16[8,64,2560]{2,1,0:T(8,128)(2,1)}, u32[]{:S(2)}, u32[]{:S(2)}) collective-permute-start(bf16[8,64,2560]{2,1,0:T(8,128)(2,1)} %fusion.6), channel_id=1, source_target_pairs={{0,16},{16,0},{8,24},{24,8},{1,17},{17,1},{9,25},{25,9},{2,18},{18... | collective-permute-start | bytes 7864328 | tf_op jit(solution)/shard_map/ppermute | solution.py:43
  896.8 119.4 %collective-permute-start.58 = (bf16[8,64,2560]{2,1,0:T(8,128)(2,1)}, bf16[8,64,2560]{2,1,0:T(8,128)(2,1)}, u32[]{:S(2)}, u32[]{:S(2)}) collective-permute-start(bf16[8,64,2560]{2,1,0:T(8,128)(2,1)} %bitcast.112), channel_id=1, source_target_pairs={{0,8},{8,0},{16,24},{24,16},{1,9},{9,1},{17,25},{25,17},{2,10},{10... | collective-permute-start | bytes 7864328 | tf_op jit(solution)/shard_map/ppermute | solution.py:43
  899.5 111.2 %collective-permute-start.71 = (bf16[8,80,2048]{2,1,0:T(8,128)(2,1)}, bf16[8,80,2048]{2,1,0:T(8,128)(2,1)}, u32[]{:S(2)}, u32[]{:S(2)}) collective-permute-start(bf16[8,80,2048]{2,1,0:T(8,128)(2,1)} %fusion), channel_id=1, source_target_pairs={{0,16},{16,0},{8,24},{24,8},{1,17},{17,1},{9,25},{25,9},{2,18},{18... | collective-permute-start | bytes 7864328 | tf_op jit(solution)/shard_map/ppermute | solution.py:43
  903.7 161.0 %collective-permute-start.60 = (bf16[8,64,2560]{2,1,0:T(8,128)(2,1)}, bf16[8,64,2560]{2,1,0:T(8,128)(2,1)}, u32[]{:S(2)}, u32[]{:S(2)}) collective-permute-start(bf16[8,64,2560]{2,1,0:T(8,128)(2,1)} %fusion.3), channel_id=1, source_target_pairs={{0,16},{16,0},{8,24},{24,8},{1,17},{17,1},{9,25},{25,9},{2,18},{18... | collective-permute-start | bytes 7864328 | tf_op jit(solution)/shard_map/ppermute | solution.py:43
  958.2 111.7 %collective-permute-start.50 = (bf16[32,2560]{1,0:T(8,128)(2,1)S(1)}, bf16[32,2560]{1,0:T(8,128)(2,1)S(1)}, u32[]{:S(2)}, u32[]{:S(2)}) collective-permute-start(bf16[32,2560]{1,0:T(8,128)(2,1)S(1)} %get-tuple-element.150), channel_id=1, source_target_pairs={{1,3},{3,5},{5,7},{7,6},{6,4},{4,2},{2,0},{0,1},{9,11},{11,13},{13... | collective-permute-start | bytes 491528 | tf_op jit(solution)/shard_map/ppermute | solution.py:43
  959.3 111.1 %collective-permute-start.54 = (bf16[32,2560]{1,0:T(8,128)(2,1)S(1)}, bf16[32,2560]{1,0:T(8,128)(2,1)S(1)}, u32[]{:S(2)}, u32[]{:S(2)}) collective-permute-start(bf16[32,2560]{1,0:T(8,128)(2,1)S(1)} %get-tuple-element.152), channel_id=1, source_target_pairs={{1,0},{3,1},{5,3},{7,5},{6,7},{4,6},{2,4},{0,2},{9,8},{11,9},{13,1... | collective-permute-start | bytes 491528 | tf_op jit(solution)/shard_map/ppermute | solution.py:43
  1015.1 62.6 %collective-permute-start.72 = (bf16[80,2048]{1,0:T(8,128)(2,1)S(1)}, bf16[80,2048]{1,0:T(8,128)(2,1)S(1)}, u32[]{:S(2)}, u32[]{:S(2)}) collective-permute-start(bf16[80,2048]{1,0:T(8,128)(2,1)S(1)} %get-tuple-element.136), channel_id=1, source_target_pairs={{1,3},{3,5},{5,7},{7,6},{6,4},{4,2},{2,0},{0,1},{9,11},{11,13},{13... | collective-permute-start | bytes 983048 | tf_op jit(solution)/shard_map/ppermute | solution.py:43
  1016.1 98.1 %collective-permute-start.76 = (bf16[80,2048]{1,0:T(8,128)(2,1)S(1)}, bf16[80,2048]{1,0:T(8,128)(2,1)S(1)}, u32[]{:S(2)}, u32[]{:S(2)}) collective-permute-start(bf16[80,2048]{1,0:T(8,128)(2,1)S(1)} %get-tuple-element.137), channel_id=1, source_target_pairs={{1,0},{3,1},{5,3},{7,5},{6,7},{4,6},{2,4},{0,2},{9,8},{11,9},{13,1... | collective-permute-start | bytes 983048 | tf_op jit(solution)/shard_map/ppermute | solution.py:43
  (191 other events, 2688.7 us)

commit v3 on v2

--- a/solution.py
+++ b/solution.py
@@ -49,57 +49,76 @@
                 table[device] = i
         return jnp.asarray(table, jnp.int32)[lax.axis_index(self.axis)]
 
-    def gather(self, value):
+    def gather_steps(self, value):
         count, half = self.count, self.count // 2
         blocks = [value] * count
         if count == 1:
             return blocks
         ahead = behind = value
         for step in range(1, half):
-            behind = self.shift(behind, 1)
-            ahead = self.shift(ahead, -1)
+            behind, ahead = yield [self.shift(behind, 1), self.shift(ahead, -1)]
             blocks[count - step] = behind
             blocks[step] = ahead
         rows = value.shape[0]
         if half > 1 and rows % 32 == 0:
-            top = self.shift(behind[: rows // 2], 1)
-            bottom = self.shift(ahead[rows // 2 :], -1)
+            top, bottom = yield [
+                self.shift(behind[: rows // 2], 1),
+                self.shift(ahead[rows // 2 :], -1),
+            ]
             blocks[half] = jnp.concatenate([top, bottom], 0)
         else:
-            blocks[half] = self.shift(behind, 1)
+            (blocks[half],) = yield [self.shift(behind, 1)]
         return blocks
 
-    def scatter(self, part):
+    def scatter_steps(self, part):
         count, half = self.count, self.count // 2
         if count == 1:
             return part(0).astype(f32)
         far = part(half).astype(bf16)
         if half == 1:
-            return part(0).astype(f32) + self.shift(far, 1).astype(f32)
+            (got,) = yield [self.shift(far, 1)]
+            return part(0).astype(f32) + got.astype(f32)
         rows = far.shape[0]
-        cut = rows // 2 if rows % 32 == 0 else rows
+        assert rows % 2 == 0
+        cut = rows // 2
         ahead, behind = far[:cut], far[cut:]
-        for k in range(half - 1, 0, -1):
-            got_ahead = self.shift(ahead, 1).astype(f32)
-            mine_ahead = part(k).astype(f32)
-            mine_behind = part(count - k).astype(f32)
-            if k == half - 1 and cut == rows:
-                ahead = (mine_ahead + got_ahead).astype(bf16)
-                behind = mine_behind.astype(bf16)
-                continue
-            got_behind = self.shift(behind, -1).astype(f32)
+        for k in range(half - 1, -1, -1):
+            got_ahead, got_behind = yield [self.shift(ahead, 1), self.shift(behind, -1)]
+            got_ahead, got_behind = got_ahead.astype(f32), got_behind.astype(f32)
+            if k == 0:
+                return part(0).astype(f32) + got_ahead + got_behind
+            ahead, behind = part(k).astype(f32), part(count - k).astype(f32)
             if k == half - 1:
-                ahead = jnp.concatenate([mine_ahead[:cut] + got_ahead, mine_ahead[cut:]], 0)
-                behind = jnp.concatenate([mine_behind[:cut], mine_behind[cut:] + got_behind], 0)
+                ahead = jnp.concatenate([ahead[:cut] + got_ahead, ahead[cut:]], 0)
+                behind = jnp.concatenate([behind[:cut], behind[cut:] + got_behind], 0)
             else:
-                ahead = mine_ahead + got_ahead
-                behind = mine_behind + got_behind
+                ahead, behind = ahead + got_ahead, behind + got_behind
             ahead, behind = ahead.astype(bf16), behind.astype(bf16)
-        return (
-            part(0).astype(f32)
-            + self.shift(ahead, 1).astype(f32)
-            + self.shift(behind, -1).astype(f32)
-        )
+
+
+class Flow:
+    def __init__(self, steps):
+        self.steps, self.pending, self.result = steps, [], None
+        self.advance(None)
+
+    def advance(self, arrived):
+        try:
+            self.pending = self.steps.send(arrived)
+        except StopIteration as stop:
+            self.pending, self.result = [], stop.value
+
+    def finish(self):
+        while self.pending:
+            self.advance(self.pending)
+        return self.result
+
+
+def beside(values, *flows):
+    values, arrived = lax.optimization_barrier((values, [flow.pending for flow in flows]))
+    for flow, got in zip(flows, arrived):
+        if got:
+            flow.advance(got)
+    return values
 
 
 class Net:
@@ -142,38 +161,19 @@
             pieces.append(lax.dynamic_slice_in_dim(values, at * chunk, chunk, 1))
         return jnp.concatenate(pieces, 1)
 
-    def gather_dp(self, value):
-        blocks = self.chip.gather(value)
+    def gather_dp_steps(self, value):
+        blocks = yield from self.chip.gather_steps(value)
         if self.cores == 1:
             return blocks
-        return blocks + [self.core.shift(block, 1) for block in blocks]
-
-    def scatter_dp(self, part):
+        others = yield [self.core.shift(block, 1) for block in blocks]
+        return blocks + others
+
+    def scatter_dp_steps(self, part):
         sums = [part(0, k) for k in range(self.chips)]
         if self.cores > 1:
-            sums = [
-                mine.astype(f32) + self.core.shift(part(1, k).astype(bf16), 1).astype(f32)
-                for k, mine in enumerate(sums)
-            ]
-        return self.chip.scatter(lambda k: sums[k])
-
-    def gather_seq_placed(self, value):
-        blocks = self.seq.gather(value)
-        whole = jnp.zeros((self.seq_count,) + value.shape, value.dtype)
-        for k, block in enumerate(blocks):
-            whole = lax.dynamic_update_index_in_dim(whole, block, self.seq_at(k), 0)
-        return whole
-
-    def gather_all(self, value):
-        return self.gather_dp(self.gather_seq_placed(value))
-
-    def scatter_seq_placed(self, whole):
-        return self.seq.scatter(
-            lambda k: lax.dynamic_index_in_dim(whole, self.seq_at(k), 0, keepdims=False)
-        )
-
-    def scatter_all(self, part):
-        return self.scatter_seq_placed(self.scatter_dp(part).astype(bf16))
+            got = yield [self.core.shift(part(1, k).astype(bf16), 1) for k in range(self.chips)]
+            sums = [mine.astype(f32) + theirs.astype(f32) for mine, theirs in zip(sums, got)]
+        return (yield from self.chip.scatter_steps(lambda k: sums[k]))
 
 
 def lookup(table, index):
@@ -420,6 +420,237 @@
     )(*arrays)
 
 
+def add_rows(target, terms, rows):
+    if rows % 16:
+        target[...] = total([term[...].astype(f32) for term in terms]).astype(target.dtype)
+        return
+
+    def body(t, carry):
+        at = pl.ds(pl.multiple_of(t * 16, 16), 16)
+        target[at] = total([term[at].astype(f32) for term in terms]).astype(target.dtype)
+        return carry
+
+    lax.fori_loop(0, rows // 16, body, 0)
+
+
+def total(terms):
+    result = terms[0]
+    for term in terms[1:]:
+        result = result + term
+    return result
+
+
+def reduce_kernel(order, chips, cores, pieces, arrays, *refs):
+    slots = chips * cores
+    count, half = len(order), len(order) // 2
+    parts = [refs[i * slots : (i + 1) * slots] for i in range(arrays)]
+    refs = refs[arrays * slots :]
+    outs, refs = refs[:arrays], refs[arrays:]
+    mine, refs = refs[:arrays], refs[arrays:]
+    other, refs = refs[:arrays], refs[arrays:]
+    chip_in, refs = refs[: len(pieces)], refs[len(pieces) :]
+    ring_in, refs = refs[: len(pieces)], refs[len(pieces) :]
+    load_sem, core_send, core_recv, chip_send, chip_recv, ring_send, ring_recv = refs
+    links = Links(order, chips, cores)
+    everyone = range(len(pieces))
+    method = [piece[3] for piece in pieces]
+
+    loads = [
+        [
+            pltpu.make_async_copy(parts[i][k], mine[i].at[k], load_sem.at[i, k])
+            for k in range(chips)
+        ]
+        for i in range(arrays)
+    ]
+    for copies in loads:
+        for copy in copies:
+            copy.start()
+    links.greet()
+    sent = []
+
+    def start(copy):
+        copy.start()
+        sent.append(copy)
+
+    def rows_of_piece(ref, p, first=0, rows=None):
+        array, start_row, piece_rows, _ = pieces[p]
+        rows = piece_rows if rows is None else rows
+        if rows == ref.shape[0]:
+            return ref
+        return ref.at[pl.ds(start_row + first, rows)]
+
+    def held(p, k, q):
+        return rows_of_piece(mine[pieces[p][0]].at[k, links.seq_at[q]], p)
+
+    def core_copy(p, k, q):
+        array = pieces[p][0]
+        return remote(
+            rows_of_piece(parts[array][chips + k].at[links.seq_at[q]], p),
+            rows_of_piece(other[array].at[k, links.seq_at[q]], p),
+            core_send.at[p, k, q], core_recv.at[p, k, q], links.core,
+        )
+
+    def steps(d):
+        return sorted({d % count, (count - d) % count})
+
+    def planes(p):
+        return range(chips) if method[p] == RING_FIRST else range(1)
+
+    if cores == 2:
+        for d in range(half, -1, -1):
+            for p in everyone:
+                for k in reversed(range(chips)):
+                    for q in steps(d):
+                        start(core_copy(p, k, q))
+
+    loaded = set()
+
+    def core_sum(p, k, q):
+        array = pieces[p][0]
+        if (array, k) not in loaded:
+            loaded.add((array, k))
+            loads[array][k].wait()
+        if cores == 2:
+            core_copy(p, k, q).wait_recv()
+            theirs = rows_of_piece(other[array].at[k, links.seq_at[q]], p)
+            add_rows(held(p, k, q), [held(p, k, q), theirs], pieces[p][2])
+
+    def chip_copy(p, k, q):
+        if method[p] == CHIP_FIRST:
+            target = chip_in[p].at[k - 1, links.seq_at[q]]
+        else:
+            target = chip_in[p].at[k - 1]
+        return remote(
+            held(p, k, q), target, chip_send.at[p, k - 1, q], chip_recv.at[p, k - 1, q], links.chip[k - 1]
+        )
+
+    def chip_sum(p, q):
+        for k in range(1, chips):
+            chip_copy(p, k, q).wait_recv()
+            if method[p] == CHIP_FIRST:
+                add_rows(held(p, 0, q), [held(p, 0, q), chip_in[p].at[k - 1, links.seq_at[q]]], pieces[p][2])
+            else:
+                out = rows_of_piece(outs[pieces[p][0]], p)
+                add_rows(out, [out, chip_in[p].at[k - 1]], pieces[p][2])
+
+    def span(p, side, d):
+        rows = pieces[p][2]
+        cut = rows // 32 * 16
+        if d < half:
+            return (0, rows)
+        if not cut:
+            return (0, rows) if side == 0 else None
+        return (0, cut) if side == 0 else (cut, rows - cut)
+
+    def ring_copy(p, k, side, d):
+        first, rows = span(p, side, d)
+        q = d if side == 0 else (count - d) % count
+        source = held(p, k, q)
+        target = ring_in[p].at[k, side, d - 1]
+        if rows != pieces[p][2]:
+            source, target = source.at[pl.ds(first, rows)], target.at[pl.ds(first, rows)]
+        return remote(
+            source, target, ring_send.at[p, k, side, d - 1], ring_recv.at[p, k, side, d - 1], links.ring[side]
+        )
+
+    def ring_step(p, k, d):
+        if d == 0:
+            got = []
+            for side in range(2):
+                if half > 1 or span(p, side, 1):
+                    ring_copy(p, k, side, 1).wait_recv()
+                    got.append(ring_in[p].at[k, side, 0])
+            target = rows_of_piece(outs[pieces[p][0]], p) if k == 0 else held(p, k, 0)
+            add_rows(target, [held(p, k, 0)] + got, pieces[p][2])
+            return
+        for side in range(2):
+            if span(p, side, d) is None:
+                continue
+            if d < half and span(p, side, d + 1) is not None:
+                ring_copy(p, k, side, d + 1).wait_recv()
+                first, rows = span(p, side, d + 1)
+                target = held(p, k, d if side == 0 else count - d)
+                term = ring_in[p].at[k, side, d]
+                if rows != pieces[p][2]:
+                    target, term = target.at[pl.ds(first, rows)], term.at[pl.ds(first, rows)]
+                add_rows(target, [target, term], rows)
+            start(ring_copy(p, k, side, d))
+
+    for d in range(half, -1, -1):
+        for p in everyone:
+            if method[p] == RING_FIRST:
+                for k in reversed(planes(p)):
+                    for q in steps(d):
+                        core_sum(p, k, q)
+                    ring_step(p, k, d)
+                    if d == 0 and k > 0:
+                        start(chip_copy(p, k, 0))
+        for p in everyone:
+            if method[p] == CHIP_FIRST:
+                for q in steps(d):
+                    for k in reversed(range(chips)):
+                        core_sum(p, k, q)
+                        if k > 0:
+                            start(chip_copy(p, k, q))
+        for p in everyone:
+            if method[p] == CHIP_FIRST and d < half:
+                for q in steps(d + 1):
+                    chip_sum(p, q)
+                ring_step(p, 0, d + 1)
+    for p in everyone:
+        if method[p] == CHIP_FIRST:
+            chip_sum(p, 0)
+            ring_step(p, 0, 0)
+    for p in everyone:
+        if method[p] == RING_FIRST:
+            chip_sum(p, 0)
+    for copy in sent:
+        copy.wait_send()
+
+
+def reduce_call(net, arrays, pieces):
+    chips, cores, count = net.chips, net.cores, net.seq_count
+    half = count // 2
+    anywhere = pl.BlockSpec(memory_space=pl.ANY)
+    shapes = [parts[0].shape[1:] for parts in arrays]
+    ahead = max(chips - 1, 1)
+    blocks = [(piece[2], shapes[piece[0]][1]) for piece in pieces]
+    chip_shapes = [
+        (ahead, count) + block if piece[3] == CHIP_FIRST else (ahead,) + block
+        for piece, block in zip(pieces, blocks)
+    ]
+    ring_shapes = [
+        (chips if piece[3] == RING_FIRST else 1, 2, half) + block
+        for piece, block in zip(pieces, blocks)
+    ]
+    n = len(pieces)
+    return pl.pallas_call(
+        functools.partial(reduce_kernel, net.order, chips, cores, pieces, len(arrays)),
+        out_shape=[jax.ShapeDtypeStruct(shape, f32) for shape in shapes],
+        in_specs=[anywhere] * sum(len(parts) for parts in arrays),
+        out_specs=[pl.BlockSpec(memory_space=pltpu.VMEM)] * len(arrays),
+        scratch_shapes=[pltpu.VMEM((chips, count) + shape, bf16) for shape in shapes]
+        + [pltpu.VMEM((chips, count) + shape, bf16) for shape in shapes]
+        + [pltpu.VMEM(shape, bf16) for shape in chip_shapes]
+        + [pltpu.VMEM(shape, bf16) for shape in ring_shapes]
+        + [
+            pltpu.SemaphoreType.DMA((len(arrays), chips)),
+            pltpu.SemaphoreType.DMA((n, chips, count)),
+            pltpu.SemaphoreType.DMA((n, chips, count)),
+            pltpu.SemaphoreType.DMA((n, ahead, count)),
+            pltpu.SemaphoreType.DMA((n, ahead, count)),
+            pltpu.SemaphoreType.DMA((n, chips, 2, half)),
+            pltpu.SemaphoreType.DMA((n, chips, 2, half)),
+        ],
+        compiler_params=pltpu.CompilerParams(
+            collective_id=4, has_side_effects=True, vmem_limit_bytes=62 * 2**20
+        ),
+        cost_estimate=pl.CostEstimate(
+            flops=0, bytes_accessed=sum(p.size for parts in arrays for p in parts) * 4, transcendentals=0
+        ),
+    )(*[part for parts in arrays for part in parts])
+
+
 def exchange(totals, everyone, send_sem, recv_sem, count):
     me = lax.axis_index("seq")
     everyone[me] = totals[...]
@@ -862,13 +1093,6 @@
     return lax.dot_general(left, right, (((0,), (0,)), ((), ())), preferred_element_type=f32)
 
 
-def total(terms):
-    result = terms[0]
-    for term in terms[1:]:
-        result = result + term
-    return result
-
-
 def per_device(
     inputs,
     reset,
@@ -951,13 +1175,9 @@
     w_ffgate, w_ffup, w_ffdown, cotangent, in_blocks[0] = lax.optimization_barrier(
         (w_ffgate, w_ffup, w_ffdown, cotangent, in_blocks[0])
     )
-    slab_gate = jnp.concatenate(net.gather_dp(w_ffgate), 0)
-    slab_up = jnp.concatenate(net.gather_dp(w_ffup), 0)
-    slab_down = jnp.concatenate(net.gather_dp(w_ffdown), 1)
     cotan_rows = cotangent.reshape(rows_here, width)
-    cot_blocks = net.seq.gather(net.columns_out(cotan_rows))
-    slots = pair_slots(seq_count)
-    group_cotan = jnp.stack([cot_blocks[k] for k in slots], 0)
+    cot_flow = Flow(net.seq.gather_steps(net.columns_out(cotan_rows)))
+    slab_flows = [Flow(net.gather_dp_steps(w)) for w in (w_ffgate, w_ffup, w_ffdown)]
 
     token_rows = inputs.reshape(rows_here, width).astype(f32)
     normed_f, scale_one, unit_one = rms_parts(token_rows, full_norm1)
@@ -965,6 +1185,7 @@
     step_cols = width // dp_count
     normed_parts = [normed[:, i * step_cols : (i + 1) * step_cols] for i in range(dp_count)]
     branch = total([dot(n, w) for n, w in zip(normed_parts, in_blocks)]).astype(bf16)
+    branch = beside(branch, cot_flow)
     gate_pre = total([dot(n, w) for n, w in zip(normed_parts, gate_blocks)])
     reset_flags = reset.reshape(rows_here).astype(bf16)
     rim_branch, rim_flags = passed_along(
@@ -1000,6 +1221,7 @@
         + full_ibias
     )
     reset_col = reset.astype(f32).reshape(rows_here, 1)
+    rate_pre, input_pre, gate_pre = beside((rate_pre, input_pre, gate_pre), cot_flow, *slab_flows)
 
     def gate_local(rate_in, input_in, conv_in, decay_in):
         return gate_math(rate_in, input_in, conv_in, decay_in, reset_col)
@@ -1015,6 +1237,7 @@
         (decay_rows, drive_rows, start_state),
         [row_shape, row_shape, jax.ShapeDtypeStruct((1, channels), f32)],
     )
+    states = beside(states, cot_flow, *slab_flows)
     final_here = initial_state.shape[1]
     final_state = lax.dynamic_slice_in_dim(
         last_state, lax.axis_index("seq") * final_here, final_here, 1
@@ -1026,6 +1249,11 @@
     mixed_parts = [mixed_rows[:, i * step_chan : (i + 1) * step_chan] for i in range(dp_count)]
     residual = token_rows + total([dot(m, w) for m, w in zip(mixed_parts, out_blocks)])
 
+    slots = pair_slots(seq_count)
+    cot_blocks = cot_flow.finish()
+    group_cotan = jnp.stack([cot_blocks[k] for k in slots], 0)
+    slab_gate, slab_up = (jnp.concatenate(flow.finish(), 0) for flow in slab_flows[:2])
+    slab_down = jnp.concatenate(slab_flows[2].finish(), 1)
     normed_two_f, scale_two, unit_two = rms_parts(residual, full_norm2)
     normed_two = net.columns_out(normed_two_f.astype(bf16))
     group_normed, hidden, d_ffgate, d_ffup, out_part, d_normed_part = ff_call(
@@ -1040,29 +1268,32 @@
         whole = whole.reshape(seq_count, rows_here, width)
         return lambda k: whole[slots.index(k)]
 
-    d_normed_sum = net.seq.scatter(block_rows(d_normed_part))
-    d_normed_sum, out_part = lax.optimization_barrier((d_normed_sum, out_part))
-    d_normed_two = net.columns_back(d_normed_sum)
-    ff_out = net.columns_back(net.seq.scatter(block_rows(out_part)))
-    gate_part = t_dot(group_normed, d_ffgate).astype(bf16)
-    up_part = t_dot(group_normed, d_ffup).astype(bf16)
-    down_part = t_dot(hidden, group_cotan).astype(bf16)
-
     def dp_chunk(whole, axis):
         size = whole.shape[axis] // dp_count
         return lambda c, k: lax.slice_in_dim(
             whole, (c * net.chips + k) * size, (c * net.chips + k + 1) * size, axis=axis
         )
 
-    grad_ffgate = net.scatter_dp(dp_chunk(gate_part, 0))
-    grad_ffup = net.scatter_dp(dp_chunk(up_part, 0))
-    grad_ffdown = net.scatter_dp(dp_chunk(down_part, 1))
-    output = (residual + ff_out).astype(bf16).reshape(seqs_here, len_here, width)
+    d_normed_flow = Flow(net.seq.scatter_steps(block_rows(d_normed_part)))
+    gate_part = beside(t_dot(group_normed, d_ffgate).astype(bf16), d_normed_flow)
+    up_part = beside(t_dot(group_normed, d_ffup).astype(bf16), d_normed_flow)
+    down_part = beside(t_dot(hidden, group_cotan).astype(bf16), d_normed_flow)
+    d_normed_sum = d_normed_flow.finish()
+    d_normed_sum, out_part, gate_part, up_part, down_part = lax.optimization_barrier(
+        (d_normed_sum, out_part, gate_part, up_part, down_part)
+    )
+    d_normed_two = net.columns_back(d_normed_sum)
+    out_flow = Flow(net.seq.scatter_steps(block_rows(out_part)))
+    ff_flows = [
+        Flow(net.scatter_dp_steps(dp_chunk(part, axis)))
+        for part, axis in ((gate_part, 0), (up_part, 0), (down_part, 1))
+    ]
 
     grad_norm2, d_resid_norm = norm_back(d_normed_two, full_norm2, scale_two, unit_two)
     d_residual = cotan_rows.astype(f32) + d_resid_norm
     d_residual_low = d_residual.astype(bf16)
     d_mixed = net.columns_back(jnp.concatenate([dot_t(d_residual_low, w) for w in out_blocks], 1))
+    d_mixed = beside(d_mixed, out_flow, *ff_flows)
     d_state = (d_mixed * gate_act).astype(bf16)
     d_gate_pre = gate_back(d_mixed * state_f)[0].astype(bf16)
     d_drive, d_decay = scan_call(
@@ -1073,18 +1304,15 @@
         [row_shape, row_shape],
     )
 
-    def grad_all(parts, right):
-        return net.scatter_all(
-            lambda c, k: t_dot(parts[c * net.chips + k], right)
-            .astype(bf16)
-            .reshape(seq_count, -1, right.shape[1])
-        )
-
-    grad_out = grad_all(mixed_parts, d_residual_low)
-    grad_gate = grad_all(normed_parts, d_gate_pre)
+    def grad_terms(parts, right):
+        return [t_dot(part, right).astype(bf16).reshape(seq_count, -1, right.shape[1]) for part in parts]
+
+    out_terms = grad_terms(mixed_parts, d_residual_low)
+    gate_terms = grad_terms(normed_parts, d_gate_pre)
     d_rate_pre, d_input_pre, d_conv_direct, grad_decay = gate_grad_fn((d_decay, d_drive))
-    d_rate_low = d_rate_pre.astype(bf16)
-    d_input_low = d_input_pre.astype(bf16)
+    d_rate_low, d_input_low = beside(
+        (d_rate_pre.astype(bf16), d_input_pre.astype(bf16)), out_flow, *ff_flows
+    )
     d_rate_heads = d_rate_low.reshape(rows_here, head_count, HW)
     d_input_heads = d_input_low.reshape(rows_here, head_count, HW)
     grad_rgate = jnp.einsum("nhi,nhj->hij", head_view, d_rate_heads, preferred_element_type=f32)
@@ -1120,8 +1348,8 @@
         )
     grad_conv = jnp.stack(conv_grads, 0)
     grad_cbias = jnp.sum(d_conv_f, axis=0)
-    d_branch_low = d_branch.astype(bf16)
-    grad_in = grad_all(normed_parts, d_branch_low)
+    d_branch_low = beside(d_branch.astype(bf16), out_flow)
+    in_terms = grad_terms(normed_parts, d_branch_low)
     d_normed_one = net.columns_back(
         jnp.concatenate(
             [
@@ -1133,6 +1361,11 @@
     )
     grad_norm1, d_token_norm = norm_back(d_normed_one, full_norm1, scale_one, unit_one)
     input_grad = (d_residual + d_token_norm).reshape(seqs_here, len_here, width)
+
+    grad_norm1, input_grad = beside((grad_norm1, input_grad), out_flow)
+    ff_out = net.columns_back(out_flow.finish())
+    output = (residual + ff_out).astype(bf16).reshape(seqs_here, len_here, width)
+    grad_ffgate, grad_ffup, grad_ffdown = (flow.finish() for flow in ff_flows)
 
     conv_flat = grad_conv.reshape(taps, devices, chan_here).transpose(1, 0, 2)
     flat_grads = jnp.concatenate(
@@ -1151,8 +1384,16 @@
         ],
         1,
     ).reshape(dp_count, seq_count, 2 * chan_here + small_rows, HW)
-    pack_mine = net.scatter_all(
-        lambda c, k: lax.dynamic_index_in_dim(pack_grads, net.dp_at(c, k), 0, keepdims=False)
+    pack_terms = [
+        lax.dynamic_index_in_dim(pack_grads, net.dp_at(c, k), 0, keepdims=False) for c, k in rel
+    ]
+    out_pieces = [(2, first, rows, RING_FIRST + CHIP_FIRST - way) for _, first, rows, way in out_pieces]
+    grad_in, grad_gate, grad_out, pack_mine = reduce_call(
+        net,
+        [in_terms, gate_terms, out_terms, pack_terms],
+        [(1, 0, wide_here, RING_FIRST)]
+        + out_pieces
+        + [(3, 0, packed.shape[0], CHIP_FIRST), (0, 0, wide_here, CHIP_FIRST)],
     )
     flat_mine = pack_mine[2 * chan_here :].reshape(-1)
     mine, at = [], 0

time: 1160 us -> 895 us (0.77)
  waiting for transfers between devices: 435 us -> 98.9 us
  Pallas kernels: 271 us -> 424 us
  starting transfers between devices: 87.6 us -> 52.5 us
  other arithmetic: 127 us -> 99.9 us
  between operations: 25.2 us -> 2.74 us
    ppermute x84 -> x42, waiting for transfers between devices: 429 us -> 85.1 us  [shift(): return lax.ppermute(value, self.axis, pairs)]
    pallas_call x0 -> x1, Pallas kernels: none -> 128 us  [reduce_call(): pl.pallas_call(functools.partial(reduce_kernel, net.order, chips, cores,...]
    ppermute x84 -> x42, starting transfers between devices: 76.2 us -> 42 us  [shift(): return lax.ppermute(value, self.axis, pairs)]
    pallas_call x2, Pallas kernels: 25.5 us -> 51.1 us  [scan_call(): pl.pallas_call(functools.partial(kernel, count), out_shape=out_shapes, in...]
    convert_element_type x31 -> x10, other arithmetic: 28.2 us -> 21.4 us  [the longest x4 10.5 us: scatter_steps(): ahead, behind = (ahead.astype(bf16), behind.astype(bf16))]
    unnamed x263 -> x236, local copies, waits for them, and re-layouts: 38 us -> 42 us
  transfers between devices with their start and end apart: 88 -> 46, of which waited for: 44 -> 12; matrix products, arithmetic and copies ran while one was open for 15% -> 19% of each run, Pallas kernels for 1% -> 6%
where the time goes in v3:
time: 895 us; the launch traced here: 885 us
  Pallas kernels  424 us (47%)
  matrix products  108 us (12%)
  other arithmetic  99.9 us (11%)
  local copies, waits for them, and re-layouts  99.1 us (11%)
  waiting for transfers between devices  98.9 us (11%)
  starting transfers between devices  52.5 us (6%)
    pallas_call x1, Pallas kernels, gather_call(): pl.pallas_call(functools.partial(gather_kernel, net.order, chips, cores,...  142 us
    pallas_call x1, Pallas kernels, reduce_call(): pl.pallas_call(functools.partial(reduce_kernel, net.order, chips, cores,...  128 us
    pallas_call x1, Pallas kernels, ff_call(): pl.pallas_call(functools.partial(ff_kernel, order), out_shape=[shape((cou...  103 us
    ppermute x42, waiting for transfers between devices, shift(): return lax.ppermute(value, self.axis, pairs)  85.1 us
    dot_general x15, matrix products, t_dot(): lax.dot_general(left, right, (((0,), (0,)), ((), ())), preferred_element_...  61.3 us
    pallas_call x2, Pallas kernels, scan_call(): pl.pallas_call(functools.partial(kernel, count), out_shape=out_shapes, in...  51.1 us
    ppermute x42, starting transfers between devices, shift(): return lax.ppermute(value, self.axis, pairs)  42 us
    unnamed x236, local copies, waits for them, and re-layouts  42 us
  transfers between devices with their start and end apart: 46, of which 12 were waited for; matrix products, arithmetic and copies ran while one was open for 19% of the time, Pallas kernels for 6%

profile of v3, /device:TPU:0, one launch (start us, length us, event | category | flops | bytes accessed | tf_op | source)
XLA Modules:
  0.0 884.6 jit_solution(1088940434507275797)
XLA Ops:
  1.5 4.1 concatenate.86
  10.0 142.1 %shard_map.322 = (bf16[4,8,176,256]{3,2,1,0:T(8,128)(2,1)S(1)}, bf16[4,8,64,2560]{3,2,1,0:T(8,128)(2,1)S(1)}, bf16[4,8,64,2560]{3,2,1,0:T(8,128)(2,1)}, bf16[4,8...) custom-call(bf16[176,256]{1,0:T(8,128)(2,1)S(1)} %pad_maximum_fusion.15.refs_0_, bf16[64,2560]{1,0:T(8,128)(2,1)S(1)} %copy-done.8, ...), custom_call_target="tpu_custom_call" | custom-call | bytes 68722688 | tf_op jit(solution)/shard_map/pallas_call | solution.py:399
  153.7 9.7 %fusion.107 = (bf16[1,8,64,2560]{3,2,1,0:T(8,128)(2,1)}, bf16[1,8,64,2560]{3,2,1,0:T(8,128)(2,1)}, bf16[1,8,64,2560]{3,2,1,0:T(8,128)(2,1)}, bf16[1,8,64,2560]{3...) fusion(bf16[4,8,64,2560]{3,2,1,0:T(8,128)(2,1)} %get-tuple-elem, ...), kind=kLoop, calls=%fused_computation.309 | loop fusion | bytes 41943040 | tf_op jit(solution)/shard_map/slice | solution.py:1171
  169.9 4.5 collective-permute-start.3
  179.5 4.5 fusion.71
  216.1 13.8 %collective-permute-done.2 = bf16[3,2560]{1,0:T(4,128)(2,1)S(1)} collective-permute-done((bf16[3,2560]{1,0:T(4,128)(2,1)S(1)}, bf16[3,2560]{1,0:T(4,128)(2,1)S(1)}, u32[]{:S(2)}, u32[]{:S(2)}) %collective-permute-start.2) | collective-permute-done | bytes 15392 | tf_op jit(solution)/shard_map/ppermute | solution.py:1047
  256.9 6.1 convert_multiply_fusion.3
  263.0 21.5 %shard_map.323 = (f32[256,2560]{1,0:T(8,128)S(1)}, f32[256,2560]{1,0:T(8,128)S(1)}, f32[1,2560]{1,0:T(1,128)S(1)}) custom-call(f32[256,2560]{1,0:T(8,128)S(1)} %get-tuple-element.252.decay_ref, f32[256,2560]{1,0:T(8,128)S(1)} %get-tuple-element.251.drive_ref, f32[1,2560]{1,0:T(1,128)S(1)} %reshape.383.start_ref), custom_call_target="tpu_custom_call" | custom-call | flops 5242880 | bytes 13107200 | tf_op jit(solution)/shard_map/pallas_call | solution.py:808
  316.7 102.7 %shard_map.324 = (bf16[8,256,2048]{2,1,0:T(8,128)(2,1)}, bf16[4,512,768]{2,1,0:T(8,128)(2,1)S(1)}, bf16[4,512,768]{2,1,0:T(8,128)(2,1)}, bf16[4,512,768]{2,1,0:T...) custom-call(bf16[256,2048]{1,0:T(8,128)(2,1)S(1)} %pad_maximum_fusion.10.own_ref, ...), custom_call_target="tpu_custom_call" | custom-call | flops 38654705664 | bytes 62914560 | tf_op jit(solution)/shard_map/pallas_call | solution.py:1012
  424.4 10.7 %convolution_convert_fusion.9 = bf16[2048,768]{1,0:T(8,128)(2,1)} fusion(bf16[2048,2048]{1,0:T(8,128)(2,1)} %bitcast.353, bf16[2048,768]{1,0:T(8,128)(2,1)S(1)} %bitcast.358), kind=kOutput, calls=%fused_computation.20 | convolution fusion | flops 6444023808 | bytes 14680064 | tf_op jit(solution)/shard_map/dot_general | solution.py:1093
  437.8 8.5 convolution_convert_fusion.10
  446.3 10.2 %collective-permute-done.21 = bf16[256,2048]{1,0:T(8,128)(2,1)S(1)} collective-permute-done((bf16[256,2048]{1,0:T(8,128)(2,1)S(1)}, bf16[256,2048]{1,0:T(8,128)(2,1)S(1)}, u32[]{:S(2)}, u32[]{:S(2)}) %collective-permute-start.21) | collective-permute-done | bytes 1048608 | tf_op jit(solution)/shard_map/ppermute | solution.py:43
  463.2 10.4 %convolution_convert_fusion.8 = bf16[768,2048]{1,0:T(8,128)(2,1)} fusion(bf16[2048,768]{1,0:T(8,128)(2,1)S(1)} %bitcast.267, bf16[2048,2048]{1,0:T(8,128)(2,1)} %bitcast.41), kind=kOutput, calls=%fused_computation.19 | convolution fusion | flops 6444023808 | bytes 14680064 | tf_op jit(solution)/shard_map/dot_general | solution.py:1093
  473.6 8.2 collective-permute-done.24
  486.6 15.3 %collective-permute-done.25 = bf16[256,2048]{1,0:T(8,128)(2,1)} collective-permute-done((bf16[256,2048]{1,0:T(8,128)(2,1)}, bf16[256,2048]{1,0:T(8,128)(2,1)}, u32[]{:S(2)}, u32[]{:S(2)}) %collective-permute-start.25) | collective-permute-done | bytes 1048608 | tf_op jit(solution)/shard_map/ppermute | solution.py:43
  534.4 10.1 %collective-permute-done.28 = bf16[128,2048]{1,0:T(8,128)(2,1)S(1)} collective-permute-done((bf16[128,2048]{1,0:T(8,128)(2,1)S(1)}, bf16[128,2048]{1,0:T(8,128)(2,1)S(1)}, u32[]{:S(2)}, u32[]{:S(2)}) %collective-permute-start.28) | collective-permute-done | bytes 524320 | tf_op jit(solution)/shard_map/ppermute | solution.py:43
  587.6 29.6 %shard_map.325 = (f32[256,2560]{1,0:T(8,128)S(1)}, f32[256,2560]{1,0:T(8,128)S(1)}) custom-call(f32[256,2560]{1,0:T(8,128)S(1)} %get-tuple-element.252.decay_ref, f32[256,2560]{1,0:T(8,128)S(1)} %get-tuple-element.236.d_state_ref, f32[256,2560]{1,0:T(8,128)S(1)} %copy-done.7), custom_call_target="tpu_custom_call" | custom-call | flops 5242880 | bytes 13107200 | tf_op jit(solution)/shard_map/pallas_call | solution.py:808
  617.2 7.6 multiply_reduce_fusion
  642.5 4.6 fusion.32
  654.1 5.7 add_convert_fusion
  677.0 4.3 multiply_reduce_fusion.4
  681.9 15.8 %collective-permute-done.42 = bf16[256,2048]{1,0:T(8,128)(2,1)} collective-permute-done((bf16[256,2048]{1,0:T(8,128)(2,1)}, bf16[256,2048]{1,0:T(8,128)(2,1)}, u32[]{:S(2)}, u32[]{:S(2)}) %collective-permute-start.42) | collective-permute-done | bytes 1048608 | tf_op jit(solution)/shard_map/ppermute | solution.py:43
  723.6 16.0 %collective-permute-done.45 = bf16[256,2048]{1,0:T(8,128)(2,1)} collective-permute-done((bf16[256,2048]{1,0:T(8,128)(2,1)S(1)}, bf16[256,2048]{1,0:T(8,128)(2,1)}, u32[]{:S(2)}, u32[]{:S(2)}) %collective-permute-start.45) | collective-permute-done | bytes 1048608 | tf_op jit(solution)/shard_map/ppermute | solution.py:43
  743.2 128.0 %shard_map.326 = (f32[64,2560]{1,0:T(8,128)}, f32[64,2560]{1,0:T(8,128)}, f32[80,2048]{1,0:T(8,128)}, f32[176,256]{1,0:T(8,128)}) custom-call(bf16[8,64,2560]{2,1,0:T(8,128)(2,1)} %bitcast.291, bf16[8,64,2560]{2,1,0:T(8,128)(2,1)} %bitcast.290, bf16[8,64,2560]{2,1,0:T(8,128)(2,1)} %bitcast.289, bf16[8,64,2560]{2,1,0:T(8,128)(2,1)} %bitcast.288, ...), custom_call_target="tpu_custom_call" | custom-call | bytes 68681728 | tf_op jit(solution)/shard_map/pallas_call | solution.py:627
  (499 shorter events, 288.0 us)
Async XLA Ops:
  166.5 38.8 %collective-permute-start.1 = (bf16[256,2048]{1,0:T(8,128)(2,1)}, bf16[256,2048]{1,0:T(8,128)(2,1)}, u32[]{:S(2)}, u32[]{:S(2)}) collective-permute-start(bf16[256,2048]{1,0:T(8,128)(2,1)} %pad_maximum_fusion.9), channel_id=1, source_target_pairs={{1,0},{3,1},{5,3},{7,5},{6,7},{4,6},{2,4},{0,2},{9,8},{11,9},{13,1... | collective-permute-start | bytes 3145736 | tf_op jit(solution)/shard_map/ppermute | solution.py:43
  168.0 37.3 %collective-permute-start = (bf16[256,2048]{1,0:T(8,128)(2,1)}, bf16[256,2048]{1,0:T(8,128)(2,1)}, u32[]{:S(2)}, u32[]{:S(2)}) collective-permute-start(bf16[256,2048]{1,0:T(8,128)(2,1)} %pad_maximum_fusion.9), channel_id=1, source_target_pairs={{1,3},{3,5},{5,7},{7,6},{6,4},{4,2},{2,0},{0,1},{9,11},{11,13},{13... | collective-permute-start | bytes 3145736 | tf_op jit(solution)/shard_map/ppermute | solution.py:43
  168.6 34.5 %collective-permute-start.41 = (bf16[3]{0:T(256)(128)(2,1)S(1)}, bf16[3]{0:T(256)(128)(2,1)S(1)}, u32[]{:S(2)}, u32[]{:S(2)}) collective-permute-start(bf16[3]{0:T(256)(128)(2,1)S(1)} %get-tuple-element.292), channel_id=1, source_target_pairs={{1,0},{2,1},{3,2},{4,3},{5,4},{6,5},{7,6},{9,8},{10,9},{11,10},{12... | collective-permute-start | bytes 26 | tf_op jit(solution)/shard_map/ppermute | solution.py:1047
  169.9 34.7 %collective-permute-start.3 = (bf16[3]{0:T(256)(128)(2,1)S(1)}, bf16[3]{0:T(256)(128)(2,1)S(1)}, u32[]{:S(2)}, u32[]{:S(2)}) collective-permute-start(bf16[3]{0:T(256)(128)(2,1)S(1)} %get-tuple-element.293), channel_id=1, source_target_pairs={{0,1},{1,2},{2,3},{3,4},{4,5},{5,6},{6,7},{8,9},{9,10},{10,11},{11... | collective-permute-start | bytes 26 | tf_op jit(solution)/shard_map/ppermute | solution.py:1047
  174.5 79.0 %collective-permute-start.6 = (bf16[512,768]{1,0:T(8,128)(2,1)}, bf16[512,768]{1,0:T(8,128)(2,1)}, u32[]{:S(2)}, u32[]{:S(2)}) collective-permute-start(bf16[512,768]{1,0:T(8,128)(2,1)} %param.35), channel_id=1, source_target_pairs={{0,16},{16,0},{8,24},{24,8},{1,17},{17,1},{9,25},{25,9},{2,18},{18... | collective-permute-start | bytes 2359304 | tf_op jit(solution)/shard_map/ppermute | solution.py:43
  203.2 51.1 %collective-permute-start.7 = (bf16[512,768]{1,0:T(8,128)(2,1)}, bf16[512,768]{1,0:T(8,128)(2,1)}, u32[]{:S(2)}, u32[]{:S(2)}) collective-permute-start(bf16[512,768]{1,0:T(8,128)(2,1)} %param.36), channel_id=1, source_target_pairs={{0,16},{16,0},{8,24},{24,8},{1,17},{17,1},{9,25},{25,9},{2,18},{18... | collective-permute-start | bytes 2359304 | tf_op jit(solution)/shard_map/ppermute | solution.py:43
  204.6 50.1 %collective-permute-start.8 = (bf16[768,512]{1,0:T(8,128)(2,1)}, bf16[768,512]{1,0:T(8,128)(2,1)}, u32[]{:S(2)}, u32[]{:S(2)}) collective-permute-start(bf16[768,512]{1,0:T(8,128)(2,1)} %param.37), channel_id=1, source_target_pairs={{0,16},{16,0},{8,24},{24,8},{1,17},{17,1},{9,25},{25,9},{2,18},{18... | collective-permute-start | bytes 2359304 | tf_op jit(solution)/shard_map/ppermute | solution.py:43
  205.4 49.5 %collective-permute-start.4 = (bf16[256,2048]{1,0:T(8,128)(2,1)}, bf16[256,2048]{1,0:T(8,128)(2,1)}, u32[]{:S(2)}, u32[]{:S(2)}) collective-permute-start(bf16[256,2048]{1,0:T(8,128)(2,1)} %collective-permute-done), channel_id=1, source_target_pairs={{1,3},{3,5},{5,7},{7,6},{6,4},{4,2},{2,0},{0,1},{9,11},{11,13},{13... | collective-permute-start | bytes 3145736 | tf_op jit(solution)/shard_map/ppermute | solution.py:43
  230.0 24.9 %collective-permute-start.5 = (bf16[256,2048]{1,0:T(8,128)(2,1)}, bf16[256,2048]{1,0:T(8,128)(2,1)}, u32[]{:S(2)}, u32[]{:S(2)}) collective-permute-start(bf16[256,2048]{1,0:T(8,128)(2,1)} %collective-permute-done.1), channel_id=1, source_target_pairs={{1,0},{3,1},{5,3},{7,5},{6,7},{4,6},{2,4},{0,2},{9,8},{11,9},{13,1... | collective-permute-start | bytes 3145736 | tf_op jit(solution)/shard_map/ppermute | solution.py:43
  254.3 30.3 %collective-permute-start.11 = (bf16[512,768]{1,0:T(8,128)(2,1)S(1)}, bf16[512,768]{1,0:T(8,128)(2,1)S(1)}, u32[]{:S(2)}, u32[]{:S(2)}) collective-permute-start(bf16[512,768]{1,0:T(8,128)(2,1)S(1)} %copy-done.83), channel_id=1, source_target_pairs={{0,8},{8,0},{16,24},{24,16},{1,9},{9,1},{17,25},{25,17},{2,10},{10... | collective-permute-start | bytes 2359304 | tf_op jit(solution)/shard_map/ppermute | solution.py:43
  254.3 30.3 %collective-permute-start.13 = (bf16[512,768]{1,0:T(8,128)(2,1)}, bf16[512,768]{1,0:T(8,128)(2,1)S(1)}, u32[]{:S(2)}, u32[]{:S(2)}) collective-permute-start(bf16[512,768]{1,0:T(8,128)(2,1)} %param.36), channel_id=1, source_target_pairs={{0,8},{8,0},{16,24},{24,16},{1,9},{9,1},{17,25},{25,17},{2,10},{10... | collective-permute-start | bytes 2359304 | tf_op jit(solution)/shard_map/ppermute | solution.py:43
  254.8 30.3 %collective-permute-start.15 = (bf16[768,512]{1,0:T(8,128)(2,1)}, bf16[768,512]{1,0:T(8,128)(2,1)S(1)}, u32[]{:S(2)}, u32[]{:S(2)}) collective-permute-start(bf16[768,512]{1,0:T(8,128)(2,1)} %param.37), channel_id=1, source_target_pairs={{0,8},{8,0},{16,24},{24,16},{1,9},{9,1},{17,25},{25,17},{2,10},{10... | collective-permute-start | bytes 2359304 | tf_op jit(solution)/shard_map/ppermute | solution.py:43
  254.9 35.9 %collective-permute-start.9 = (bf16[256,2048]{1,0:T(8,128)(2,1)}, bf16[256,2048]{1,0:T(8,128)(2,1)S(1)}, u32[]{:S(2)}, u32[]{:S(2)}) collective-permute-start(bf16[256,2048]{1,0:T(8,128)(2,1)} %collective-permute-done.4), channel_id=1, source_target_pairs={{1,3},{3,5},{5,7},{7,6},{6,4},{4,2},{2,0},{0,1},{9,11},{11,13},{13... | collective-permute-start | bytes 3145736 | tf_op jit(solution)/shard_map/ppermute | solution.py:43
  255.7 35.0 %collective-permute-start.10 = (bf16[256,2048]{1,0:T(8,128)(2,1)}, bf16[256,2048]{1,0:T(8,128)(2,1)S(1)}, u32[]{:S(2)}, u32[]{:S(2)}) collective-permute-start(bf16[256,2048]{1,0:T(8,128)(2,1)} %collective-permute-done.5), channel_id=1, source_target_pairs={{1,0},{3,1},{5,3},{7,5},{6,7},{4,6},{2,4},{0,2},{9,8},{11,9},{13,1... | collective-permute-start | bytes 3145736 | tf_op jit(solution)/shard_map/ppermute | solution.py:43
  290.8 23.7 %collective-permute-start.18 = (bf16[128,2048]{1,0:T(8,128)(2,1)S(1)}, bf16[128,2048]{1,0:T(8,128)(2,1)S(1)}, u32[]{:S(2)}, u32[]{:S(2)}) collective-permute-start(bf16[128,2048]{1,0:T(8,128)(2,1)S(1)} %slice.417), channel_id=1, source_target_pairs={{1,0},{3,1},{5,3},{7,5},{6,7},{4,6},{2,4},{0,2},{9,8},{11,9},{13,1... | collective-permute-start | bytes 1572872 | tf_op jit(solution)/shard_map/ppermute | solution.py:43
  525.1 26.2 %collective-permute-start.29 = (bf16[512,768]{1,0:T(8,128)(2,1)}, bf16[512,768]{1,0:T(8,128)(2,1)}, u32[]{:S(2)}, u32[]{:S(2)}) collective-permute-start(bf16[512,768]{1,0:T(8,128)(2,1)} %get-tuple-element.243), channel_id=1, source_target_pairs={{0,8},{8,0},{16,24},{24,16},{1,9},{9,1},{17,25},{25,17},{2,10},{10... | collective-permute-start | bytes 2359304 | tf_op jit(solution)/shard_map/ppermute | solution.py:43
  527.5 23.8 %collective-permute-start.32 = (bf16[512,768]{1,0:T(8,128)(2,1)}, bf16[512,768]{1,0:T(8,128)(2,1)}, u32[]{:S(2)}, u32[]{:S(2)}) collective-permute-start(bf16[512,768]{1,0:T(8,128)(2,1)} %get-tuple-element.240), channel_id=1, source_target_pairs={{0,8},{8,0},{16,24},{24,16},{1,9},{9,1},{17,25},{25,17},{2,10},{10... | collective-permute-start | bytes 2359304 | tf_op jit(solution)/shard_map/ppermute | solution.py:43
  578.3 51.1 %collective-permute-start.39 = (bf16[768,512]{1,0:T(8,128)(2,1)}, bf16[768,512]{1,0:T(8,128)(2,1)}, u32[]{:S(2)}, u32[]{:S(2)}) collective-permute-start(bf16[768,512]{1,0:T(8,128)(2,1)} %add_convert_fusion.2), channel_id=1, source_target_pairs={{0,16},{16,0},{8,24},{24,8},{1,17},{17,1},{9,25},{25,9},{2,18},{18... | collective-permute-start | bytes 2359304 | tf_op jit(solution)/shard_map/ppermute | solution.py:43
  579.7 49.7 %collective-permute-start.38 = (bf16[512,768]{1,0:T(8,128)(2,1)}, bf16[512,768]{1,0:T(8,128)(2,1)}, u32[]{:S(2)}, u32[]{:S(2)}) collective-permute-start(bf16[512,768]{1,0:T(8,128)(2,1)} %add_convert_fusion.3), channel_id=1, source_target_pairs={{0,16},{16,0},{8,24},{24,8},{1,17},{17,1},{9,25},{25,9},{2,18},{18... | collective-permute-start | bytes 2359304 | tf_op jit(solution)/shard_map/ppermute | solution.py:43
  580.3 51.6 %collective-permute-start.37 = (bf16[512,768]{1,0:T(8,128)(2,1)S(1)}, bf16[512,768]{1,0:T(8,128)(2,1)}, u32[]{:S(2)}, u32[]{:S(2)}) collective-permute-start(bf16[512,768]{1,0:T(8,128)(2,1)S(1)} %add_convert_fusion.4), channel_id=1, source_target_pairs={{0,16},{16,0},{8,24},{24,8},{1,17},{17,1},{9,25},{25,9},{2,18},{18... | collective-permute-start | bytes 2359304 | tf_op jit(solution)/shard_map/ppermute | solution.py:43
  584.4 47.6 %collective-permute-start.35 = (bf16[256,2048]{1,0:T(8,128)(2,1)}, bf16[256,2048]{1,0:T(8,128)(2,1)}, u32[]{:S(2)}, u32[]{:S(2)}) collective-permute-start(bf16[256,2048]{1,0:T(8,128)(2,1)} %pad_maximum_fusion.13), channel_id=1, source_target_pairs={{1,3},{3,5},{5,7},{7,6},{6,4},{4,2},{2,0},{0,1},{9,11},{11,13},{13... | collective-permute-start | bytes 3145736 | tf_op jit(solution)/shard_map/ppermute | solution.py:43
  587.1 44.9 %collective-permute-start.36 = (bf16[256,2048]{1,0:T(8,128)(2,1)}, bf16[256,2048]{1,0:T(8,128)(2,1)}, u32[]{:S(2)}, u32[]{:S(2)}) collective-permute-start(bf16[256,2048]{1,0:T(8,128)(2,1)} %pad_maximum_fusion.14), channel_id=1, source_target_pairs={{1,0},{3,1},{5,3},{7,5},{6,7},{4,6},{2,4},{0,2},{9,8},{11,9},{13,1... | collective-permute-start | bytes 3145736 | tf_op jit(solution)/shard_map/ppermute | solution.py:43
  647.1 34.8 %collective-permute-start.43 = (bf16[256,2048]{1,0:T(8,128)(2,1)}, bf16[256,2048]{1,0:T(8,128)(2,1)}, u32[]{:S(2)}, u32[]{:S(2)}) collective-permute-start(bf16[256,2048]{1,0:T(8,128)(2,1)} %get-tuple-element.218), channel_id=1, source_target_pairs={{1,0},{3,1},{5,3},{7,5},{6,7},{4,6},{2,4},{0,2},{9,8},{11,9},{13,1... | collective-permute-start | bytes 3145736 | tf_op jit(solution)/shard_map/ppermute | solution.py:43
  672.4 25.3 %collective-permute-start.42 = (bf16[256,2048]{1,0:T(8,128)(2,1)}, bf16[256,2048]{1,0:T(8,128)(2,1)}, u32[]{:S(2)}, u32[]{:S(2)}) collective-permute-start(bf16[256,2048]{1,0:T(8,128)(2,1)} %get-tuple-element.219), channel_id=1, source_target_pairs={{1,3},{3,5},{5,7},{7,6},{6,4},{4,2},{2,0},{0,1},{9,11},{11,13},{13... | collective-permute-start | bytes 3145736 | tf_op jit(solution)/shard_map/ppermute | solution.py:43
  (134 other events, 907.3 us)

commit v4 on v3

--- a/solution.py
+++ b/solution.py
@@ -65,9 +65,9 @@
                 self.shift(behind[: rows // 2], 1),
                 self.shift(ahead[rows // 2 :], -1),
             ]
-            blocks[half] = jnp.concatenate([top, bottom], 0)
+            blocks[half] = [top, bottom]
         else:
-            (blocks[half],) = yield [self.shift(behind, 1)]
+            blocks[half] = yield [self.shift(behind, 1)]
         return blocks
 
     def scatter_steps(self, part):
@@ -129,51 +129,6 @@
         self.seq = Ring("seq", [self.order])
         self.cores = 2 if self.dp_count % 2 == 0 else 1
         self.chips = self.dp_count // self.cores
-        cores, chips = self.cores, self.chips
-        self.chip = Ring("dp", [[o * cores + c for o in range(chips)] for c in range(cores)])
-        self.core = Ring("dp", [[o * cores + c for c in range(cores)] for o in range(chips)])
-        self.place = self.seq.place()
-        dp = lax.axis_index("dp")
-        self.my_chip, self.my_core = dp // cores, dp % cores
-
-    def seq_at(self, k):
-        return jnp.asarray(self.order, jnp.int32)[(self.place + k) % self.seq_count]
-
-    def rel(self):
-        return [(c, k) for c in range(self.cores) for k in range(self.chips)]
-
-    def dp_at(self, c, k):
-        return ((self.my_chip + k) % self.chips) * self.cores + (self.my_core + c) % self.cores
-
-    def columns_out(self, values):
-        chunk = values.shape[1] // self.dp_count
-        return jnp.concatenate(
-            [lax.dynamic_slice_in_dim(values, self.dp_at(c, k) * chunk, chunk, 1) for c, k in self.rel()],
-            1,
-        )
-
-    def columns_back(self, values):
-        chunk = values.shape[1] // self.dp_count
-        pieces = []
-        for dp in range(self.dp_count):
-            chip, core = dp // self.cores, dp % self.cores
-            at = ((core - self.my_core) % self.cores) * self.chips + (chip - self.my_chip) % self.chips
-            pieces.append(lax.dynamic_slice_in_dim(values, at * chunk, chunk, 1))
-        return jnp.concatenate(pieces, 1)
-
-    def gather_dp_steps(self, value):
-        blocks = yield from self.chip.gather_steps(value)
-        if self.cores == 1:
-            return blocks
-        others = yield [self.core.shift(block, 1) for block in blocks]
-        return blocks + others
-
-    def scatter_dp_steps(self, part):
-        sums = [part(0, k) for k in range(self.chips)]
-        if self.cores > 1:
-            got = yield [self.core.shift(part(1, k).astype(bf16), 1) for k in range(self.chips)]
-            sums = [mine.astype(f32) + theirs.astype(f32) for mine, theirs in zip(sums, got)]
-        return (yield from self.chip.scatter_steps(lambda k: sums[k]))
 
 
 def lookup(table, index):
@@ -200,6 +155,11 @@
             {"dp": lax.rem(chip + step, chips) * cores + core} for step in range(1, chips)
         ]
         self.core = {"dp": chip * cores + (1 - core)} if cores == 2 else None
+        self.dp_at = [
+            lax.rem(chip + k, chips) * cores + lax.rem(core + c, cores)
+            for c in range(cores)
+            for k in range(chips)
+        ]
 
     def greet(self):
         barrier = pltpu.get_barrier_semaphore()
@@ -231,9 +191,16 @@
     links = Links(order, chips, cores)
     count, half = links.count, links.count // 2
     links.greet()
+    method = [piece[3] for piece in pieces]
+    only_ring = {piece[0] for piece in pieces if piece[3] == RING_ONLY}
+
+    base = [sum(chips if way == CHIP_FIRST else 1 for way in method[:p]) for p in range(len(pieces) + 1)]
+
+    def slot(i, r, k):
+        return outs[i].at[0 if i in only_ring else links.dp_at[r], links.seq_at[k]]
 
     owns = [
-        pltpu.make_async_copy(ins[i], outs[i].at[0, links.seq_at[0]], own_sem.at[i])
+        pltpu.make_async_copy(ins[i], slot(i, 0, 0), own_sem.at[i])
         for i in range(arrays)
     ]
     for copy in owns:
@@ -242,11 +209,11 @@
 
     def whole(p, r, k):
         array, first, rows, _ = pieces[p]
-        place = outs[array].at[r, links.seq_at[k]]
+        place = slot(array, r, k)
         return place if rows == ins[array].shape[0] else place.at[pl.ds(first, rows)]
 
     def rows_in(p, r, k, first, rows):
-        return outs[pieces[p][0]].at[r, links.seq_at[k], pl.ds(pieces[p][1] + first, rows)]
+        return slot(pieces[p][0], r, k).at[pl.ds(pieces[p][1] + first, rows)]
 
     def held(p, r, k):
         array, first, rows, _ = pieces[p]
@@ -267,11 +234,11 @@
             return [
                 remote(
                     held(p, r, (count - s) % count), whole(p, r, (count - s) % count),
-                    ring_sem.at[p, r, 0, s], recv_sem.at[p, r, count - s - 1], links.ring[0],
+                    ring_sem.at[base[p] + r, 0, s], recv_sem.at[p, r, count - s - 1], links.ring[0],
                 ),
                 remote(
                     held(p, r, s), whole(p, r, s),
-                    ring_sem.at[p, r, 1, s], recv_sem.at[p, r, s + 1], links.ring[1],
+                    ring_sem.at[base[p] + r, 1, s], recv_sem.at[p, r, s + 1], links.ring[1],
                 ),
             ]
         back = count - s
@@ -279,14 +246,14 @@
             return [
                 remote(
                     whole(p, r, back), whole(p, r, back),
-                    ring_sem.at[p, r, 0, s], recv_sem.at[p, r, half], links.ring[0],
+                    ring_sem.at[base[p] + r, 0, s], recv_sem.at[p, r, half], links.ring[0],
                 )
             ]
         top, bottom = rows_in(p, r, back, 0, cut), rows_in(p, r, s, cut, rows - cut)
         return [
-            remote(top, top, ring_sem.at[p, r, 0, s], recv_sem.at[p, r, half], links.ring[0]),
+            remote(top, top, ring_sem.at[base[p] + r, 0, s], recv_sem.at[p, r, half], links.ring[0]),
             remote(
-                bottom, bottom, ring_sem.at[p, r, 1, s], recv_sem.at[p, r, count], links.ring[1]
+                bottom, bottom, ring_sem.at[base[p] + r, 1, s], recv_sem.at[p, r, count], links.ring[1]
             ),
         ]
 
@@ -295,16 +262,16 @@
         if k == half and cut:
             for part, sem in (((0, cut), half), ((cut, rows - cut), count)):
                 ref = rows_in(p, r, k, *part)
-                remote(ref, ref, ring_sem.at[p, r, 0, 0], recv_sem.at[p, r, sem], links.ring[0]).wait_recv()
+                remote(ref, ref, ring_sem.at[base[p], 0, 0], recv_sem.at[p, r, sem], links.ring[0]).wait_recv()
         else:
             ref = whole(p, r, k)
-            remote(ref, ref, ring_sem.at[p, r, 0, 0], recv_sem.at[p, r, k], links.ring[0]).wait_recv()
+            remote(ref, ref, ring_sem.at[base[p], 0, 0], recv_sem.at[p, r, k], links.ring[0]).wait_recv()
 
     def to_chips(p, k):
         for step in range(1, chips):
             start(
                 remote(
-                    held(p, 0, k), whole(p, chips - step, k),
+                    held(p, 0, k), whole(p, 0, k),
                     chip_sem.at[p, step - 1, k], recv_sem.at[p, chips - step, k], links.chip[step - 1],
                 )
             )
@@ -313,12 +280,11 @@
         if cores == 2:
             start(
                 remote(
-                    held(p, r, k), whole(p, chips + r, k),
+                    held(p, r, k), whole(p, r, k),
                     core_sem.at[p, r, k], recv_sem.at[p, chips + r, k], links.core,
                 )
             )
 
-    method = [piece[3] for piece in pieces]
     everyone = range(len(pieces))
 
     def planes(p):
@@ -407,7 +373,9 @@
         scratch_shapes=[
             pltpu.SemaphoreType.DMA((len(arrays),)),
             pltpu.SemaphoreType.DMA((len(pieces), slots, count + 1)),
-            pltpu.SemaphoreType.DMA((len(pieces), chips, 2, count // 2)),
+            pltpu.SemaphoreType.DMA(
+                (sum(chips if piece[3] == CHIP_FIRST else 1 for piece in pieces), 2, count // 2)
+            ),
             pltpu.SemaphoreType.DMA((len(pieces), max(chips - 1, 1), count)),
             pltpu.SemaphoreType.DMA((len(pieces), chips, count)),
         ],
@@ -441,10 +409,8 @@
 
 
 def reduce_kernel(order, chips, cores, pieces, arrays, *refs):
-    slots = chips * cores
     count, half = len(order), len(order) // 2
-    parts = [refs[i * slots : (i + 1) * slots] for i in range(arrays)]
-    refs = refs[arrays * slots :]
+    parts, refs = refs[:arrays], refs[arrays:]
     outs, refs = refs[:arrays], refs[arrays:]
     mine, refs = refs[:arrays], refs[arrays:]
     other, refs = refs[:arrays], refs[arrays:]
@@ -457,7 +423,7 @@
 
     loads = [
         [
-            pltpu.make_async_copy(parts[i][k], mine[i].at[k], load_sem.at[i, k])
+            pltpu.make_async_copy(parts[i].at[links.dp_at[k]], mine[i].at[k], load_sem.at[i, k])
             for k in range(chips)
         ]
         for i in range(arrays)
@@ -485,7 +451,7 @@
     def core_copy(p, k, q):
         array = pieces[p][0]
         return remote(
-            rows_of_piece(parts[array][chips + k].at[links.seq_at[q]], p),
+            rows_of_piece(parts[array].at[links.dp_at[chips + k], links.seq_at[q]], p),
             rows_of_piece(other[array].at[k, links.seq_at[q]], p),
             core_send.at[p, k, q], core_recv.at[p, k, q], links.core,
         )
@@ -612,7 +578,7 @@
     chips, cores, count = net.chips, net.cores, net.seq_count
     half = count // 2
     anywhere = pl.BlockSpec(memory_space=pl.ANY)
-    shapes = [parts[0].shape[1:] for parts in arrays]
+    shapes = [terms.shape[2:] for terms in arrays]
     ahead = max(chips - 1, 1)
     blocks = [(piece[2], shapes[piece[0]][1]) for piece in pieces]
     chip_shapes = [
@@ -627,7 +593,7 @@
     return pl.pallas_call(
         functools.partial(reduce_kernel, net.order, chips, cores, pieces, len(arrays)),
         out_shape=[jax.ShapeDtypeStruct(shape, f32) for shape in shapes],
-        in_specs=[anywhere] * sum(len(parts) for parts in arrays),
+        in_specs=[anywhere] * len(arrays),
         out_specs=[pl.BlockSpec(memory_space=pltpu.VMEM)] * len(arrays),
         scratch_shapes=[pltpu.VMEM((chips, count) + shape, bf16) for shape in shapes]
         + [pltpu.VMEM((chips, count) + shape, bf16) for shape in shapes]
@@ -646,9 +612,9 @@
             collective_id=4, has_side_effects=True, vmem_limit_bytes=62 * 2**20
         ),
         cost_estimate=pl.CostEstimate(
-            flops=0, bytes_accessed=sum(p.size for parts in arrays for p in parts) * 4, transcendentals=0
+            flops=0, bytes_accessed=sum(terms.size for terms in arrays) * 4, transcendentals=0
         ),
-    )(*[part for parts in arrays for part in parts])
+    )(*arrays)
 
 
 def exchange(totals, everyone, send_sem, recv_sem, count):
@@ -825,6 +791,82 @@
     )(*operands)
 
 
+def gate_parts(conv_ref, both_ref, vectors_ref, reset_ref):
+    conv = conv_ref[...].astype(f32)
+    pre = contract(conv_ref[...], both_ref[...], 1, 0)
+    rate = jax.nn.sigmoid(pre[:, :HW] + vectors_ref[0:1])
+    in_gate = jax.nn.sigmoid(pre[:, HW:] + vectors_ref[1:2])
+    log_decay = vectors_ref[2:3] * rate
+    reset = reset_ref[...]
+    keep = 1.0 - reset
+    decay = jnp.exp(log_decay)
+    bend = jnp.tanh(-log_decay)
+    power = 2.0 * bend / (1.0 + bend)
+    root = jnp.sqrt(jnp.maximum(power, floor_value))
+    return conv, rate, in_gate, decay, keep, power, root, reset + keep * root
+
+
+def gate_kernel(conv_ref, both_ref, vectors_ref, reset_ref, decay_ref, drive_ref):
+    conv, _, in_gate, decay, keep, _, _, share = gate_parts(
+        conv_ref, both_ref, vectors_ref, reset_ref
+    )
+    decay_ref[...] = decay * keep
+    drive_ref[...] = share * in_gate * conv
+
+
+def gate_back_kernel(
+    conv_ref, both_ref, vectors_ref, reset_ref, d_decay_ref, d_drive_ref,
+    d_conv_ref, grad_ref, sums_ref,
+):
+    conv, rate, in_gate, decay, keep, power, root, share = gate_parts(
+        conv_ref, both_ref, vectors_ref, reset_ref
+    )
+    d_drive = d_drive_ref[...]
+    through = jnp.where(
+        power > floor_value, d_drive * keep * in_gate * conv * (decay * decay) / root, 0.0
+    )
+    d_log = d_decay_ref[...] * decay * keep - through
+    d_rate = (d_log * vectors_ref[2:3] * rate * (1.0 - rate)).astype(bf16)
+    d_input = (d_drive * share * conv * in_gate * (1.0 - in_gate)).astype(bf16)
+    d_both = jnp.concatenate([d_rate, d_input], 1)
+    d_conv = (d_drive * share * in_gate + contract(d_both, both_ref[...], 1, 1)).astype(bf16)
+    d_conv_ref[...] = d_conv
+    grad_ref[...] = contract(conv_ref[...], d_both, 0, 0).astype(bf16)
+    sums_ref[0:1] = jnp.sum(d_rate.astype(f32), axis=0, keepdims=True)
+    sums_ref[1:2] = jnp.sum(d_input.astype(f32), axis=0, keepdims=True)
+    sums_ref[2:3] = jnp.sum(d_log * rate, axis=0, keepdims=True)
+    sums_ref[3:4] = jnp.sum(d_conv.astype(f32), axis=0, keepdims=True)
+
+
+def gate_call(kernel, conv, both, vectors, reset, grads, out_kinds):
+    rows, channels = conv.shape
+    per_row = pl.BlockSpec((rows, HW), lambda h: (0, h))
+    kinds = {
+        "rows": (per_row, (rows, channels)),
+        "weights": (pl.BlockSpec((HW, 2 * HW), lambda h: (h, 0)), (channels, 2 * HW)),
+        "sums": (pl.BlockSpec((4, HW), lambda h: (0, h)), (4, channels)),
+    }
+    return pl.pallas_call(
+        kernel,
+        grid=(channels // HW,),
+        out_shape=[jax.ShapeDtypeStruct(kinds[kind][1], dtype) for kind, dtype in out_kinds],
+        in_specs=[
+            per_row,
+            kinds["weights"][0],
+            pl.BlockSpec((vectors.shape[0], HW), lambda h: (0, h)),
+            pl.BlockSpec((rows, 1), lambda h: (0, 0)),
+        ]
+        + [per_row] * len(grads),
+        out_specs=[kinds[kind][0] for kind, _ in out_kinds],
+        compiler_params=pltpu.CompilerParams(vmem_limit_bytes=32 * 2**20),
+        cost_estimate=pl.CostEstimate(
+            flops=4 * rows * channels * HW * (1 + 2 * len(grads)),
+            bytes_accessed=24 * rows * channels,
+            transcendentals=6 * rows * channels,
+        ),
+    )(conv, both, vectors, reset, *grads)
+
+
 def pair_slots(count):
     half = count // 2
     return [k for s in range(1, half) for k in (count - s, s)] + [half, 0]
@@ -847,11 +889,13 @@
 
 
 def ff_kernel(
-    order, own_ref, cot_ref, gate_hbm, up_hbm, down_hbm,
-    blocks_ref, hidden_ref, d_gate_ref, d_up_ref, out_ref, d_in_ref,
-    gate_ref, up_ref, down_ref, rows_ref, cots_ref, h_ref, g_ref, u_ref, o_ref, d_ref,
-    send_sem, recv_sem, load_sem, store_sem,
+    order, own_ref, gate_hbm, up_hbm, down_hbm, *refs
 ):
+    cot_count = len(refs) - 21
+    cot_hbm, refs = refs[:cot_count], refs[cot_count:]
+    blocks_ref, cot_ref, hidden_ref, d_gate_ref, d_up_ref, out_ref, d_in_ref, *refs = refs
+    gate_ref, up_ref, down_ref, rows_ref, cots_ref, h_ref, g_ref, u_ref, o_ref, d_ref, *refs = refs
+    send_sem, recv_sem, load_sem, store_sem = refs
     count = len(order)
     half = count // 2
     rows, width = own_ref.shape
@@ -908,17 +952,34 @@
     for copy in weights:
         copy.wait()
 
-    def loads(s):
-        return [
-            pltpu.make_async_copy(blocks_ref.at[pl.ds(2 * (s - 1), 2)], rows_ref, load_sem.at[4]),
-            pltpu.make_async_copy(cot_ref.at[pl.ds(2 * (s - 1), 2)], cots_ref, load_sem.at[5]),
-        ]
+    rows_load = lambda s: pltpu.make_async_copy(
+        blocks_ref.at[pl.ds(2 * (s - 1), 2)], rows_ref, load_sem.at[4]
+    )
+
+    def cot_loads(s):
+        if s < half:
+            return [
+                pltpu.make_async_copy(cot_hbm[2 * s - 1 + i], cots_ref.at[i], load_sem.at[5 + i])
+                for i in range(2)
+            ]
+        copies = [pltpu.make_async_copy(cot_hbm[0], cots_ref.at[1], load_sem.at[5])]
+        first = 0
+        for i, part_hbm in enumerate(cot_hbm[2 * half - 1 :]):
+            part_rows = part_hbm.shape[0]
+            copies.append(
+                pltpu.make_async_copy(
+                    part_hbm, cots_ref.at[0, pl.ds(first, part_rows)], load_sem.at[6 + i]
+                )
+            )
+            first += part_rows
+        return copies
 
     def stores(s):
         return [
             pltpu.make_async_copy(vmem, hbm.at[s - 1], store_sem.at[i])
             for i, (vmem, hbm) in enumerate(
                 (
+                    (cots_ref, cot_ref),
                     (h_ref, hidden_ref),
                     (g_ref, d_gate_ref),
                     (u_ref, d_up_ref),
@@ -950,16 +1011,24 @@
             for side in range(2):
                 part(side).wait_recv()
 
-        for copy in loads(s):
-            copy.start()
+        rows_load(s).start()
 
         @pl.when(s > 1)
         def _():
             for copy in stores(s - 1):
                 copy.wait()
 
-        for copy in loads(s):
-            copy.wait()
+        for at_step in range(1, half + 1):
+
+            @pl.when(s == at_step)
+            def _():
+                copies = cot_loads(at_step)
+                for copy in copies:
+                    copy.start()
+                for copy in copies:
+                    copy.wait()
+
+        rows_load(s).wait()
         wide = 256 if hidden_here % 256 == 0 else 128
 
         def inner(j, carry):
@@ -1001,7 +1070,7 @@
         part(side).wait_send()
 
 
-def ff_call(order, own, cot, slab_gate, slab_up, slab_down):
+def ff_call(order, own, cots, slab_gate, slab_up, slab_down):
     rows, width = own.shape
     count, half = len(order), len(order) // 2
     hidden_here = slab_gate.shape[1]
@@ -1011,11 +1080,11 @@
     flops = 12 * count * rows * width * hidden_here
     return pl.pallas_call(
         functools.partial(ff_kernel, order),
-        out_shape=[shape((count, rows, width), bf16)]
+        out_shape=[shape((count, rows, width), bf16), shape((half, 2, rows, width), bf16)]
         + [shape((half, pair, hidden_here), bf16)] * 3
         + [shape((half, pair, width), bf16)] * 2,
-        in_specs=[anywhere] * 5,
-        out_specs=[anywhere] * 6,
+        in_specs=[anywhere] * (4 + len(cots)),
+        out_specs=[anywhere] * 7,
         scratch_shapes=[
             pltpu.VMEM((width, hidden_here), bf16),
             pltpu.VMEM((width, hidden_here), bf16),
@@ -1029,8 +1098,8 @@
             pltpu.VMEM((pair, width), bf16),
             pltpu.SemaphoreType.DMA((2, half)),
             pltpu.SemaphoreType.DMA((count,)),
+            pltpu.SemaphoreType.DMA((8,)),
             pltpu.SemaphoreType.DMA((6,)),
-            pltpu.SemaphoreType.DMA((5,)),
         ],
         compiler_params=pltpu.CompilerParams(
             collective_id=2, has_side_effects=True, vmem_limit_bytes=48 * 2**20
@@ -1038,7 +1107,7 @@
         cost_estimate=pl.CostEstimate(
             flops=flops, bytes_accessed=60 * 2**20, transcendentals=count * rows * hidden_here
         ),
-    )(own, cot, slab_gate, slab_up, slab_down)
+    )(own, slab_gate, slab_up, slab_down, *cots)
 
 
 def passed_along(value, axis, steps):
@@ -1068,17 +1137,6 @@
 
 def rows_of(values, first_row, row_count):
     return lax.slice_in_dim(values, first_row, first_row + row_count, axis=values.ndim - 2)
-
-
-def gate_math(rate_pre, input_pre, conv_vals, decay_param, reset_col):
-    rate = jax.nn.sigmoid(rate_pre)
-    in_gate = jax.nn.sigmoid(input_pre)
-    log_decay = -8.0 * jax.nn.softplus(-decay_param) * rate
-    keep_mask = 1.0 - reset_col
-    decay_rows = jnp.exp(log_decay) * keep_mask
-    root_term = jnp.sqrt(jnp.maximum(-jnp.expm1(2.0 * log_decay), floor_value))
-    drive_rows = (reset_col + keep_mask * root_term) * in_gate * conv_vals
-    return (decay_rows, drive_rows)
 
 
 def dot(left, right):
@@ -1122,41 +1180,39 @@
     devices = dp_count * seq_count
     chan_here, channels = w_rgate.shape[0], w_rgate.shape[0] * devices
     wide_here = norm1_gain.shape[0]
-    head_count = channels // HW
     taps = conv_w.shape[0]
     rim_rows = taps - 1
-    rel = net.rel()
 
     vectors = [norm1_gain, norm2_gain, conv_w.reshape(-1), conv_bias, rgate_bias, igate_bias, decay_param]
     lengths = [v.shape[0] for v in vectors]
     flat = jnp.concatenate(vectors)
     small_rows = -(-flat.shape[0] // HW)
-    small_rows += -(2 * chan_here + small_rows) % 16
     flat = jnp.pad(flat, (0, small_rows * HW - flat.shape[0]))
-    packed = jnp.concatenate([w_rgate, w_igate, flat.reshape(small_rows, HW)], 0)
     half_rows = chan_here * 3 // 5 // 16 * 16
-    out_pieces = [(3, 0, half_rows, RING_FIRST), (3, half_rows, chan_here - half_rows, CHIP_FIRST)]
+    out_pieces = [(2, 0, half_rows, RING_FIRST), (2, half_rows, chan_here - half_rows, CHIP_FIRST)]
     if half_rows == 0 or chan_here % 16:
-        out_pieces = [(3, 0, chan_here, RING_FIRST)]
-    pack_got, in_got, gate_got, out_got, start_got = gather_call(
+        out_pieces = [(2, 0, chan_here, RING_FIRST)]
+    small_pieces = [(3, 0, small_rows, RING_FIRST), (4, 0, chan_here, RING_FIRST)]
+    full_in, full_gate, full_out, flat_all, full_both, start_state = gather_call(
         net,
-        (packed, w_in, w_gate, w_out, initial_state),
-        [
-            (0, 0, packed.shape[0], RING_FIRST),
-            (1, 0, wide_here, RING_FIRST),
-            (2, 0, wide_here, CHIP_FIRST),
-        ]
+        (
+            w_in,
+            w_gate,
+            w_out,
+            flat.reshape(small_rows, HW),
+            jnp.concatenate([w_rgate, w_igate], 1),
+            initial_state,
+        ),
+        small_pieces
+        + [(0, 0, wide_here, RING_FIRST), (1, 0, wide_here, CHIP_FIRST)]
         + out_pieces
-        + [(4, 0, 1, RING_ONLY)],
-    )
-    pack_blocks = [pack_got[i] for i in range(dp_count)]
-    pack_all = jnp.zeros((dp_count,) + pack_blocks[0].shape, bf16)
-    for (c, k), block in zip(rel, pack_blocks):
-        pack_all = lax.dynamic_update_index_in_dim(pack_all, block, net.dp_at(c, k), 0)
-    pack_all = pack_all.reshape((devices,) + packed.shape)
-    full_rgate = pack_all[:, :chan_here].reshape(channels, HW)
-    full_igate = pack_all[:, chan_here : 2 * chan_here].reshape(channels, HW)
-    flat_all = pack_all[:, 2 * chan_here :].reshape(devices, small_rows * HW)
+        + [(5, 0, 1, RING_ONLY)],
+    )
+    full_in, full_gate = (v.reshape(width, channels) for v in (full_in, full_gate))
+    full_out = full_out.reshape(channels, width)
+    full_both = full_both.reshape(channels, 2 * HW)
+    start_state = start_state.reshape(1, channels)
+    flat_all = flat_all.reshape(devices, small_rows * HW)
     pieces, at = [], 0
     for length in lengths:
         pieces.append(flat_all[:, at : at + length])
@@ -1165,28 +1221,24 @@
     full_norm2 = pieces[1].reshape(-1).astype(f32)
     conv_wf = pieces[2].reshape(devices, taps, chan_here).transpose(1, 0, 2).reshape(taps, channels).astype(f32)
     full_cbias, full_rbias, full_ibias, decay_f = (p.reshape(-1).astype(f32) for p in pieces[3:])
-    start_state = start_got.reshape(1, channels)
-
-    in_blocks, gate_blocks = (
-        [got[i].reshape(seq_count * wide_here, channels) for i in range(dp_count)]
-        for got in (in_got, gate_got)
-    )
-    out_blocks = [out_got[i].reshape(seq_count * chan_here, width) for i in range(dp_count)]
-    w_ffgate, w_ffup, w_ffdown, cotangent, in_blocks[0] = lax.optimization_barrier(
-        (w_ffgate, w_ffup, w_ffdown, cotangent, in_blocks[0])
+    gate_vectors = jnp.stack([full_rbias, full_ibias, -8.0 * jax.nn.softplus(-decay_f)], 0)
+    w_ffgate, w_ffup, w_ffdown, cotangent, full_in = lax.optimization_barrier(
+        (w_ffgate, w_ffup, w_ffdown, cotangent, full_in)
+    )
+    slab_gate, slab_up, slab_down = (
+        lax.all_gather(w_ffgate, "dp", axis=0, tiled=True),
+        lax.all_gather(w_ffup, "dp", axis=0, tiled=True),
+        lax.all_gather(w_ffdown, "dp", axis=1, tiled=True),
     )
     cotan_rows = cotangent.reshape(rows_here, width)
-    cot_flow = Flow(net.seq.gather_steps(net.columns_out(cotan_rows)))
-    slab_flows = [Flow(net.gather_dp_steps(w)) for w in (w_ffgate, w_ffup, w_ffdown)]
+    cot_flow = Flow(net.seq.gather_steps(cotan_rows))
 
     token_rows = inputs.reshape(rows_here, width).astype(f32)
     normed_f, scale_one, unit_one = rms_parts(token_rows, full_norm1)
-    normed = net.columns_out(normed_f.astype(bf16))
-    step_cols = width // dp_count
-    normed_parts = [normed[:, i * step_cols : (i + 1) * step_cols] for i in range(dp_count)]
-    branch = total([dot(n, w) for n, w in zip(normed_parts, in_blocks)]).astype(bf16)
+    normed = normed_f.astype(bf16)
+    branch = dot(normed, full_in).astype(bf16)
     branch = beside(branch, cot_flow)
-    gate_pre = total([dot(n, w) for n, w in zip(normed_parts, gate_blocks)])
+    gate_pre = dot(normed, full_gate)
     reset_flags = reset.reshape(rows_here).astype(bf16)
     rim_branch, rim_flags = passed_along(
         (branch[len_here - rim_rows :], reset_flags[len_here - rim_rows :]), "seq", 1
@@ -1204,30 +1256,10 @@
             padded, rim_rows - offset, len_here
         )
     conv_low = conv_total.astype(bf16)
-    conv_f = conv_low.astype(f32)
-    head_view = conv_low.reshape(rows_here, head_count, HW)
-    rgate_blocks = full_rgate.reshape(head_count, HW, HW)
-    igate_blocks = full_igate.reshape(head_count, HW, HW)
-    rate_pre = (
-        jnp.einsum("nhi,hij->nhj", head_view, rgate_blocks, preferred_element_type=f32).reshape(
-            rows_here, channels
-        )
-        + full_rbias
-    )
-    input_pre = (
-        jnp.einsum("nhi,hij->nhj", head_view, igate_blocks, preferred_element_type=f32).reshape(
-            rows_here, channels
-        )
-        + full_ibias
-    )
     reset_col = reset.astype(f32).reshape(rows_here, 1)
-    rate_pre, input_pre, gate_pre = beside((rate_pre, input_pre, gate_pre), cot_flow, *slab_flows)
-
-    def gate_local(rate_in, input_in, conv_in, decay_in):
-        return gate_math(rate_in, input_in, conv_in, decay_in, reset_col)
-
-    (decay_rows, drive_rows), gate_grad_fn = jax.vjp(
-        gate_local, rate_pre, input_pre, conv_f, decay_f
+    conv_low, gate_pre = beside((conv_low, gate_pre), cot_flow)
+    decay_rows, drive_rows = gate_call(
+        gate_kernel, conv_low, full_both, gate_vectors, reset_col, (), [("rows", f32)] * 2
     )
     row_shape = jax.ShapeDtypeStruct((rows_here, channels), f32)
     states, prev_states, last_state = scan_call(
@@ -1237,27 +1269,23 @@
         (decay_rows, drive_rows, start_state),
         [row_shape, row_shape, jax.ShapeDtypeStruct((1, channels), f32)],
     )
-    states = beside(states, cot_flow, *slab_flows)
+    states = beside(states, cot_flow)
     final_here = initial_state.shape[1]
     final_state = lax.dynamic_slice_in_dim(
         last_state, lax.axis_index("seq") * final_here, final_here, 1
     )
     state_f = states.astype(bf16).astype(f32)
     gate_act, gate_back = jax.vjp(gelu_tanh, gate_pre)
-    mixed_rows = net.columns_out((state_f * gate_act).astype(bf16))
-    step_chan = channels // dp_count
-    mixed_parts = [mixed_rows[:, i * step_chan : (i + 1) * step_chan] for i in range(dp_count)]
-    residual = token_rows + total([dot(m, w) for m, w in zip(mixed_parts, out_blocks)])
+    mixed_rows = (state_f * gate_act).astype(bf16)
+    residual = token_rows + dot(mixed_rows, full_out)
 
     slots = pair_slots(seq_count)
     cot_blocks = cot_flow.finish()
-    group_cotan = jnp.stack([cot_blocks[k] for k in slots], 0)
-    slab_gate, slab_up = (jnp.concatenate(flow.finish(), 0) for flow in slab_flows[:2])
-    slab_down = jnp.concatenate(slab_flows[2].finish(), 1)
+    cots = [cotan_rows] + [cot_blocks[k] for k in slots[:-2]] + cot_blocks[seq_count // 2]
     normed_two_f, scale_two, unit_two = rms_parts(residual, full_norm2)
-    normed_two = net.columns_out(normed_two_f.astype(bf16))
-    group_normed, hidden, d_ffgate, d_ffup, out_part, d_normed_part = ff_call(
-        net.order, normed_two, group_cotan, slab_gate, slab_up, slab_down
+    normed_two = normed_two_f.astype(bf16)
+    group_normed, group_cotan, hidden, d_ffgate, d_ffup, out_part, d_normed_part = ff_call(
+        net.order, normed_two, cots, slab_gate, slab_up, slab_down
     )
     group_rows = seq_count * rows_here
     group_normed = group_normed.reshape(group_rows, width)
@@ -1267,12 +1295,6 @@
     def block_rows(whole):
         whole = whole.reshape(seq_count, rows_here, width)
         return lambda k: whole[slots.index(k)]
-
-    def dp_chunk(whole, axis):
-        size = whole.shape[axis] // dp_count
-        return lambda c, k: lax.slice_in_dim(
-            whole, (c * net.chips + k) * size, (c * net.chips + k + 1) * size, axis=axis
-        )
 
     d_normed_flow = Flow(net.seq.scatter_steps(block_rows(d_normed_part)))
     gate_part = beside(t_dot(group_normed, d_ffgate).astype(bf16), d_normed_flow)
@@ -1282,20 +1304,25 @@
     d_normed_sum, out_part, gate_part, up_part, down_part = lax.optimization_barrier(
         (d_normed_sum, out_part, gate_part, up_part, down_part)
     )
-    d_normed_two = net.columns_back(d_normed_sum)
+    d_normed_two = d_normed_sum
     out_flow = Flow(net.seq.scatter_steps(block_rows(out_part)))
-    ff_flows = [
-        Flow(net.scatter_dp_steps(dp_chunk(part, axis)))
+    grad_ffgate, grad_ffup, grad_ffdown = (
+        lax.psum_scatter(part, "dp", scatter_dimension=axis, tiled=True).astype(f32)
         for part, axis in ((gate_part, 0), (up_part, 0), (down_part, 1))
-    ]
+    )
 
     grad_norm2, d_resid_norm = norm_back(d_normed_two, full_norm2, scale_two, unit_two)
     d_residual = cotan_rows.astype(f32) + d_resid_norm
     d_residual_low = d_residual.astype(bf16)
-    d_mixed = net.columns_back(jnp.concatenate([dot_t(d_residual_low, w) for w in out_blocks], 1))
-    d_mixed = beside(d_mixed, out_flow, *ff_flows)
+    d_mixed = dot_t(d_residual_low, full_out)
     d_state = (d_mixed * gate_act).astype(bf16)
     d_gate_pre = gate_back(d_mixed * state_f)[0].astype(bf16)
+    d_state, d_gate_pre = beside((d_state, d_gate_pre), out_flow)
+
+    def grad_terms(left, right):
+        return t_dot(left, right).astype(bf16).reshape(dp_count, seq_count, -1, right.shape[1])
+
+    gate_terms = grad_terms(normed, d_gate_pre)
     d_drive, d_decay = scan_call(
         scan_back_kernel,
         1,
@@ -1303,32 +1330,20 @@
         (decay_rows, d_state.astype(f32), prev_states),
         [row_shape, row_shape],
     )
-
-    def grad_terms(parts, right):
-        return [t_dot(part, right).astype(bf16).reshape(seq_count, -1, right.shape[1]) for part in parts]
-
-    out_terms = grad_terms(mixed_parts, d_residual_low)
-    gate_terms = grad_terms(normed_parts, d_gate_pre)
-    d_rate_pre, d_input_pre, d_conv_direct, grad_decay = gate_grad_fn((d_decay, d_drive))
-    d_rate_low, d_input_low = beside(
-        (d_rate_pre.astype(bf16), d_input_pre.astype(bf16)), out_flow, *ff_flows
-    )
-    d_rate_heads = d_rate_low.reshape(rows_here, head_count, HW)
-    d_input_heads = d_input_low.reshape(rows_here, head_count, HW)
-    grad_rgate = jnp.einsum("nhi,nhj->hij", head_view, d_rate_heads, preferred_element_type=f32)
-    grad_igate = jnp.einsum("nhi,nhj->hij", head_view, d_input_heads, preferred_element_type=f32)
-    grad_rbias = jnp.sum(d_rate_low.astype(f32), axis=0)
-    grad_ibias = jnp.sum(d_input_low.astype(f32), axis=0)
-    d_conv = (
-        d_conv_direct
-        + jnp.einsum("nhj,hij->nhi", d_rate_heads, rgate_blocks, preferred_element_type=f32).reshape(
-            rows_here, channels
-        )
-        + jnp.einsum("nhj,hij->nhi", d_input_heads, igate_blocks, preferred_element_type=f32).reshape(
-            rows_here, channels
-        )
-    )
-    d_conv_low = d_conv.astype(bf16)
+    d_drive, d_decay, gate_terms = beside((d_drive, d_decay, gate_terms), out_flow)
+    out_terms = grad_terms(mixed_rows, d_residual_low)
+    d_conv_low, both_terms, gate_sums = gate_call(
+        gate_back_kernel,
+        conv_low,
+        full_both,
+        gate_vectors,
+        reset_col,
+        (d_decay, d_drive),
+        [("rows", bf16), ("weights", bf16), ("sums", f32)],
+    )
+    d_conv_low, out_terms = beside((d_conv_low, out_terms), out_flow)
+    grad_rbias, grad_ibias, rate_sum, grad_cbias = gate_sums
+    grad_decay = 8.0 * jax.nn.sigmoid(-decay_f) * rate_sum
     rim_grad, rim_next = passed_along((d_conv_low[:rim_rows], reset_flags[:rim_rows]), "seq", -1)
     grad_ext = jnp.concatenate([d_conv_low, rim_grad], 0).astype(f32)
     open_next = (1.0 - jnp.concatenate([reset_flags, rim_next], 0).astype(f32))[:, None]
@@ -1347,25 +1362,15 @@
             )
         )
     grad_conv = jnp.stack(conv_grads, 0)
-    grad_cbias = jnp.sum(d_conv_f, axis=0)
-    d_branch_low = beside(d_branch.astype(bf16), out_flow)
-    in_terms = grad_terms(normed_parts, d_branch_low)
-    d_normed_one = net.columns_back(
-        jnp.concatenate(
-            [
-                dot_t(d_branch_low, left) + dot_t(d_gate_pre, right)
-                for left, right in zip(in_blocks, gate_blocks)
-            ],
-            1,
-        )
-    )
+    d_branch_low = d_branch.astype(bf16)
+    in_terms = grad_terms(normed, d_branch_low)
+    d_normed_one = dot_t(d_branch_low, full_in) + dot_t(d_gate_pre, full_gate)
     grad_norm1, d_token_norm = norm_back(d_normed_one, full_norm1, scale_one, unit_one)
     input_grad = (d_residual + d_token_norm).reshape(seqs_here, len_here, width)
 
     grad_norm1, input_grad = beside((grad_norm1, input_grad), out_flow)
-    ff_out = net.columns_back(out_flow.finish())
+    ff_out = out_flow.finish()
     output = (residual + ff_out).astype(bf16).reshape(seqs_here, len_here, width)
-    grad_ffgate, grad_ffup, grad_ffdown = (flow.finish() for flow in ff_flows)
 
     conv_flat = grad_conv.reshape(taps, devices, chan_here).transpose(1, 0, 2)
     flat_grads = jnp.concatenate(
@@ -1376,26 +1381,22 @@
         1,
     )
     flat_grads = jnp.pad(flat_grads, ((0, 0), (0, small_rows * HW - flat_grads.shape[1])))
-    pack_grads = jnp.concatenate(
+    flat_terms = flat_grads.astype(bf16).reshape(dp_count, seq_count, small_rows, HW)
+    turned = [(i, first, rows, RING_FIRST + CHIP_FIRST - way) for i, first, rows, way in out_pieces]
+    grad_in, grad_gate, grad_out, flat_mine, both_mine = reduce_call(
+        net,
         [
-            grad_rgate.astype(bf16).reshape(devices, chan_here, HW),
-            grad_igate.astype(bf16).reshape(devices, chan_here, HW),
-            flat_grads.astype(bf16).reshape(devices, small_rows, HW),
+            in_terms,
+            gate_terms,
+            out_terms,
+            flat_terms,
+            both_terms.reshape(dp_count, seq_count, chan_here, 2 * HW),
         ],
-        1,
-    ).reshape(dp_count, seq_count, 2 * chan_here + small_rows, HW)
-    pack_terms = [
-        lax.dynamic_index_in_dim(pack_grads, net.dp_at(c, k), 0, keepdims=False) for c, k in rel
-    ]
-    out_pieces = [(2, first, rows, RING_FIRST + CHIP_FIRST - way) for _, first, rows, way in out_pieces]
-    grad_in, grad_gate, grad_out, pack_mine = reduce_call(
-        net,
-        [in_terms, gate_terms, out_terms, pack_terms],
         [(1, 0, wide_here, RING_FIRST)]
-        + out_pieces
-        + [(3, 0, packed.shape[0], CHIP_FIRST), (0, 0, wide_here, CHIP_FIRST)],
-    )
-    flat_mine = pack_mine[2 * chan_here :].reshape(-1)
+        + turned
+        + [(3, 0, small_rows, CHIP_FIRST), (4, 0, chan_here, CHIP_FIRST), (0, 0, wide_here, CHIP_FIRST)],
+    )
+    flat_mine = flat_mine.reshape(-1)
     mine, at = [], 0
     for length in lengths:
         mine.append(flat_mine[at : at + length])
@@ -1409,9 +1410,9 @@
         grad_in,
         mine[2].reshape(taps, chan_here),
         mine[3],
-        pack_mine[:chan_here],
+        both_mine[:, :HW],
         mine[4],
-        pack_mine[chan_here : 2 * chan_here],
+        both_mine[:, HW:],
         mine[5],
         mine[6],
         grad_out,

time: 895 us -> 730 us (0.82)
  local copies, waits for them, and re-layouts: 99.1 us -> 39.9 us
  other arithmetic: 99.9 us -> 54.8 us
  waiting for transfers between devices: 98.9 us -> 57.6 us
  starting transfers between devices: 52.5 us -> 38.2 us
  between operations: 2.74 us -> 15.6 us
  matrix products: 108 us -> 97.2 us
    ppermute x42 -> x24, waiting for transfers between devices: 85.1 us -> 54.6 us  [shift(): return lax.ppermute(value, self.axis, pairs)]
    unnamed x236 -> x142, local copies, waits for them, and re-layouts: 42 us -> 20.8 us
    slice x8 -> x1, local copies, waits for them, and re-layouts: 20.5 us -> 1.59 us  [per_device(): both_mine[:, HW:]]
    pallas_call x2, Pallas kernels: 51.1 us -> 34.2 us  [scan_call(): pl.pallas_call(functools.partial(kernel, count), out_shape=out_shapes, in...]
    ppermute x42 -> x24, starting transfers between devices: 42 us -> 27.5 us  [shift(): return lax.ppermute(value, self.axis, pairs)]
    dot_general x12 -> x3, matrix products: 14.2 us -> 28.4 us  [dot_t(): lax.dot_general(left, right, (((1,), (1,)), ((), ())), preferred_element_...]
    pallas_call x0 -> x2, Pallas kernels: none -> 14.1 us  [gate_call(): pl.pallas_call(kernel, grid=(channels // HW,), out_shape=[jax.ShapeDtypeS...]
    dot_general x15 -> x6, matrix products: 61.3 us -> 48.5 us  [t_dot(): lax.dot_general(left, right, (((0,), (0,)), ((), ())), preferred_element_...]
  transfers between devices with their start and end apart: 46 -> 34, of which waited for: 12 -> 10; matrix products, arithmetic and copies ran while one was open for 19% -> 20% of each run, Pallas kernels for 6% -> 24%
where the time goes in v4:
time: 730 us; the launch traced here: 721 us
  Pallas kernels  418 us (57%)
  matrix products  97.2 us (13%)
  waiting for transfers between devices  57.6 us (8%)
  other arithmetic  54.8 us (8%)
  local copies, waits for them, and re-layouts  39.9 us (5%)
  starting transfers between devices  38.2 us (5%)
  between operations  15.6 us (2%)
    pallas_call x1, Pallas kernels, gather_call(): pl.pallas_call(functools.partial(gather_kernel, net.order, chips, cores,...  142 us
    pallas_call x1, Pallas kernels, reduce_call(): pl.pallas_call(functools.partial(reduce_kernel, net.order, chips, cores,...  127 us
    pallas_call x1, Pallas kernels, ff_call(): pl.pallas_call(functools.partial(ff_kernel, order), out_shape=[shape((cou...  101 us
    ppermute x24, waiting for transfers between devices, shift(): return lax.ppermute(value, self.axis, pairs)  54.6 us
    dot_general x6, matrix products, t_dot(): lax.dot_general(left, right, (((0,), (0,)), ((), ())), preferred_element_...  48.5 us
    pallas_call x2, Pallas kernels, scan_call(): pl.pallas_call(functools.partial(kernel, count), out_shape=out_shapes, in...  34.2 us
    dot_general x3, matrix products, dot_t(): lax.dot_general(left, right, (((1,), (1,)), ((), ())), preferred_element_...  28.4 us
    ppermute x24, starting transfers between devices, shift(): return lax.ppermute(value, self.axis, pairs)  27.5 us
  transfers between devices with their start and end apart: 34, of which 10 were waited for; matrix products, arithmetic and copies ran while one was open for 20% of the time, Pallas kernels for 24%

profile of v4, /device:TPU:0, one launch (start us, length us, event | category | flops | bytes accessed | tf_op | source)
XLA Modules:
  0.0 720.9 jit_solution(13803118281934637025)
XLA Ops:
  16.6 141.5 %shard_map.322 = (bf16[4,8,64,2560]{3,2,1,0:T(8,128)(2,1)S(1)}, bf16[4,8,64,2560]{3,2,1,0:T(8,128)(2,1)}, bf16[4,8,80,2048]{3,2,1,0:T(8,128)(2,1)}, bf16[4,8,3,2...) custom-call(bf16[64,2560]{1,0:T(8,128)(2,1)S(1)} %copy-done.11, ...), custom_call_target="tpu_custom_call" | custom-call | bytes 68296704 | tf_op jit(solution)/shard_map/pallas_call | solution.py:365
  167.9 4.5 collective-permute-start.3
  173.5 8.0 %convolution_convert_fusion.3 = bf16[256,2560]{1,0:T(8,128)(2,1)} fusion(bf16[2048,2560]{1,0:T(8,128)(2,1)} %bitcast.179, bf16[1,256,2048]{2,1,0:T(8,128)(2,1)S(1)} %copy-done.27, f32[2048]{0:T(1024)S(1)} %reshape.382, f32[256]{0:T(256)S(1)} %add_rsqrt_fusion.1), kind=kOutput, calls=%fused_computation.3 | convolution fusion | flops 2687107072 | bytes 12854272 | tf_op jit(solution)/shard_map/dot_general | solution.py:1143
  182.5 6.1 fusion.43
  199.6 20.2 %collective-permute-done.4.refs_3_ = bf16[256,2048]{1,0:T(8,128)(2,1)S(1)} collective-permute-done((bf16[256,2048]{1,0:T(8,128)(2,1)}, bf16[256,2048]{1,0:T(8,128)(2,1)S(1)}, u32[]{:S(2)}, u32[]{:S(2)}) %collective-permute-start.4) | collective-permute-done | bytes 1048608 | tf_op jit(solution)/shard_map/ppermute | solution.py:43
  223.4 4.9 shard_map.323
  228.3 22.6 %shard_map.324 = (f32[256,2560]{1,0:T(8,128)S(1)}, f32[256,2560]{1,0:T(8,128)S(1)}, f32[1,2560]{1,0:T(1,128)S(1)}) custom-call(f32[256,2560]{1,0:T(8,128)S(1)} %get-tuple-element.102.decay_ref, f32[256,2560]{1,0:T(8,128)S(1)} %get-tuple-element.103.drive_ref, f32[1,2560]{1,0:T(1,128)S(1)} %reshape.360.start_ref), custom_call_target="tpu_custom_call" | custom-call | flops 5242880 | bytes 13107200 | tf_op jit(solution)/shard_map/pallas_call | solution.py:774
  254.3 6.2 multiply_reduce_fusion.6
  267.8 100.7 %shard_map.325 = (bf16[8,256,2048]{2,1,0:T(8,128)(2,1)}, bf16[4,2,256,2048]{3,2,1,0:T(8,128)(2,1)}, bf16[4,512,768]{2,1,0:T(8,128)(2,1)}, bf16[4,512,768]{2,1,0:...) custom-call(bf16[256,2048]{1,0:T(8,128)(2,1)S(1)} %copy-done.10, ...), custom_call_target="tpu_custom_call" | custom-call | flops 38654705664 | bytes 62914560 | tf_op jit(solution)/shard_map/pallas_call | solution.py:1081
  373.4 10.6 %convolution_convert_fusion.5 = bf16[2048,768]{1,0:T(8,128)(2,1)} fusion(bf16[2048,2048]{1,0:T(8,128)(2,1)} %bitcast.207, bf16[2048,768]{1,0:T(8,128)(2,1)S(1)} %bitcast.211), kind=kOutput, calls=%fused_computation.7 | convolution fusion | flops 6444023808 | bytes 14680064 | tf_op jit(solution)/shard_map/dot_general | solution.py:1151
  390.5 10.6 %convolution_convert_fusion.6 = bf16[2048,768]{1,0:T(8,128)(2,1)} fusion(bf16[2048,2048]{1,0:T(8,128)(2,1)} %bitcast.208, bf16[2048,768]{1,0:T(8,128)(2,1)S(1)} %bitcast.210), kind=kOutput, calls=%fused_computation.8 | convolution fusion | flops 6444023808 | bytes 14680064 | tf_op jit(solution)/shard_map/dot_general | solution.py:1151
  413.4 10.4 %convolution_convert_fusion.4 = bf16[768,2048]{1,0:T(8,128)(2,1)} fusion(bf16[2048,768]{1,0:T(8,128)(2,1)S(1)} %bitcast.209, bf16[2048,2048]{1,0:T(8,128)(2,1)} %bitcast.206), kind=kOutput, calls=%fused_computation.6 | convolution fusion | flops 6444023808 | bytes 14680064 | tf_op jit(solution)/shard_map/dot_general | solution.py:1151
  423.8 6.5 collective-permute-done.15
  437.1 13.0 %collective-permute-done.16 = bf16[256,2048]{1,0:T(8,128)(2,1)S(1)} collective-permute-done((bf16[256,2048]{1,0:T(8,128)(2,1)S(1)}, bf16[256,2048]{1,0:T(8,128)(2,1)S(1)}, u32[]{:S(2)}, u32[]{:S(2)}) %collective-permute-start.16) | collective-permute-done | bytes 1048608 | tf_op jit(solution)/shard_map/ppermute | solution.py:43
  450.1 4.5 collective-permute-done.17
  467.6 11.6 %fusion.14 = (bf16[256,2560]{1,0:T(8,128)(2,1)}, bf16[256,2560]{1,0:T(8,128)(2,1)}) fusion(f32[256,2560]{1,0:T(8,128)} %copy-done.36, f32[256,2560]{1,0:T(8,128)S(1)} %copy-done.2, bf16[2560,2048]{1,0:T(8,128)(2,1)} %bitcast.205, f32[256,2048]{1,0:T(8,128)S(1)} %multiply_add_fusion), kind=kOutput, calls=%fused_computation.27 | convolution fusion | flops 2701918208 | bytes 20447232 | tf_op jit(solution)/shard_map/dot_general | solution.py:1147
  485.2 5.6 convolution_convert_fusion.1
  493.7 11.6 %shard_map.326 = (f32[256,2560]{1,0:T(8,128)S(1)}, f32[256,2560]{1,0:T(8,128)S(1)}) custom-call(f32[256,2560]{1,0:T(8,128)S(1)} %get-tuple-element.102.decay_ref, f32[256,2560]{1,0:T(8,128)S(1)} %convert_element_type.393.d_state_ref, f32[256,2560]{1,0:T(8,128)S(1)} %copy-done.4), custom_call_target="tpu_custom_call" | custom-call | flops 5242880 | bytes 13107200 | tf_op jit(solution)/shard_map/pallas_call | solution.py:774
  505.3 5.7 convolution_convert_fusion.2
  517.4 8.5 %fusion.66 = f32[256,2048]{1,0:T(8,128)} fusion(bf16[256,2560]{1,0:T(8,128)(2,1)S(1)} %copy-done.40, bf16[2048,2560]{1,0:T(8,128)(2,1)} %bitcast.203), kind=kOutput, calls=%fused_computation.167 | convolution fusion | flops 2684354560 | bytes 13893632 | tf_op jit(solution)/shard_map/dot_general | solution.py:1147
  525.9 9.2 %shard_map.327 = (bf16[256,2560]{1,0:T(8,128)(2,1)S(1)}, bf16[2560,512]{1,0:T(8,128)(2,1)S(1)}, f32[4,2560]{1,0:T(4,128)S(1)}) custom-call(bf16[256,2560]{1,0:T(8,128)(2,1)S(1)} %copy-done.6, bf16[2560,512]{1,0:T(8,128)(2,1)S(1)} %bitcast.182, f32[3,2560]{1,0:T(4,128)S(1)} %pad_maximum_fusion.5.vectors_ref, f32[256,1]{1,0:T(8,128)S(1)} %copy.39.reset_ref, ...), custom_call_target="tpu_custom_call" | custom-call | flops 3355443200 | bytes 15728640 | tf_op jit(solution)/shard_map/pallas_call | solution.py:849
  551.6 8.3 %fusion.21 = (f32[256]{0:T(256)S(1)}, bf16[2048]{0:T(1024)(128)(2,1)S(1)}, f32[256,2048]{1,0:T(8,128)S(1)}) fusion(bf16[1,256,2048]{2,1,0:T(8,128)(2,1)S(1)} %copy-done.30, f32[2048]{0:T(1024)S(1)} %reshape.382, f32[256]{0:T(256)S(1)} %add_rsqrt_fusion.1, f32[256,2048]{1,0:T(8,128)} %fusion.66, bf16[256,2560]{1,0:T(8,128)(2,1)S(1)} %get-tuple-element.207, ...), kind=kOutput, calls=%fused_computation.44 | convolution fusion | flops 2688546560 | bytes 17053696 | tf_op jit(solution)/shard_map/dot_general | solution.py:1147
  562.1 5.7 convolution_convert_fusion
  568.7 127.0 %shard_map.328 = (f32[64,2560]{1,0:T(8,128)}, f32[64,2560]{1,0:T(8,128)}, f32[80,2048]{1,0:T(8,128)}, f32[3,256]{1,0:T(4,128)}, f32[80,512]{1,0:T(8,128)}) custom-call(bf16[4,8,64,2560]{3,2,1,0:T(8,128)(2,1)} %bitcast.185, bf16[4,8,64,2560]{3,2,1,0:T(8,128)(2,1)} %bitcast.184, bf16[4,8,80,2048]{3,2,1,0:T(8,128)(2,1)} %bitcast.183, ...), custom_call_target="tpu_custom_call" | custom-call | bytes 68255744 | tf_op jit(solution)/shard_map/pallas_call | solution.py:593
  (304 shorter events, 141.8 us)
Async XLA Ops:
  7.2 255.8 %all-gather.4.cloned.1.call-start = ((), (), s32[]{:S(2)}) async-start(), calls=%async_computation.3 | async-start | bytes 3932160 | tf_op jit(solution)/shard_map/all_gather | solution.py:1229
  163.7 99.4 %all-gather.6.cloned.1.call-start = ((), (), s32[]{:S(2)}) async-start(), calls=%async_computation.4 | async-start | bytes 3932160 | tf_op jit(solution)/shard_map/all_gather | solution.py:1230
  164.4 98.6 %all-gather.8.cloned.1.call-start = ((), (), s32[]{:S(2)}) async-start(), calls=%async_computation.5 | async-start | bytes 3932160 | tf_op jit(solution)/shard_map/all_gather | solution.py:1231
  164.5 26.0 %collective-permute-start.1 = (bf16[256,2048]{1,0:T(8,128)(2,1)S(1)}, bf16[256,2048]{1,0:T(8,128)(2,1)S(1)}, u32[]{:S(2)}, u32[]{:S(2)}) collective-permute-start(bf16[256,2048]{1,0:T(8,128)(2,1)S(1)} %bitcast.176), channel_id=1, source_target_pairs={{1,0},{3,1},{5,3},{7,5},{6,7},{4,6},{2,4},{0,2},{9,8},{11,9},{13,1... | collective-permute-start | bytes 3145736 | tf_op jit(solution)/shard_map/ppermute | solution.py:43
  166.0 25.8 %collective-permute-start = (bf16[256,2048]{1,0:T(8,128)(2,1)S(1)}, bf16[256,2048]{1,0:T(8,128)(2,1)}, u32[]{:S(2)}, u32[]{:S(2)}) collective-permute-start(bf16[256,2048]{1,0:T(8,128)(2,1)S(1)} %bitcast.177), channel_id=1, source_target_pairs={{1,3},{3,5},{5,7},{7,6},{6,4},{4,2},{2,0},{0,1},{9,11},{11,13},{13... | collective-permute-start | bytes 3145736 | tf_op jit(solution)/shard_map/ppermute | solution.py:43
  166.6 23.7 %collective-permute-start.25 = (bf16[3]{0:T(256)(128)(2,1)S(1)}, bf16[3]{0:T(256)(128)(2,1)S(1)}, u32[]{:S(2)}, u32[]{:S(2)}) collective-permute-start(bf16[3]{0:T(256)(128)(2,1)S(1)} %get-tuple-element.223), channel_id=1, source_target_pairs={{1,0},{2,1},{3,2},{4,3},{5,4},{6,5},{7,6},{9,8},{10,9},{11,10},{12... | collective-permute-start | bytes 26 | tf_op jit(solution)/shard_map/ppermute | solution.py:1116
  167.9 22.5 %collective-permute-start.3 = (bf16[3]{0:T(256)(128)(2,1)S(1)}, bf16[3]{0:T(256)(128)(2,1)S(1)}, u32[]{:S(2)}, u32[]{:S(2)}) collective-permute-start(bf16[3]{0:T(256)(128)(2,1)S(1)} %get-tuple-element.224), channel_id=1, source_target_pairs={{0,1},{1,2},{2,3},{3,4},{4,5},{5,6},{6,7},{8,9},{9,10},{10,11},{11... | collective-permute-start | bytes 26 | tf_op jit(solution)/shard_map/ppermute | solution.py:1116
  172.5 531.1 %reduce-scatter.8.cloned.1.call-start = ((), (), s32[]{:S(2)}) async-start(), calls=%async_computation.8 | async-start | bytes 3932160 | tf_op jit(solution)/shard_map/reduce_scatter | solution.py:1310
  195.3 24.5 %collective-permute-start.4 = (bf16[256,2048]{1,0:T(8,128)(2,1)}, bf16[256,2048]{1,0:T(8,128)(2,1)S(1)}, u32[]{:S(2)}, u32[]{:S(2)}) collective-permute-start(bf16[256,2048]{1,0:T(8,128)(2,1)} %collective-permute-done.refs_1_), channel_id=1, source_target_pairs={{1,3},{3,5},{5,7},{7,6},{6,4},{4,2},{2,0},{0,1},{9,11},{11,13},{13... | collective-permute-start | bytes 3145736 | tf_op jit(solution)/shard_map/ppermute | solution.py:43
  197.1 24.1 %collective-permute-start.5 = (bf16[256,2048]{1,0:T(8,128)(2,1)S(1)}, bf16[256,2048]{1,0:T(8,128)(2,1)S(1)}, u32[]{:S(2)}, u32[]{:S(2)}) collective-permute-start(bf16[256,2048]{1,0:T(8,128)(2,1)S(1)} %collective-permute-done.1.refs_2_), channel_id=1, source_target_pairs={{1,0},{3,1},{5,3},{7,5},{6,7},{4,6},{2,4},{0,2},{9,8},{11,9},{13,1... | collective-permute-start | bytes 3145736 | tf_op jit(solution)/shard_map/ppermute | solution.py:43
  221.2 29.6 %collective-permute-start.6 = (bf16[256,2048]{1,0:T(8,128)(2,1)S(1)}, bf16[256,2048]{1,0:T(8,128)(2,1)S(1)}, u32[]{:S(2)}, u32[]{:S(2)}) collective-permute-start(bf16[256,2048]{1,0:T(8,128)(2,1)S(1)} %collective-permute-done.4.refs_3_), channel_id=1, source_target_pairs={{1,3},{3,5},{5,7},{7,6},{6,4},{4,2},{2,0},{0,1},{9,11},{11,13},{13... | collective-permute-start | bytes 3145736 | tf_op jit(solution)/shard_map/ppermute | solution.py:43
  222.4 28.5 %collective-permute-start.7 = (bf16[256,2048]{1,0:T(8,128)(2,1)S(1)}, bf16[256,2048]{1,0:T(8,128)(2,1)S(1)}, u32[]{:S(2)}, u32[]{:S(2)}) collective-permute-start(bf16[256,2048]{1,0:T(8,128)(2,1)S(1)} %collective-permute-done.5.refs_4_), channel_id=1, source_target_pairs={{1,0},{3,1},{5,3},{7,5},{6,7},{4,6},{2,4},{0,2},{9,8},{11,9},{13,1... | collective-permute-start | bytes 3145736 | tf_op jit(solution)/shard_map/ppermute | solution.py:43
  389.1 18.0 %collective-permute-start.13 = (bf16[256,2048]{1,0:T(8,128)(2,1)}, bf16[256,2048]{1,0:T(8,128)(2,1)}, u32[]{:S(2)}, u32[]{:S(2)}) collective-permute-start(bf16[256,2048]{1,0:T(8,128)(2,1)} %pad_maximum_fusion.1), channel_id=1, source_target_pairs={{1,0},{3,1},{5,3},{7,5},{6,7},{4,6},{2,4},{0,2},{9,8},{11,9},{13,1... | collective-permute-start | bytes 3145736 | tf_op jit(solution)/shard_map/ppermute | solution.py:43
  411.4 18.9 %collective-permute-start.15 = (bf16[256,2048]{1,0:T(8,128)(2,1)}, bf16[256,2048]{1,0:T(8,128)(2,1)}, u32[]{:S(2)}, u32[]{:S(2)}) collective-permute-start(bf16[256,2048]{1,0:T(8,128)(2,1)} %get-tuple-element.197), channel_id=1, source_target_pairs={{1,0},{3,1},{5,3},{7,5},{6,7},{4,6},{2,4},{0,2},{9,8},{11,9},{13,1... | collective-permute-start | bytes 3145736 | tf_op jit(solution)/shard_map/ppermute | solution.py:43
  412.0 19.9 %collective-permute-start.14 = (bf16[256,2048]{1,0:T(8,128)(2,1)}, bf16[256,2048]{1,0:T(8,128)(2,1)}, u32[]{:S(2)}, u32[]{:S(2)}) collective-permute-start(bf16[256,2048]{1,0:T(8,128)(2,1)} %get-tuple-element.198), channel_id=1, source_target_pairs={{1,3},{3,5},{5,7},{7,6},{6,4},{4,2},{2,0},{0,1},{9,11},{11,13},{13... | collective-permute-start | bytes 3145736 | tf_op jit(solution)/shard_map/ppermute | solution.py:43
  436.3 18.2 %collective-permute-start.17 = (bf16[256,2048]{1,0:T(8,128)(2,1)S(1)}, bf16[256,2048]{1,0:T(8,128)(2,1)S(1)}, u32[]{:S(2)}, u32[]{:S(2)}) collective-permute-start(bf16[256,2048]{1,0:T(8,128)(2,1)S(1)} %get-tuple-element.196), channel_id=1, source_target_pairs={{1,0},{3,1},{5,3},{7,5},{6,7},{4,6},{2,4},{0,2},{9,8},{11,9},{13,1... | collective-permute-start | bytes 3145736 | tf_op jit(solution)/shard_map/ppermute | solution.py:43
  457.7 248.5 %reduce-scatter.6.cloned.1.call-start = ((), (), s32[]{:S(2)}) async-start(), calls=%async_computation.7 | async-start | bytes 3932160 | tf_op jit(solution)/shard_map/reduce_scatter | solution.py:1310
  458.3 250.4 %reduce-scatter.4.cloned.1.call-start = ((), (), s32[]{:S(2)}) async-start(), calls=%async_computation.6 | async-start | bytes 3932160 | tf_op jit(solution)/shard_map/reduce_scatter | solution.py:1310
  482.2 28.8 %collective-permute-start.20 = (bf16[256,2048]{1,0:T(8,128)(2,1)}, bf16[256,2048]{1,0:T(8,128)(2,1)}, u32[]{:S(2)}, u32[]{:S(2)}) collective-permute-start(bf16[256,2048]{1,0:T(8,128)(2,1)} %pad_maximum_fusion.2), channel_id=1, source_target_pairs={{1,3},{3,5},{5,7},{7,6},{6,4},{4,2},{2,0},{0,1},{9,11},{11,13},{13... | collective-permute-start | bytes 3145736 | tf_op jit(solution)/shard_map/ppermute | solution.py:43
  485.2 25.8 %collective-permute-start.21 = (bf16[256,2048]{1,0:T(8,128)(2,1)}, bf16[256,2048]{1,0:T(8,128)(2,1)}, u32[]{:S(2)}, u32[]{:S(2)}) collective-permute-start(bf16[256,2048]{1,0:T(8,128)(2,1)} %pad_maximum_fusion.3), channel_id=1, source_target_pairs={{1,0},{3,1},{5,3},{7,5},{6,7},{4,6},{2,4},{0,2},{9,8},{11,9},{13,1... | collective-permute-start | bytes 3145736 | tf_op jit(solution)/shard_map/ppermute | solution.py:43
  515.4 22.6 %collective-permute-start.23 = (bf16[256,2048]{1,0:T(8,128)(2,1)}, bf16[256,2048]{1,0:T(8,128)(2,1)S(1)}, u32[]{:S(2)}, u32[]{:S(2)}) collective-permute-start(bf16[256,2048]{1,0:T(8,128)(2,1)} %get-tuple-element.187), channel_id=1, source_target_pairs={{1,0},{3,1},{5,3},{7,5},{6,7},{4,6},{2,4},{0,2},{9,8},{11,9},{13,1... | collective-permute-start | bytes 3145736 | tf_op jit(solution)/shard_map/ppermute | solution.py:43
  516.8 21.1 %collective-permute-start.22 = (bf16[256,2048]{1,0:T(8,128)(2,1)}, bf16[256,2048]{1,0:T(8,128)(2,1)}, u32[]{:S(2)}, u32[]{:S(2)}) collective-permute-start(bf16[256,2048]{1,0:T(8,128)(2,1)} %get-tuple-element.188), channel_id=1, source_target_pairs={{1,3},{3,5},{5,7},{7,6},{6,4},{4,2},{2,0},{0,1},{9,11},{11,13},{13... | collective-permute-start | bytes 3145736 | tf_op jit(solution)/shard_map/ppermute | solution.py:43
  543.4 24.5 %collective-permute-start.27 = (bf16[256,2048]{1,0:T(8,128)(2,1)}, bf16[256,2048]{1,0:T(8,128)(2,1)S(1)}, u32[]{:S(2)}, u32[]{:S(2)}) collective-permute-start(bf16[256,2048]{1,0:T(8,128)(2,1)} %get-tuple-element.185), channel_id=1, source_target_pairs={{1,0},{3,1},{5,3},{7,5},{6,7},{4,6},{2,4},{0,2},{9,8},{11,9},{13,1... | collective-permute-start | bytes 3145736 | tf_op jit(solution)/shard_map/ppermute | solution.py:43
  547.0 20.9 %collective-permute-start.26 = (bf16[256,2048]{1,0:T(8,128)(2,1)}, bf16[256,2048]{1,0:T(8,128)(2,1)}, u32[]{:S(2)}, u32[]{:S(2)}) collective-permute-start(bf16[256,2048]{1,0:T(8,128)(2,1)} %get-tuple-element.186), channel_id=1, source_target_pairs={{1,3},{3,5},{5,7},{7,6},{6,4},{4,2},{2,0},{0,1},{9,11},{11,13},{13... | collective-permute-start | bytes 3145736 | tf_op jit(solution)/shard_map/ppermute | solution.py:43
  (79 other events, 1057.8 us)
Sparse Core Ops, SparseCore 0:
  163.8 28.4 all-gather.3
  193.8 28.5 all-gather.5
  224.0 28.5 all-gather.7
  457.8 37.1 reduce-scatter.7
  497.5 37.9 reduce-scatter.5
  537.9 37.9 reduce-scatter.3

commit v5 on v4

--- a/solution.py
+++ b/solution.py
@@ -9,6 +9,7 @@
 
 HW = 256
 LANES = 8
+LINE = 128
 
 
 epsilon = 1e-06
@@ -185,6 +186,10 @@
 RING_FIRST, CHIP_FIRST, RING_ONLY = 0, 1, 2
 
 
+def ring_sends(way, chips, half):
+    return {RING_FIRST: half + chips - 1, CHIP_FIRST: chips * half, RING_ONLY: half}[way]
+
+
 def gather_kernel(order, chips, cores, pieces, arrays, *refs):
     ins, outs = refs[:arrays], refs[arrays : 2 * arrays]
     own_sem, recv_sem, ring_sem, chip_sem, core_sem = refs[2 * arrays :]
@@ -194,7 +199,19 @@
     method = [piece[3] for piece in pieces]
     only_ring = {piece[0] for piece in pieces if piece[3] == RING_ONLY}
 
-    base = [sum(chips if way == CHIP_FIRST else 1 for way in method[:p]) for p in range(len(pieces) + 1)]
+    spans = [1 if way == RING_ONLY else chips * cores for way in method]
+    sharing = [p for p in range(len(pieces)) if method[p] != RING_ONLY]
+
+    def landed(p, r, k):
+        return recv_sem.at[sum(spans[:p]) + r, k]
+
+    def ring_slot(p, r, side, s):
+        at = sum(ring_sends(way, chips, half) for way in method[:p])
+        if method[p] == CHIP_FIRST or r == 0:
+            at += r * half + s
+        else:
+            at += half + r - 1
+        return ring_sem.at[at, side]
 
     def slot(i, r, k):
         return outs[i].at[0 if i in only_ring else links.dp_at[r], links.seq_at[k]]
@@ -234,11 +251,11 @@
             return [
                 remote(
                     held(p, r, (count - s) % count), whole(p, r, (count - s) % count),
-                    ring_sem.at[base[p] + r, 0, s], recv_sem.at[p, r, count - s - 1], links.ring[0],
+                    ring_slot(p, r, 0, s), landed(p, r, count - s - 1), links.ring[0],
                 ),
                 remote(
                     held(p, r, s), whole(p, r, s),
-                    ring_sem.at[base[p] + r, 1, s], recv_sem.at[p, r, s + 1], links.ring[1],
+                    ring_slot(p, r, 1, s), landed(p, r, s + 1), links.ring[1],
                 ),
             ]
         back = count - s
@@ -246,14 +263,14 @@
             return [
                 remote(
                     whole(p, r, back), whole(p, r, back),
-                    ring_sem.at[base[p] + r, 0, s], recv_sem.at[p, r, half], links.ring[0],
+                    ring_slot(p, r, 0, s), landed(p, r, half), links.ring[0],
                 )
             ]
         top, bottom = rows_in(p, r, back, 0, cut), rows_in(p, r, s, cut, rows - cut)
         return [
-            remote(top, top, ring_sem.at[base[p] + r, 0, s], recv_sem.at[p, r, half], links.ring[0]),
+            remote(top, top, ring_slot(p, r, 0, s), landed(p, r, half), links.ring[0]),
             remote(
-                bottom, bottom, ring_sem.at[base[p] + r, 1, s], recv_sem.at[p, r, count], links.ring[1]
+                bottom, bottom, ring_slot(p, r, 1, s), landed(p, r, count), links.ring[1]
             ),
         ]
 
@@ -262,17 +279,17 @@
         if k == half and cut:
             for part, sem in (((0, cut), half), ((cut, rows - cut), count)):
                 ref = rows_in(p, r, k, *part)
-                remote(ref, ref, ring_sem.at[base[p], 0, 0], recv_sem.at[p, r, sem], links.ring[0]).wait_recv()
+                remote(ref, ref, ring_slot(p, 0, 0, 0), landed(p, r, sem), links.ring[0]).wait_recv()
         else:
             ref = whole(p, r, k)
-            remote(ref, ref, ring_sem.at[base[p], 0, 0], recv_sem.at[p, r, k], links.ring[0]).wait_recv()
+            remote(ref, ref, ring_slot(p, 0, 0, 0), landed(p, r, k), links.ring[0]).wait_recv()
 
     def to_chips(p, k):
         for step in range(1, chips):
             start(
                 remote(
                     held(p, 0, k), whole(p, 0, k),
-                    chip_sem.at[p, step - 1, k], recv_sem.at[p, chips - step, k], links.chip[step - 1],
+                    chip_sem.at[sharing.index(p), step - 1, k], landed(p, chips - step, k), links.chip[step - 1],
                 )
             )
 
@@ -281,7 +298,7 @@
             start(
                 remote(
                     held(p, r, k), whole(p, r, k),
-                    core_sem.at[p, r, k], recv_sem.at[p, chips + r, k], links.core,
+                    core_sem.at[sharing.index(p), r, k], landed(p, chips + r, k), links.core,
                 )
             )
 
@@ -309,7 +326,7 @@
                     if s < half:
                         for copy in ring_copies(p, r, s):
                             start(copy)
-                    if method[p] == RING_FIRST:
+                    if method[p] == RING_FIRST and s < half:
                         for k in steps:
                             to_chips(p, k)
                     if method[p] != RING_ONLY:
@@ -319,11 +336,14 @@
             if method[p] == RING_FIRST:
                 for r in range(1, chips):
                     for k in before:
-                        arrived_from_chip(links, whole(p, r, k), chip_sem.at[p, 0, 0], recv_sem.at[p, r, k])
+                        arrived_from_chip(links, whole(p, r, k), chip_sem.at[sharing.index(p), 0, 0], landed(p, r, k))
                         to_core(p, r, k)
+                    if s == half:
+                        for copy in ring_copies(p, r, half - 1):
+                            start(copy)
             if method[p] == CHIP_FIRST and s == 1:
                 for r in range(1, chips):
-                    arrived_from_chip(links, whole(p, r, 0), chip_sem.at[p, 0, 0], recv_sem.at[p, r, 0])
+                    arrived_from_chip(links, whole(p, r, 0), chip_sem.at[sharing.index(p), 0, 0], landed(p, r, 0))
                     for copy in ring_copies(p, r, 0):
                         start(copy)
                     to_core(p, r, 0)
@@ -338,14 +358,14 @@
     for p in everyone:
         if method[p] == RING_FIRST:
             for r in range(1, chips):
-                arrived_from_chip(links, whole(p, r, half), chip_sem.at[p, 0, 0], recv_sem.at[p, r, half])
+                arrived(p, r, half)
                 to_core(p, r, half)
     for p in everyone:
         if method[p] != RING_ONLY and cores == 2:
             for r in range(chips):
                 for k in range(count):
                     arrived_from_chip(
-                        links, whole(p, chips + r, k), core_sem.at[p, r, k], recv_sem.at[p, chips + r, k]
+                        links, whole(p, chips + r, k), core_sem.at[sharing.index(p), r, k], landed(p, chips + r, k)
                     )
     for copy in sent:
         copy.wait_send()
@@ -361,6 +381,7 @@
     chips, cores, count = net.chips, net.cores, net.seq_count
     slots = chips * cores
     only_ring = {piece[0] for piece in pieces if piece[3] == RING_ONLY}
+    shared = sum(piece[3] != RING_ONLY for piece in pieces)
     anywhere = pl.BlockSpec(memory_space=pl.ANY)
     return pl.pallas_call(
         functools.partial(gather_kernel, net.order, chips, cores, pieces, len(arrays)),
@@ -372,15 +393,17 @@
         out_specs=[anywhere] * len(arrays),
         scratch_shapes=[
             pltpu.SemaphoreType.DMA((len(arrays),)),
-            pltpu.SemaphoreType.DMA((len(pieces), slots, count + 1)),
             pltpu.SemaphoreType.DMA(
-                (sum(chips if piece[3] == CHIP_FIRST else 1 for piece in pieces), 2, count // 2)
+                (sum(1 if piece[3] == RING_ONLY else slots for piece in pieces), count + 1)
             ),
-            pltpu.SemaphoreType.DMA((len(pieces), max(chips - 1, 1), count)),
-            pltpu.SemaphoreType.DMA((len(pieces), chips, count)),
+            pltpu.SemaphoreType.DMA(
+                (sum(ring_sends(piece[3], chips, count // 2) for piece in pieces), 2)
+            ),
+            pltpu.SemaphoreType.DMA((shared, max(chips - 1, 1), count)),
+            pltpu.SemaphoreType.DMA((shared, chips, count)),
         ],
         compiler_params=pltpu.CompilerParams(
-            collective_id=3, has_side_effects=True, vmem_limit_bytes=32 * 2**20
+            collective_id=3, has_side_effects=True, vmem_limit_bytes=60 * 2**20
         ),
         cost_estimate=pl.CostEstimate(
             flops=0, bytes_accessed=slots * count * sum(v.size for v in arrays) * 4, transcendentals=0
@@ -609,7 +632,7 @@
             pltpu.SemaphoreType.DMA((n, chips, 2, half)),
         ],
         compiler_params=pltpu.CompilerParams(
-            collective_id=4, has_side_effects=True, vmem_limit_bytes=62 * 2**20
+            collective_id=4, has_side_effects=True, vmem_limit_bytes=63 * 2**20
         ),
         cost_estimate=pl.CostEstimate(
             flops=0, bytes_accessed=sum(terms.size for terms in arrays) * 4, transcendentals=0
@@ -888,14 +911,14 @@
     )
 
 
-def ff_kernel(
-    order, own_ref, gate_hbm, up_hbm, down_hbm, *refs
-):
-    cot_count = len(refs) - 21
+def ff_kernel(order, cores, own_ref, gate_hbm, up_hbm, down_hbm, *refs):
+    cot_count = len(refs) - 37
     cot_hbm, refs = refs[:cot_count], refs[cot_count:]
-    blocks_ref, cot_ref, hidden_ref, d_gate_ref, d_up_ref, out_ref, d_in_ref, *refs = refs
+    blocks_ref, out_ref, d_in_ref, gate_grad, up_grad, down_grad, sum_ref, *refs = refs
     gate_ref, up_ref, down_ref, rows_ref, cots_ref, h_ref, g_ref, u_ref, o_ref, d_ref, *refs = refs
-    send_sem, recv_sem, load_sem, store_sem = refs
+    lone_refs, refs = refs[:7], refs[7:]
+    gate_sum, up_sum, down_sum, landing, mine, *refs = refs
+    send_sem, recv_sem, load_sem, store_sem, back_send, back_recv, mine_sem, done_sem = refs
     count = len(order)
     half = count // 2
     rows, width = own_ref.shape
@@ -906,13 +929,14 @@
     for i, device in enumerate(order):
         ahead_of[device] = order[(i + 1) % count]
         behind_of[device] = order[(i - 1) % count]
-    sides = (lookup(ahead_of, me), lookup(behind_of, me))
+    sides = ({"seq": lookup(ahead_of, me)}, {"seq": lookup(behind_of, me)})
+    dp = lax.axis_index("dp")
+    core = {"dp": dp + 1 - 2 * lax.rem(dp, 2)}
 
     barrier = pltpu.get_barrier_semaphore()
-    for side in sides:
-        pl.semaphore_signal(
-            barrier, inc=1, device_id={"seq": side}, device_id_type=pl.DeviceIdType.MESH
-        )
+    peers = list(sides) + ([core] if cores == 2 else [])
+    for peer in peers:
+        pl.semaphore_signal(barrier, inc=1, device_id=peer, device_id_type=pl.DeviceIdType.MESH)
     weights = [
         pltpu.make_async_copy(hbm, vmem, load_sem.at[i])
         for i, (hbm, vmem) in enumerate(
@@ -921,170 +945,309 @@
     ]
     for copy in weights:
         copy.start()
-    keep = pltpu.make_async_copy(own_ref, blocks_ref.at[count - 1], load_sem.at[3])
-    keep.start()
-    pl.semaphore_wait(barrier, 2)
+    pl.semaphore_wait(barrier, len(peers))
 
     def full(side, source, slot, s):
-        return pltpu.make_async_remote_copy(
-            src_ref=source,
-            dst_ref=blocks_ref.at[slot],
-            send_sem=send_sem.at[side, s],
-            recv_sem=recv_sem.at[slot],
-            device_id={"seq": sides[side]},
-            device_id_type=pl.DeviceIdType.MESH,
+        return remote(
+            source, blocks_ref.at[slot], send_sem.at[side, s], recv_sem.at[slot], sides[side]
         )
 
     def part(side):
         at = pl.ds(0, cut) if side == 0 else pl.ds(cut, rows - cut)
-        return pltpu.make_async_remote_copy(
-            src_ref=blocks_ref.at[2 * (half - 2) + side, at],
-            dst_ref=blocks_ref.at[count - 2, at],
-            send_sem=send_sem.at[side, half - 1],
-            recv_sem=recv_sem.at[count - 2 + side],
-            device_id={"seq": sides[side]},
-            device_id_type=pl.DeviceIdType.MESH,
+        return remote(
+            blocks_ref.at[2 * (half - 2) + side, at],
+            blocks_ref.at[count - 2, at],
+            send_sem.at[side, half - 1],
+            recv_sem.at[count - 2 + side],
+            sides[side],
         )
 
     for side in range(2):
         full(side, own_ref, side, 0).start()
-    keep.wait()
-    for copy in weights:
-        copy.wait()
-
-    rows_load = lambda s: pltpu.make_async_copy(
-        blocks_ref.at[pl.ds(2 * (s - 1), 2)], rows_ref, load_sem.at[4]
-    )
-
-    def cot_loads(s):
-        if s < half:
-            return [
-                pltpu.make_async_copy(cot_hbm[2 * s - 1 + i], cots_ref.at[i], load_sem.at[5 + i])
-                for i in range(2)
-            ]
-        copies = [pltpu.make_async_copy(cot_hbm[0], cots_ref.at[1], load_sem.at[5])]
-        first = 0
-        for i, part_hbm in enumerate(cot_hbm[2 * half - 1 :]):
-            part_rows = part_hbm.shape[0]
-            copies.append(
-                pltpu.make_async_copy(
-                    part_hbm, cots_ref.at[0, pl.ds(first, part_rows)], load_sem.at[6 + i]
-                )
-            )
-            first += part_rows
-        return copies
+
+    def rows_load(s):
+        return pltpu.make_async_copy(
+            blocks_ref.at[pl.ds(2 * (s - 1), 2)], rows_ref, load_sem.at[3]
+        )
+
+    pair_refs = (rows_ref, cots_ref, h_ref, g_ref, u_ref, o_ref, d_ref)
 
     def stores(s):
         return [
-            pltpu.make_async_copy(vmem, hbm.at[s - 1], store_sem.at[i])
-            for i, (vmem, hbm) in enumerate(
-                (
-                    (cots_ref, cot_ref),
-                    (h_ref, hidden_ref),
-                    (g_ref, d_gate_ref),
-                    (u_ref, d_up_ref),
-                    (o_ref, out_ref),
-                    (d_ref, d_in_ref),
-                )
-            )
+            pltpu.make_async_copy(o_ref, out_ref.at[s - 1], store_sem.at[0]),
+            pltpu.make_async_copy(d_ref, d_in_ref.at[s - 1], store_sem.at[1]),
         ]
 
-    def step(s, carry):
-        @pl.when(s < half)
-        def _():
-            for side in range(2):
-                full(side, own_ref, 2 * (s - 1) + side, s).wait_recv()
-
-            @pl.when(s < half - 1)
-            def _():
-                for side in range(2):
-                    slot = 2 * (s - 1) + side
-                    full(side, blocks_ref.at[slot], slot + 2, s).start()
-
-            @pl.when(s == half - 1)
-            def _():
-                for side in range(2):
-                    part(side).start()
-
-        @pl.when(s == half)
-        def _():
-            for side in range(2):
-                part(side).wait_recv()
-
-        rows_load(s).start()
-
-        @pl.when(s > 1)
-        def _():
-            for copy in stores(s - 1):
-                copy.wait()
-
-        for at_step in range(1, half + 1):
-
-            @pl.when(s == at_step)
-            def _():
-                copies = cot_loads(at_step)
-                for copy in copies:
-                    copy.start()
-                for copy in copies:
-                    copy.wait()
-
-        rows_load(s).wait()
-        wide = 256 if hidden_here % 256 == 0 else 128
+    def lone_stores(first):
+        at = pl.ds(first * rows, rows)
+        return [
+            pltpu.make_async_copy(lone_refs[5], out_ref.at[half - 1, at], store_sem.at[2]),
+            pltpu.make_async_copy(lone_refs[6], d_in_ref.at[half - 1, at], store_sem.at[3]),
+        ]
+
+    wide = 256 if hidden_here % 256 == 0 else 128
+    out_wide = 512
+
+    def multiply(refs):
+        x_ref, c_ref, h_to, g_to, u_to, o_to, d_to = refs
+        many = h_to.shape[0]
 
         def inner(j, carry):
             at = pl.ds(pl.multiple_of(j * wide, wide), wide)
-            x = rows_ref[...].reshape(2 * rows, width)
-            c = cots_ref[...].reshape(2 * rows, width)
+            x = x_ref[...].reshape(many, width)
+            c = c_ref[...].reshape(many, width)
             ff_gate = contract(x, gate_ref[:, at], 1, 0)
             ff_up = contract(x, up_ref[:, at], 1, 0)
             d_hidden = contract(c, down_ref[at, :], 1, 1)
             act, slope = gelu_parts(ff_gate)
-            h_ref[:, at] = (act * ff_up).astype(bf16)
-            g_ref[:, at] = (d_hidden * ff_up * slope).astype(bf16)
-            u_ref[:, at] = (d_hidden * act).astype(bf16)
+            h_to[:, at] = (act * ff_up).astype(bf16)
+            g_to[:, at] = (d_hidden * ff_up * slope).astype(bf16)
+            u_to[:, at] = (d_hidden * act).astype(bf16)
             return carry
 
         lax.fori_loop(0, hidden_here // wide, inner, 0)
-        out_wide = 512
 
         def outer(j, carry):
             at = pl.ds(pl.multiple_of(j * out_wide, out_wide), out_wide)
-            o_ref[:, at] = contract(h_ref[...], down_ref[:, at], 1, 0).astype(bf16)
-            d_ref[:, at] = (
-                contract(g_ref[...], gate_ref[at, :], 1, 1)
-                + contract(u_ref[...], up_ref[at, :], 1, 1)
+            d_to[:, at] = (
+                contract(g_to[...], gate_ref[at, :], 1, 1) + contract(u_to[...], up_ref[at, :], 1, 1)
             ).astype(bf16)
+            o_to[:, at] = contract(h_to[...], down_ref[:, at], 1, 0).astype(bf16)
             return carry
 
         lax.fori_loop(0, width // out_wide, outer, 0)
+
+    def gradients(refs, fresh=False):
+        x_ref, c_ref, h_to, g_to, u_to = refs[:5]
+        many = h_to.shape[0]
+        tile = 256
+
+        def body(j, carry):
+            at = pl.ds(pl.multiple_of(j * tile, tile), tile)
+            x = x_ref[..., at].reshape(many, tile)
+            c = c_ref[..., at].reshape(many, tile)
+            terms = (
+                contract(x, g_to[...], 0, 0),
+                contract(x, u_to[...], 0, 0),
+                contract(h_to[...], c, 0, 0),
+            )
+            places = (
+                (gate_sum, (at, slice(None))),
+                (up_sum, (at, slice(None))),
+                (down_sum, (slice(None), at)),
+            )
+            for term, (ref, place) in zip(terms, places):
+                ref[place] = term if fresh else ref[place] + term
+            return carry
+
+        lax.fori_loop(0, width // tile, body, 0)
+
+    def run(copies):
+        for copy in copies:
+            copy.start()
+        for copy in copies:
+            copy.wait()
+
+    run(
+        [
+            pltpu.make_async_copy(own_ref, lone_refs[0], load_sem.at[3]),
+            pltpu.make_async_copy(cot_hbm[0], lone_refs[1], load_sem.at[4]),
+        ]
+    )
+    for copy in weights:
+        copy.wait()
+    multiply(lone_refs)
+    for copy in lone_stores(1):
+        copy.start()
+    gradients(lone_refs, True)
+    for copy in lone_stores(1):
+        copy.wait()
+
+    def step(s, carry):
+        for side in range(2):
+            full(side, own_ref, 2 * (s - 1) + side, s).wait_recv()
+
+        @pl.when(s < half - 1)
+        def _():
+            for side in range(2):
+                slot = 2 * (s - 1) + side
+                full(side, blocks_ref.at[slot], slot + 2, s).start()
+
+        @pl.when(s == half - 1)
+        def _():
+            for side in range(2):
+                part(side).start()
+
+        rows_load(s).start()
+        for at_step in range(1, half):
+
+            @pl.when(s == at_step)
+            def _():
+                run(
+                    [
+                        pltpu.make_async_copy(
+                            cot_hbm[2 * at_step - 1 + i], cots_ref.at[i], load_sem.at[4 + i]
+                        )
+                        for i in range(2)
+                    ]
+                )
+
+        rows_load(s).wait()
+        multiply(pair_refs)
         for copy in stores(s):
             copy.start()
+
+        @pl.when(s < half - 1)
+        def _():
+            gradients(pair_refs)
+
+        for copy in stores(s):
+            copy.wait()
         return carry
 
-    lax.fori_loop(1, half + 1, step, 0)
-    for copy in stores(half):
+    lax.fori_loop(1, half, step, 0)
+    far, first = [], 0
+    for i, part_hbm in enumerate(cot_hbm[2 * half - 1 :]):
+        part_rows = part_hbm.shape[0]
+        far.append(
+            pltpu.make_async_copy(
+                part_hbm, lone_refs[1].at[pl.ds(first, part_rows)], load_sem.at[5 + i]
+            )
+        )
+        first += part_rows
+    run(far)
+    for side in range(2):
+        part(side).wait_recv()
+    run([pltpu.make_async_copy(blocks_ref.at[count - 2], lone_refs[0], load_sem.at[3])])
+    multiply(lone_refs)
+
+    chunks = 2
+    chunk = width // chunks
+
+    def part_of(d, side):
+        if d == 0:
+            return half - 1, rows
+        return d - 1, (rows if side == 0 else 0)
+
+    def own_load(d, side):
+        pair, first = part_of(d, side)
+        return pltpu.make_async_copy(
+            d_in_ref.at[pair, pl.ds(first, rows)], mine.at[side, d % 2], mine_sem.at[side, d % 2]
+        )
+
+    def back(d, side, c):
+        cols = pl.ds(c * chunk, chunk)
+        at = pl.ds(0, rows)
+        if d == half:
+            at = pl.ds(0, cut) if side == 0 else pl.ds(cut, rows - cut)
+            source = lone_refs[6].at[at, cols]
+        else:
+            source = mine.at[side, d % 2, at, cols]
+        return remote(
+            source,
+            landing.at[side, d - 1, at, cols],
+            back_send.at[side, d - 1, c],
+            back_recv.at[side, d - 1, c],
+            sides[side],
+        )
+
+    def add_landed(target, terms, first, many, cols):
+        def body(t, carry):
+            at = pl.ds(pl.multiple_of(first + t * 16, 16), 16)
+            target[at, cols] = total([term[at, cols].astype(f32) for term in terms]).astype(target.dtype)
+            return carry
+
+        lax.fori_loop(0, many // 16, body, 0)
+
+    for c in range(chunks):
+        for side in range(2):
+            back(half, side, c).start()
+    for copy in lone_stores(0):
+        copy.start()
+    for side in range(2):
+        own_load(half - 1, side).start()
+    gradients(pair_refs)
+    gradients(lone_refs)
+
+    def finish(total_ref, low_ref, out_hbm, sem):
+        def body(t, carry):
+            at = pl.ds(pl.multiple_of(t * 16, 16), 16)
+            low_ref[at, :] = total_ref[at, :].astype(bf16)
+            return carry
+
+        lax.fori_loop(0, total_ref.shape[0] // 16, body, 0)
+        copy = pltpu.make_async_copy(low_ref, out_hbm, load_sem.at[sem])
+        copy.start()
+        return copy
+
+    results = ((gate_sum, gate_ref, gate_grad), (up_sum, up_ref, up_grad), (down_sum, down_ref, down_grad))
+    finished = []
+    for d in range(half - 1, 0, -1):
+        for side in range(2):
+            own_load(d, side).wait()
+        for c in range(chunks):
+            cols = pl.ds(c * chunk, chunk)
+            for side in range(2):
+                back(d + 1, side, c).wait_recv()
+                first, many = (0, rows)
+                if d == half - 1:
+                    first, many = (0, cut) if side == 0 else (cut, rows - cut)
+                held = mine.at[side, d % 2]
+                add_landed(held, [held, landing.at[side, d]], first, many, cols)
+                back(d, side, c).start()
+        for side in range(2):
+            if d < half - 1:
+                for c in range(chunks):
+                    back(d + 1, side, c).wait_send()
+            if d > 1 or side == 0:
+                own_load(d - 1, side).start()
+        if len(finished) < len(results):
+            finished.append(finish(*results[len(finished)], len(finished)))
+    own_load(0, 0).wait()
+    for c in range(chunks):
+        cols = pl.ds(c * chunk, chunk)
+        for side in range(2):
+            back(1, side, c).wait_recv()
+        add_landed(sum_ref, [mine.at[0, 0], landing.at[0, 0], landing.at[1, 0]], 0, rows, cols)
+    if cores == 2:
+        pl.semaphore_signal(done_sem, inc=1, device_id=core, device_id_type=pl.DeviceIdType.MESH)
+    while len(finished) < len(results):
+        finished.append(finish(*results[len(finished)], len(finished)))
+    for copy in finished:
+        copy.wait()
+    for copy in lone_stores(0):
         copy.wait()
     for side in range(2):
+        for c in range(chunks):
+            back(half, side, c).wait_send()
+            back(1, side, c).wait_send()
         for s in range(half - 1):
             full(side, own_ref, side, s).wait_send()
         part(side).wait_send()
-
-
-def ff_call(order, own, cots, slab_gate, slab_up, slab_down):
+    if cores == 2:
+        pl.semaphore_wait(done_sem, 1)
+
+
+def ff_call(net, own, cots, slab_gate, slab_up, slab_down):
     rows, width = own.shape
-    count, half = len(order), len(order) // 2
+    count, half = net.seq_count, net.seq_count // 2
     hidden_here = slab_gate.shape[1]
     anywhere = pl.BlockSpec(memory_space=pl.ANY)
     pair = 2 * rows
     shape = jax.ShapeDtypeStruct
-    flops = 12 * count * rows * width * hidden_here
     return pl.pallas_call(
-        functools.partial(ff_kernel, order),
-        out_shape=[shape((count, rows, width), bf16), shape((half, 2, rows, width), bf16)]
-        + [shape((half, pair, hidden_here), bf16)] * 3
-        + [shape((half, pair, width), bf16)] * 2,
+        functools.partial(ff_kernel, net.order, net.cores),
+        out_shape=[
+            shape((count, rows, width), bf16),
+            shape((half, pair, width), bf16),
+            shape((half, pair, width), bf16),
+            shape((width, hidden_here), bf16),
+            shape((width, hidden_here), bf16),
+            shape((hidden_here, width), bf16),
+            shape((rows, width), f32),
+        ],
         in_specs=[anywhere] * (4 + len(cots)),
-        out_specs=[anywhere] * 7,
+        out_specs=[anywhere] * 6 + [pl.BlockSpec(memory_space=pltpu.VMEM)],
         scratch_shapes=[
             pltpu.VMEM((width, hidden_here), bf16),
             pltpu.VMEM((width, hidden_here), bf16),
@@ -1096,16 +1259,34 @@
             pltpu.VMEM((pair, hidden_here), bf16),
             pltpu.VMEM((pair, width), bf16),
             pltpu.VMEM((pair, width), bf16),
+            pltpu.VMEM((rows, width), bf16),
+            pltpu.VMEM((rows, width), bf16),
+            pltpu.VMEM((rows, hidden_here), bf16),
+            pltpu.VMEM((rows, hidden_here), bf16),
+            pltpu.VMEM((rows, hidden_here), bf16),
+            pltpu.VMEM((rows, width), bf16),
+            pltpu.VMEM((rows, width), bf16),
+            pltpu.VMEM((width, hidden_here), f32),
+            pltpu.VMEM((width, hidden_here), f32),
+            pltpu.VMEM((hidden_here, width), f32),
+            pltpu.VMEM((2, half, rows, width), bf16),
+            pltpu.VMEM((2, 2, rows, width), bf16),
             pltpu.SemaphoreType.DMA((2, half)),
             pltpu.SemaphoreType.DMA((count,)),
             pltpu.SemaphoreType.DMA((8,)),
-            pltpu.SemaphoreType.DMA((6,)),
+            pltpu.SemaphoreType.DMA((4,)),
+            pltpu.SemaphoreType.DMA((2, half, 2)),
+            pltpu.SemaphoreType.DMA((2, half, 2)),
+            pltpu.SemaphoreType.DMA((2, 2)),
+            pltpu.SemaphoreType.REGULAR,
         ],
         compiler_params=pltpu.CompilerParams(
-            collective_id=2, has_side_effects=True, vmem_limit_bytes=48 * 2**20
+            collective_id=2, has_side_effects=True, vmem_limit_bytes=62 * 2**20
         ),
         cost_estimate=pl.CostEstimate(
-            flops=flops, bytes_accessed=60 * 2**20, transcendentals=count * rows * hidden_here
+            flops=18 * count * rows * width * hidden_here,
+            bytes_accessed=80 * 2**20,
+            transcendentals=count * rows * hidden_here,
         ),
     )(own, slab_gate, slab_up, slab_down, *cots)
 
@@ -1183,45 +1364,58 @@
     taps = conv_w.shape[0]
     rim_rows = taps - 1
 
-    vectors = [norm1_gain, norm2_gain, conv_w.reshape(-1), conv_bias, rgate_bias, igate_bias, decay_param]
-    lengths = [v.shape[0] for v in vectors]
-    flat = jnp.concatenate(vectors)
-    small_rows = -(-flat.shape[0] // HW)
-    flat = jnp.pad(flat, (0, small_rows * HW - flat.shape[0]))
-    half_rows = chan_here * 3 // 5 // 16 * 16
-    out_pieces = [(2, 0, half_rows, RING_FIRST), (2, half_rows, chan_here - half_rows, CHIP_FIRST)]
-    if half_rows == 0 or chan_here % 16:
-        out_pieces = [(2, 0, chan_here, RING_FIRST)]
-    small_pieces = [(3, 0, small_rows, RING_FIRST), (4, 0, chan_here, RING_FIRST)]
-    full_in, full_gate, full_out, flat_all, full_both, start_state = gather_call(
+    def lanes(rows):
+        return jnp.pad(rows, ((0, 0),) * (rows.ndim - 1) + ((0, LINE - rows.shape[-1]),))
+
+    vectors = [norm1_gain, norm2_gain, conv_w, conv_bias, rgate_bias, igate_bias, decay_param]
+    small = jnp.concatenate([lanes(v.reshape(-1, v.shape[-1])) for v in vectors], 0)
+    rim_inputs = inputs.reshape(rows_here, width)[rows_here - rim_rows :]
+    full_in, full_gate, full_out, small_all, full_both, start_state, rims, flags = gather_call(
         net,
         (
             w_in,
             w_gate,
             w_out,
-            flat.reshape(small_rows, HW),
+            small,
             jnp.concatenate([w_rgate, w_igate], 1),
             initial_state,
+            rim_inputs,
+            reset.astype(f32),
         ),
-        small_pieces
-        + [(0, 0, wide_here, RING_FIRST), (1, 0, wide_here, CHIP_FIRST)]
-        + out_pieces
-        + [(5, 0, 1, RING_ONLY)],
+        [
+            (6, 0, rim_rows, RING_ONLY),
+            (7, 0, 1, RING_ONLY),
+            (3, 0, small.shape[0], RING_FIRST),
+            (4, 0, chan_here, RING_FIRST),
+            (0, 0, wide_here, RING_FIRST),
+            (1, 0, wide_here, CHIP_FIRST),
+            (2, 0, chan_here, RING_FIRST),
+            (5, 0, 1, RING_ONLY),
+        ],
     )
     full_in, full_gate = (v.reshape(width, channels) for v in (full_in, full_gate))
     full_out = full_out.reshape(channels, width)
     full_both = full_both.reshape(channels, 2 * HW)
     start_state = start_state.reshape(1, channels)
-    flat_all = flat_all.reshape(devices, small_rows * HW)
-    pieces, at = [], 0
-    for length in lengths:
-        pieces.append(flat_all[:, at : at + length])
-        at += length
-    full_norm1 = pieces[0].reshape(-1).astype(f32)
-    full_norm2 = pieces[1].reshape(-1).astype(f32)
-    conv_wf = pieces[2].reshape(devices, taps, chan_here).transpose(1, 0, 2).reshape(taps, channels).astype(f32)
-    full_cbias, full_rbias, full_ibias, decay_f = (p.reshape(-1).astype(f32) for p in pieces[3:])
+    small_all = small_all.reshape(devices, -1, LINE)
+    full_norm1 = small_all[:, 0, :wide_here].reshape(-1).astype(f32)
+    full_norm2 = small_all[:, 1, :wide_here].reshape(-1).astype(f32)
+    conv_wf = small_all[:, 2 : 2 + taps, :chan_here].transpose(1, 0, 2).reshape(taps, channels).astype(f32)
+    full_cbias, full_rbias, full_ibias, decay_f = (
+        small_all[:, i, :chan_here].reshape(-1).astype(f32) for i in range(2 + taps, 6 + taps)
+    )
     gate_vectors = jnp.stack([full_rbias, full_ibias, -8.0 * jax.nn.softplus(-decay_f)], 0)
+    at_seq = lax.axis_index("seq")
+    last_seq = seq_count - 1
+
+    def neighbour(values, index, there):
+        picked = lax.dynamic_index_in_dim(values[0], jnp.clip(index, 0, last_seq), 0, keepdims=False)
+        return jnp.where(there, picked, jnp.zeros_like(picked))
+
+    rim_before = neighbour(rims, at_seq - 1, at_seq > 0)
+    flags_before = neighbour(flags, at_seq - 1, at_seq > 0)[0, rows_here - rim_rows :]
+    flags_after = neighbour(flags, at_seq + 1, at_seq < last_seq)[0, :rim_rows]
+    flags_here = reset.reshape(rows_here).astype(f32)
     w_ffgate, w_ffup, w_ffdown, cotangent, full_in = lax.optimization_barrier(
         (w_ffgate, w_ffup, w_ffdown, cotangent, full_in)
     )
@@ -1233,18 +1427,17 @@
     cotan_rows = cotangent.reshape(rows_here, width)
     cot_flow = Flow(net.seq.gather_steps(cotan_rows))
 
+    lead = 8 - rim_rows
     token_rows = inputs.reshape(rows_here, width).astype(f32)
     normed_f, scale_one, unit_one = rms_parts(token_rows, full_norm1)
     normed = normed_f.astype(bf16)
-    branch = dot(normed, full_in).astype(bf16)
-    branch = beside(branch, cot_flow)
+    rim_normed = rms_parts(rim_before.astype(f32), full_norm1)[0].astype(bf16)
+    extended = jnp.concatenate([jnp.pad(rim_normed, ((lead, 0), (0, 0))), normed], 0)
+    branch = dot(extended, full_in).astype(bf16)
     gate_pre = dot(normed, full_gate)
-    reset_flags = reset.reshape(rows_here).astype(bf16)
-    rim_branch, rim_flags = passed_along(
-        (branch[len_here - rim_rows :], reset_flags[len_here - rim_rows :]), "seq", 1
-    )
-    padded = jnp.concatenate([rim_branch, branch], 0).astype(f32)
-    open_pad = (1.0 - jnp.concatenate([rim_flags, reset_flags], 0).astype(f32))[:, None]
+    branch, gate_pre = beside((branch, gate_pre), cot_flow)
+    padded = branch[lead:].astype(f32)
+    open_pad = (1.0 - jnp.concatenate([flags_before, flags_here], 0))[:, None]
     open_masks = [None]
     conv_total = full_cbias + conv_wf[0] * rows_of(padded, rim_rows, len_here)
     running = rows_of(open_pad, rim_rows, len_here)
@@ -1257,7 +1450,6 @@
         )
     conv_low = conv_total.astype(bf16)
     reset_col = reset.astype(f32).reshape(rows_here, 1)
-    conv_low, gate_pre = beside((conv_low, gate_pre), cot_flow)
     decay_rows, drive_rows = gate_call(
         gate_kernel, conv_low, full_both, gate_vectors, reset_col, (), [("rows", f32)] * 2
     )
@@ -1284,27 +1476,17 @@
     cots = [cotan_rows] + [cot_blocks[k] for k in slots[:-2]] + cot_blocks[seq_count // 2]
     normed_two_f, scale_two, unit_two = rms_parts(residual, full_norm2)
     normed_two = normed_two_f.astype(bf16)
-    group_normed, group_cotan, hidden, d_ffgate, d_ffup, out_part, d_normed_part = ff_call(
-        net.order, normed_two, cots, slab_gate, slab_up, slab_down
-    )
-    group_rows = seq_count * rows_here
-    group_normed = group_normed.reshape(group_rows, width)
-    group_cotan = group_cotan.reshape(group_rows, width)
-    hidden, d_ffgate, d_ffup = (v.reshape(group_rows, -1) for v in (hidden, d_ffgate, d_ffup))
+    _, out_part, _, gate_part, up_part, down_part, d_normed_two = ff_call(
+        net, normed_two, cots, slab_gate, slab_up, slab_down
+    )
 
     def block_rows(whole):
         whole = whole.reshape(seq_count, rows_here, width)
         return lambda k: whole[slots.index(k)]
 
-    d_normed_flow = Flow(net.seq.scatter_steps(block_rows(d_normed_part)))
-    gate_part = beside(t_dot(group_normed, d_ffgate).astype(bf16), d_normed_flow)
-    up_part = beside(t_dot(group_normed, d_ffup).astype(bf16), d_normed_flow)
-    down_part = beside(t_dot(hidden, group_cotan).astype(bf16), d_normed_flow)
-    d_normed_sum = d_normed_flow.finish()
-    d_normed_sum, out_part, gate_part, up_part, down_part = lax.optimization_barrier(
-        (d_normed_sum, out_part, gate_part, up_part, down_part)
-    )
-    d_normed_two = d_normed_sum
+    d_normed_two, out_part, gate_part, up_part, down_part = lax.optimization_barrier(
+        (d_normed_two, out_part, gate_part, up_part, down_part)
+    )
     out_flow = Flow(net.seq.scatter_steps(block_rows(out_part)))
     grad_ffgate, grad_ffup, grad_ffdown = (
         lax.psum_scatter(part, "dp", scatter_dimension=axis, tiled=True).astype(f32)
@@ -1344,9 +1526,9 @@
     d_conv_low, out_terms = beside((d_conv_low, out_terms), out_flow)
     grad_rbias, grad_ibias, rate_sum, grad_cbias = gate_sums
     grad_decay = 8.0 * jax.nn.sigmoid(-decay_f) * rate_sum
-    rim_grad, rim_next = passed_along((d_conv_low[:rim_rows], reset_flags[:rim_rows]), "seq", -1)
+    rim_grad = passed_along(d_conv_low[:rim_rows], "seq", -1)
     grad_ext = jnp.concatenate([d_conv_low, rim_grad], 0).astype(f32)
-    open_next = (1.0 - jnp.concatenate([reset_flags, rim_next], 0).astype(f32))[:, None]
+    open_next = (1.0 - jnp.concatenate([flags_here, flags_after], 0))[:, None]
     d_conv_f = rows_of(grad_ext, 0, len_here)
     d_branch = conv_wf[0] * d_conv_f
     ahead = None
@@ -1372,35 +1554,35 @@
     ff_out = out_flow.finish()
     output = (residual + ff_out).astype(bf16).reshape(seqs_here, len_here, width)
 
-    conv_flat = grad_conv.reshape(taps, devices, chan_here).transpose(1, 0, 2)
-    flat_grads = jnp.concatenate(
-        [
-            v.reshape(devices, -1)
-            for v in (grad_norm1, grad_norm2, conv_flat, grad_cbias, grad_rbias, grad_ibias, grad_decay)
-        ],
-        1,
-    )
-    flat_grads = jnp.pad(flat_grads, ((0, 0), (0, small_rows * HW - flat_grads.shape[1])))
-    flat_terms = flat_grads.astype(bf16).reshape(dp_count, seq_count, small_rows, HW)
-    turned = [(i, first, rows, RING_FIRST + CHIP_FIRST - way) for i, first, rows, way in out_pieces]
-    grad_in, grad_gate, grad_out, flat_mine, both_mine = reduce_call(
+    small_grads = [
+        lanes(v.reshape(-1, devices, v.shape[-1] // devices).transpose(1, 0, 2)).astype(bf16)
+        for v in (grad_norm1, grad_norm2, grad_conv, grad_cbias, grad_rbias, grad_ibias, grad_decay)
+    ]
+    small_terms = jnp.concatenate(small_grads, 1).reshape(dp_count, seq_count, -1, LINE)
+    half_rows = chan_here * 3 // 5 // 16 * 16
+    out_pieces = [(2, 0, half_rows, CHIP_FIRST), (2, half_rows, chan_here - half_rows, RING_FIRST)]
+    if half_rows == 0 or chan_here % 16:
+        out_pieces = [(2, 0, chan_here, CHIP_FIRST)]
+    grad_in, grad_gate, grad_out, small_mine, both_mine = reduce_call(
         net,
         [
             in_terms,
             gate_terms,
             out_terms,
-            flat_terms,
+            small_terms,
             both_terms.reshape(dp_count, seq_count, chan_here, 2 * HW),
         ],
         [(1, 0, wide_here, RING_FIRST)]
-        + turned
-        + [(3, 0, small_rows, CHIP_FIRST), (4, 0, chan_here, CHIP_FIRST), (0, 0, wide_here, CHIP_FIRST)],
-    )
-    flat_mine = flat_mine.reshape(-1)
-    mine, at = [], 0
-    for length in lengths:
-        mine.append(flat_mine[at : at + length])
-        at += length
+        + out_pieces
+        + [
+            (3, 0, small.shape[0], CHIP_FIRST),
+            (4, 0, chan_here, CHIP_FIRST),
+            (0, 0, wide_here, CHIP_FIRST),
+        ],
+    )
+    mine = [small_mine[i, :wide_here] for i in range(2)]
+    mine += [small_mine[2 : 2 + taps, :chan_here]]
+    mine += [small_mine[i, :chan_here] for i in range(2 + taps, 6 + taps)]
     return (
         output,
         input_grad,
@@ -1408,7 +1590,7 @@
         mine[0],
         grad_gate,
         grad_in,
-        mine[2].reshape(taps, chan_here),
+        mine[2],
         mine[3],
         both_mine[:, :HW],
         mine[4],

time: 730 us -> 721 us (0.988)
  Pallas kernels: 418 us -> 497 us
  matrix products: 97.2 us -> 61.9 us
  waiting for transfers between devices: 57.6 us -> 34.7 us
  local copies, waits for them, and re-layouts: 39.9 us -> 26 us
  starting transfers between devices: 38.2 us -> 30 us
    pallas_call x1, Pallas kernels: 101 us -> 178 us  [ff_call(): pl.pallas_call(functools.partial(ff_kernel, net.order, net.cores), out_sh...]
    dot_general x6 -> x3, matrix products: 48.5 us -> 17 us  [t_dot(): lax.dot_general(left, right, (((0,), (0,)), ((), ())), preferred_element_...]
    ppermute x24 -> x16, waiting for transfers between devices: 54.6 us -> 33.4 us  [shift(): return lax.ppermute(value, self.axis, pairs)]
    unnamed x142 -> x101, local copies, waits for them, and re-layouts: 20.8 us -> 6.93 us
    ppermute x4 -> x1, starting transfers between devices: 10.5 us -> 1.29 us  [passed_along(): lax.ppermute(value, axis, [(source, source + steps) for source in range(f...]
    pallas_call x2, Pallas kernels: 34.2 us -> 42.7 us  [scan_call(): pl.pallas_call(functools.partial(kernel, count), out_shape=out_shapes, in...]
    convert_element_type x4 -> x2, other arithmetic: 16 us -> 8.44 us  [scatter_steps(): ahead, behind = (ahead.astype(bf16), behind.astype(bf16))]
    ppermute x24 -> x16, starting transfers between devices: 27.5 us -> 28.5 us  [shift(): return lax.ppermute(value, self.axis, pairs)]
  transfers between devices with their start and end apart: 34 -> 23, of which waited for: 10 -> 7; matrix products, arithmetic and copies ran while one was open for 20% -> 16% of each run, Pallas kernels for 24% -> 26%
where the time goes in v5:
time: 721 us; the launch traced here: 713 us
  Pallas kernels  497 us (69%)
  matrix products  61.9 us (9%)
  other arithmetic  47.5 us (7%)
  waiting for transfers between devices  34.7 us (5%)
  starting transfers between devices  30 us (4%)
  local copies, waits for them, and re-layouts  26 us (4%)
  between operations  15.5 us (2%)
    pallas_call x1, Pallas kernels, ff_call(): pl.pallas_call(functools.partial(ff_kernel, net.order, net.cores), out_sh...  178 us
    pallas_call x1, Pallas kernels, gather_call(): pl.pallas_call(functools.partial(gather_kernel, net.order, chips, cores,...  135 us
    pallas_call x1, Pallas kernels, reduce_call(): pl.pallas_call(functools.partial(reduce_kernel, net.order, chips, cores,...  127 us
    pallas_call x2, Pallas kernels, scan_call(): pl.pallas_call(functools.partial(kernel, count), out_shape=out_shapes, in...  42.7 us
    ppermute x16, waiting for transfers between devices, shift(): return lax.ppermute(value, self.axis, pairs)  33.4 us
    ppermute x16, starting transfers between devices, shift(): return lax.ppermute(value, self.axis, pairs)  28.5 us
    dot_general x3, matrix products, dot_t(): lax.dot_general(left, right, (((1,), (1,)), ((), ())), preferred_element_...  28.4 us
    dot_general x3, matrix products, t_dot(): lax.dot_general(left, right, (((0,), (0,)), ((), ())), preferred_element_...  17 us
  transfers between devices with their start and end apart: 23, of which 7 were waited for; matrix products, arithmetic and copies ran while one was open for 16% of the time, Pallas kernels for 26%

profile of v5, /device:TPU:0, one launch (start us, length us, event | category | flops | bytes accessed | tf_op | source)
XLA Modules:
  0.0 712.7 jit_solution(7030616605687721494)
XLA Ops:
  17.2 135.1 %shard_map.322 = (bf16[4,8,64,2560]{3,2,1,0:T(8,128)(2,1)}, bf16[4,8,64,2560]{3,2,1,0:T(8,128)(2,1)}, bf16[4,8,80,2048]{3,2,1,0:T(8,128)(2,1)}, bf16[4,8,10,128]...) custom-call(bf16[64,2560]{1,0:T(8,128)(2,1)} %refs_0_.1, ...), custom_call_target="tpu_custom_call" | custom-call | bytes 69181440 | tf_op jit(solution)/shard_map/pallas_call | solution.py:386
  159.2 6.9 fusion.44
  167.1 3.0 convolution_convert_fusion.3
  170.3 9.0 %collective-permute-done.1.refs_2_ = bf16[256,2048]{1,0:T(8,128)(2,1)} collective-permute-done((bf16[256,2048]{1,0:T(8,128)(2,1)}, bf16[256,2048]{1,0:T(8,128)(2,1)}, u32[]{:S(2)}, u32[]{:S(2)}) %collective-permute-start.1) | collective-permute-done | bytes 1048608 | tf_op jit(solution)/shard_map/ppermute | solution.py:44
  185.0 4.9 shard_map.323
  189.9 22.0 %shard_map.324 = (f32[256,2560]{1,0:T(8,128)S(1)}, f32[256,2560]{1,0:T(8,128)S(1)}, f32[1,2560]{1,0:T(1,128)S(1)}) custom-call(f32[256,2560]{1,0:T(8,128)S(1)} %get-tuple-element.89.decay_ref, f32[256,2560]{1,0:T(8,128)S(1)} %get-tuple-element.90.drive_ref, f32[1,2560]{1,0:T(1,128)S(1)} %reshape.357.start_ref), custom_call_target="tpu_custom_call" | custom-call | flops 5242880 | bytes 13107200 | tf_op jit(solution)/shard_map/pallas_call | solution.py:797
  215.2 6.6 multiply_reduce_fusion.6
  221.9 12.6 %collective-permute-done.4.refs_5_ = bf16[256,2048]{1,0:T(8,128)(2,1)S(1)} collective-permute-done((bf16[256,2048]{1,0:T(8,128)(2,1)S(1)}, bf16[256,2048]{1,0:T(8,128)(2,1)S(1)}, u32[]{:S(2)}, u32[]{:S(2)}) %collective-permute-start.4) | collective-permute-done | bytes 1048608 | tf_op jit(solution)/shard_map/ppermute | solution.py:44
  238.0 6.9 collective-permute-done.6.refs_7_
  246.0 177.9 %shard_map.325 = (bf16[8,256,2048]{2,1,0:T(8,128)(2,1)}, bf16[4,512,2048]{2,1,0:T(8,128)(2,1)}, bf16[4,512,2048]{2,1,0:T(8,128)(2,1)}, bf16[2048,768]{1,0:T(8,12...) custom-call(bf16[256,2048]{1,0:T(8,128)(2,1)} %multiply_convert_fusion.1.own_ref, ...), custom_call_target="tpu_custom_call" | custom-call | flops 57982058496 | bytes 83886080 | tf_op jit(solution)/shard_map/pallas_call | solution.py:1238
  429.7 11.5 %collective-permute-start.8 = (bf16[128,2048]{1,0:T(8,128)(2,1)}, bf16[128,2048]{1,0:T(8,128)(2,1)}, u32[]{:S(2)}, u32[]{:S(2)}) collective-permute-start(bf16[128,2048]{1,0:T(8,128)(2,1)} %get-tuple-element.170), channel_id=1, source_target_pairs={{1,3},{3,5},{5,7},{7,6},{6,4},{4,2},{2,0},{0,1},{9,11},{11,13},{13... | collective-permute-start | bytes 1572872 | tf_op jit(solution)/shard_map/ppermute | solution.py:44
  446.1 11.7 %fusion.14 = (bf16[256,2560]{1,0:T(8,128)(2,1)}, bf16[256,2560]{1,0:T(8,128)(2,1)}) fusion(f32[256,2560]{1,0:T(8,128)} %copy-done.25, f32[256,2560]{1,0:T(8,128)S(1)} %copy-done.4, bf16[2560,2048]{1,0:T(8,128)(2,1)} %bitcast.178, f32[256,2048]{1,0:T(8,128)S(1)} %multiply_add_fusion), kind=kOutput, calls=%fused_computation.24 | convolution fusion | flops 2701918208 | bytes 20447232 | tf_op jit(solution)/shard_map/dot_general | solution.py:1328
  463.7 5.6 convolution_convert_fusion.1
  473.1 20.6 %shard_map.326 = (f32[256,2560]{1,0:T(8,128)S(1)}, f32[256,2560]{1,0:T(8,128)S(1)}) custom-call(f32[256,2560]{1,0:T(8,128)S(1)} %copy-done.1, f32[256,2560]{1,0:T(8,128)S(1)} %convert_element_type.310.d_state_ref, f32[256,2560]{1,0:T(8,128)S(1)} %copy-done.6), custom_call_target="tpu_custom_call" | custom-call | flops 5242880 | bytes 13107200 | tf_op jit(solution)/shard_map/pallas_call | solution.py:797
  493.8 5.6 convolution_convert_fusion.2
  499.4 4.5 fusion.32
  505.9 8.9 %fusion.73 = f32[256,2048]{1,0:T(8,128)} fusion(bf16[256,2560]{1,0:T(8,128)(2,1)S(1)} %copy-done.27, bf16[2048,2560]{1,0:T(8,128)(2,1)} %bitcast.176), kind=kOutput, calls=%fused_computation.173 | convolution fusion | flops 2684354560 | bytes 13893632 | tf_op jit(solution)/shard_map/dot_general | solution.py:1328
  514.7 9.2 %shard_map.327 = (bf16[256,2560]{1,0:T(8,128)(2,1)S(1)}, bf16[2560,512]{1,0:T(8,128)(2,1)S(1)}, f32[4,2560]{1,0:T(4,128)S(1)}) custom-call(bf16[256,2560]{1,0:T(8,128)(2,1)S(1)} %copy-done.8, bf16[2560,512]{1,0:T(8,128)(2,1)S(1)} %bitcast.156, f32[3,2560]{1,0:T(4,128)S(1)} %pad_maximum_fusion.3.vectors_ref, f32[256,1]{1,0:T(8,128)S(1)} %copy.44.reset_ref, ...), custom_call_target="tpu_custom_call" | custom-call | flops 3355443200 | bytes 15728640 | tf_op jit(solution)/shard_map/pallas_call | solution.py:872
  528.7 4.0 fusion.30
  536.2 3.6 multiply_reduce_fusion.3
  540.1 7.9 %fusion.22 = (f32[256]{0:T(256)S(1)}, bf16[2048]{0:T(1024)(128)(2,1)S(1)}, f32[256,2048]{1,0:T(8,128)S(1)}) fusion(bf16[1,256,2048]{2,1,0:T(8,128)(2,1)S(1)} %copy-done.21, f32[2048]{0:T(1024)S(1)} %reshape.370, f32[256]{0:T(256)S(1)} %add_rsqrt_fusion.1, f32[256,2048]{1,0:T(8,128)} %fusion.73, bf16[256,2560]{1,0:T(8,128)(2,1)S(1)} %get-tuple-element.175, ...), kind=kOutput, calls=%fused_computation.43 | convolution fusion | flops 2688546560 | bytes 17053696 | tf_op jit(solution)/shard_map/dot_general | solution.py:1328
  550.1 5.8 convolution_convert_fusion
  558.5 127.4 %shard_map.328 = (f32[64,2560]{1,0:T(8,128)}, f32[64,2560]{1,0:T(8,128)}, f32[80,2048]{1,0:T(8,128)}, f32[10,128]{1,0:T(8,128)}, f32[80,512]{1,0:T(8,128)}) custom-call(bf16[4,8,64,2560]{3,2,1,0:T(8,128)(2,1)} %bitcast.159, bf16[4,8,64,2560]{3,2,1,0:T(8,128)(2,1)} %bitcast.158, bf16[4,8,80,2048]{3,2,1,0:T(8,128)(2,1)} %bitcast.157, ...), custom_call_target="tpu_custom_call" | custom-call | bytes 68321280 | tf_op jit(solution)/shard_map/pallas_call | solution.py:616
  691.3 4.1 fusion.42
  (238 shorter events, 82.2 us)
Async XLA Ops:
  7.2 148.2 %copy-start.20 = (bf16[1,256,2048]{2,1,0:T(8,128)(2,1)S(1)}, bf16[1,256,2048]{2,1,0:T(8,128)(2,1)}, u32[]{:S(2)}) copy-start(bf16[1,256,2048]{2,1,0:T(8,128)(2,1)} %param.19) | copy-start | bytes 3145732
  7.2 238.8 %all-gather.4.cloned.1.call-start = ((), (), s32[]{:S(2)}) async-start(), calls=%async_computation.3 | async-start | bytes 3932160 | tf_op jit(solution)/shard_map/all_gather | solution.py:1423
  152.4 93.6 %all-gather.6.cloned.1.call-start = ((), (), s32[]{:S(2)}) async-start(), calls=%async_computation.4 | async-start | bytes 3932160 | tf_op jit(solution)/shard_map/all_gather | solution.py:1424
  153.1 92.9 %all-gather.8.cloned.1.call-start = ((), (), s32[]{:S(2)}) async-start(), calls=%async_computation.5 | async-start | bytes 3932160 | tf_op jit(solution)/shard_map/all_gather | solution.py:1425
  153.2 26.1 %collective-permute-start.1 = (bf16[256,2048]{1,0:T(8,128)(2,1)}, bf16[256,2048]{1,0:T(8,128)(2,1)}, u32[]{:S(2)}, u32[]{:S(2)}) collective-permute-start(bf16[256,2048]{1,0:T(8,128)(2,1)} %bitcast.15.refs_0_), channel_id=1, source_target_pairs={{1,0},{3,1},{5,3},{7,5},{6,7},{4,6},{2,4},{0,2},{9,8},{11,9},{13,1... | collective-permute-start | bytes 3145736 | tf_op jit(solution)/shard_map/ppermute | solution.py:44
  154.1 25.8 %collective-permute-start = (bf16[256,2048]{1,0:T(8,128)(2,1)}, bf16[256,2048]{1,0:T(8,128)(2,1)}, u32[]{:S(2)}, u32[]{:S(2)}) collective-permute-start(bf16[256,2048]{1,0:T(8,128)(2,1)} %bitcast.15.refs_0_), channel_id=1, source_target_pairs={{1,3},{3,5},{5,7},{7,6},{6,4},{4,2},{2,0},{0,1},{9,11},{11,13},{13... | collective-permute-start | bytes 3145736 | tf_op jit(solution)/shard_map/ppermute | solution.py:44
  155.3 540.1 %reduce-scatter.8.cloned.1.call-start = ((), (), s32[]{:S(2)}) async-start(), calls=%async_computation.8 | async-start | bytes 3932160 | tf_op jit(solution)/shard_map/reduce_scatter | solution.py:1492
  179.8 32.1 %collective-permute-start.2 = (bf16[256,2048]{1,0:T(8,128)(2,1)}, bf16[256,2048]{1,0:T(8,128)(2,1)S(1)}, u32[]{:S(2)}, u32[]{:S(2)}) collective-permute-start(bf16[256,2048]{1,0:T(8,128)(2,1)} %collective-permute-done.refs_1_), channel_id=1, source_target_pairs={{1,3},{3,5},{5,7},{7,6},{6,4},{4,2},{2,0},{0,1},{9,11},{11,13},{13... | collective-permute-start | bytes 3145736 | tf_op jit(solution)/shard_map/ppermute | solution.py:44
  181.0 30.9 %collective-permute-start.3 = (bf16[256,2048]{1,0:T(8,128)(2,1)}, bf16[256,2048]{1,0:T(8,128)(2,1)S(1)}, u32[]{:S(2)}, u32[]{:S(2)}) collective-permute-start(bf16[256,2048]{1,0:T(8,128)(2,1)} %collective-permute-done.1.refs_2_), channel_id=1, source_target_pairs={{1,0},{3,1},{5,3},{7,5},{6,7},{4,6},{2,4},{0,2},{9,8},{11,9},{13,1... | collective-permute-start | bytes 3145736 | tf_op jit(solution)/shard_map/ppermute | solution.py:44
  212.0 22.4 %collective-permute-start.4 = (bf16[256,2048]{1,0:T(8,128)(2,1)S(1)}, bf16[256,2048]{1,0:T(8,128)(2,1)S(1)}, u32[]{:S(2)}, u32[]{:S(2)}) collective-permute-start(bf16[256,2048]{1,0:T(8,128)(2,1)S(1)} %collective-permute-done.2.refs_3_), channel_id=1, source_target_pairs={{1,3},{3,5},{5,7},{7,6},{6,4},{4,2},{2,0},{0,1},{9,11},{11,13},{13... | collective-permute-start | bytes 3145736 | tf_op jit(solution)/shard_map/ppermute | solution.py:44
  212.8 23.0 %collective-permute-start.5 = (bf16[256,2048]{1,0:T(8,128)(2,1)S(1)}, bf16[256,2048]{1,0:T(8,128)(2,1)S(1)}, u32[]{:S(2)}, u32[]{:S(2)}) collective-permute-start(bf16[256,2048]{1,0:T(8,128)(2,1)S(1)} %collective-permute-done.3.refs_4_), channel_id=1, source_target_pairs={{1,0},{3,1},{5,3},{7,5},{6,7},{4,6},{2,4},{0,2},{9,8},{11,9},{13,1... | collective-permute-start | bytes 3145736 | tf_op jit(solution)/shard_map/ppermute | solution.py:44
  234.5 10.4 %collective-permute-start.6 = (bf16[128,2048]{1,0:T(8,128)(2,1)S(1)}, bf16[128,2048]{1,0:T(8,128)(2,1)S(1)}, u32[]{:S(2)}, u32[]{:S(2)}) collective-permute-start(bf16[128,2048]{1,0:T(8,128)(2,1)S(1)} %slice.291), channel_id=1, source_target_pairs={{1,3},{3,5},{5,7},{7,6},{6,4},{4,2},{2,0},{0,1},{9,11},{11,13},{13... | collective-permute-start | bytes 1572872 | tf_op jit(solution)/shard_map/ppermute | solution.py:44
  235.9 10.1 %collective-permute-start.7 = (bf16[128,2048]{1,0:T(8,128)(2,1)S(1)}, bf16[128,2048]{1,0:T(8,128)(2,1)}, u32[]{:S(2)}, u32[]{:S(2)}) collective-permute-start(bf16[128,2048]{1,0:T(8,128)(2,1)S(1)} %slice.292), channel_id=1, source_target_pairs={{1,0},{3,1},{5,3},{7,5},{6,7},{4,6},{2,4},{0,2},{9,8},{11,9},{13,1... | collective-permute-start | bytes 1572872 | tf_op jit(solution)/shard_map/ppermute | solution.py:44
  424.0 274.0 %reduce-scatter.6.cloned.1.call-start = ((), (), s32[]{:S(2)}) async-start(), calls=%async_computation.7 | async-start | bytes 3932160 | tf_op jit(solution)/shard_map/reduce_scatter | solution.py:1492
  424.5 275.9 %reduce-scatter.4.cloned.1.call-start = ((), (), s32[]{:S(2)}) async-start(), calls=%async_computation.6 | async-start | bytes 3932160 | tf_op jit(solution)/shard_map/reduce_scatter | solution.py:1492
  428.5 29.2 %collective-permute-start.9 = (bf16[128,2048]{1,0:T(8,128)(2,1)}, bf16[128,2048]{1,0:T(8,128)(2,1)S(1)}, u32[]{:S(2)}, u32[]{:S(2)}) collective-permute-start(bf16[128,2048]{1,0:T(8,128)(2,1)} %get-tuple-element.169), channel_id=1, source_target_pairs={{1,0},{3,1},{5,3},{7,5},{6,7},{4,6},{2,4},{0,2},{9,8},{11,9},{13,1... | collective-permute-start | bytes 1572872 | tf_op jit(solution)/shard_map/ppermute | solution.py:44
  429.7 28.1 %collective-permute-start.8 = (bf16[128,2048]{1,0:T(8,128)(2,1)}, bf16[128,2048]{1,0:T(8,128)(2,1)}, u32[]{:S(2)}, u32[]{:S(2)}) collective-permute-start(bf16[128,2048]{1,0:T(8,128)(2,1)} %get-tuple-element.170), channel_id=1, source_target_pairs={{1,3},{3,5},{5,7},{7,6},{6,4},{4,2},{2,0},{0,1},{9,11},{11,13},{13... | collective-permute-start | bytes 1572872 | tf_op jit(solution)/shard_map/ppermute | solution.py:44
  460.6 38.8 %collective-permute-start.10 = (bf16[256,2048]{1,0:T(8,128)(2,1)}, bf16[256,2048]{1,0:T(8,128)(2,1)}, u32[]{:S(2)}, u32[]{:S(2)}) collective-permute-start(bf16[256,2048]{1,0:T(8,128)(2,1)} %pad_maximum_fusion), channel_id=1, source_target_pairs={{1,3},{3,5},{5,7},{7,6},{6,4},{4,2},{2,0},{0,1},{9,11},{11,13},{13... | collective-permute-start | bytes 3145736 | tf_op jit(solution)/shard_map/ppermute | solution.py:44
  462.8 36.6 %collective-permute-start.11 = (bf16[256,2048]{1,0:T(8,128)(2,1)}, bf16[256,2048]{1,0:T(8,128)(2,1)}, u32[]{:S(2)}, u32[]{:S(2)}) collective-permute-start(bf16[256,2048]{1,0:T(8,128)(2,1)} %pad_maximum_fusion.1), channel_id=1, source_target_pairs={{1,0},{3,1},{5,3},{7,5},{6,7},{4,6},{2,4},{0,2},{9,8},{11,9},{13,1... | collective-permute-start | bytes 3145736 | tf_op jit(solution)/shard_map/ppermute | solution.py:44
  503.8 22.1 %collective-permute-start.13 = (bf16[256,2048]{1,0:T(8,128)(2,1)}, bf16[256,2048]{1,0:T(8,128)(2,1)S(1)}, u32[]{:S(2)}, u32[]{:S(2)}) collective-permute-start(bf16[256,2048]{1,0:T(8,128)(2,1)} %get-tuple-element.165), channel_id=1, source_target_pairs={{1,0},{3,1},{5,3},{7,5},{6,7},{4,6},{2,4},{0,2},{9,8},{11,9},{13,1... | collective-permute-start | bytes 3145736 | tf_op jit(solution)/shard_map/ppermute | solution.py:44
  504.8 22.6 %collective-permute-start.12 = (bf16[256,2048]{1,0:T(8,128)(2,1)}, bf16[256,2048]{1,0:T(8,128)(2,1)}, u32[]{:S(2)}, u32[]{:S(2)}) collective-permute-start(bf16[256,2048]{1,0:T(8,128)(2,1)} %get-tuple-element.166), channel_id=1, source_target_pairs={{1,3},{3,5},{5,7},{7,6},{6,4},{4,2},{2,0},{0,1},{9,11},{11,13},{13... | collective-permute-start | bytes 3145736 | tf_op jit(solution)/shard_map/ppermute | solution.py:44
  527.4 8.4 %collective-permute-start.14 = (bf16[3,2560]{1,0:T(4,128)(2,1)S(1)}, bf16[3,2560]{1,0:T(4,128)(2,1)S(1)}, u32[]{:S(2)}, u32[]{:S(2)}) collective-permute-start(bf16[3,2560]{1,0:T(4,128)(2,1)S(1)} %slice.253), channel_id=1, source_target_pairs={{1,0},{2,1},{3,2},{4,3},{5,4},{6,5},{7,6},{9,8},{10,9},{11,10},{12... | collective-permute-start | bytes 46088 | tf_op jit(solution)/shard_map/ppermute | solution.py:1297
  532.7 23.2 %collective-permute-start.16 = (bf16[256,2048]{1,0:T(8,128)(2,1)}, bf16[256,2048]{1,0:T(8,128)(2,1)}, u32[]{:S(2)}, u32[]{:S(2)}) collective-permute-start(bf16[256,2048]{1,0:T(8,128)(2,1)} %get-tuple-element.163), channel_id=1, source_target_pairs={{1,0},{3,1},{5,3},{7,5},{6,7},{4,6},{2,4},{0,2},{9,8},{11,9},{13,1... | collective-permute-start | bytes 3145736 | tf_op jit(solution)/shard_map/ppermute | solution.py:44
  535.6 22.1 %collective-permute-start.15 = (bf16[256,2048]{1,0:T(8,128)(2,1)S(1)}, bf16[256,2048]{1,0:T(8,128)(2,1)}, u32[]{:S(2)}, u32[]{:S(2)}) collective-permute-start(bf16[256,2048]{1,0:T(8,128)(2,1)S(1)} %get-tuple-element.164), channel_id=1, source_target_pairs={{1,3},{3,5},{5,7},{7,6},{6,4},{4,2},{2,0},{0,1},{9,11},{11,13},{13... | collective-permute-start | bytes 3145736 | tf_op jit(solution)/shard_map/ppermute | solution.py:44
  (45 other events, 358.6 us)
Sparse Core Ops, SparseCore 0:
  152.5 28.2 all-gather.3
  182.3 28.5 all-gather.5
  212.5 28.5 all-gather.7
  424.1 36.1 reduce-scatter.7
  462.8 37.9 reduce-scatter.5
  503.2 37.9 reduce-scatter.3

commit v6 on v5

--- a/solution.py
+++ b/solution.py
@@ -74,20 +74,19 @@
     def scatter_steps(self, part):
         count, half = self.count, self.count // 2
         if count == 1:
-            return part(0).astype(f32)
+            return []
         far = part(half).astype(bf16)
         if half == 1:
-            (got,) = yield [self.shift(far, 1)]
-            return part(0).astype(f32) + got.astype(f32)
+            return (yield [self.shift(far, 1)])
         rows = far.shape[0]
         assert rows % 2 == 0
         cut = rows // 2
         ahead, behind = far[:cut], far[cut:]
         for k in range(half - 1, -1, -1):
             got_ahead, got_behind = yield [self.shift(ahead, 1), self.shift(behind, -1)]
+            if k == 0:
+                return [got_ahead, got_behind]
             got_ahead, got_behind = got_ahead.astype(f32), got_behind.astype(f32)
-            if k == 0:
-                return part(0).astype(f32) + got_ahead + got_behind
             ahead, behind = part(k).astype(f32), part(count - k).astype(f32)
             if k == half - 1:
                 ahead = jnp.concatenate([ahead[:cut] + got_ahead, ahead[cut:]], 0)
@@ -1291,6 +1290,34 @@
     )(own, slab_gate, slab_up, slab_down, *cots)
 
 
+def result_kernel(arrived, *refs):
+    ins, outs = refs[: 5 + arrived], refs[5 + arrived :]
+    for source, target in zip(ins[:3], outs[:3]):
+        target[...] = source[...].astype(f32)
+    terms = [ins[3][0]] + [ref[...] for ref in ins[4 : 4 + arrived]]
+    outs[3][...] = (ins[4 + arrived][...] + total([term.astype(f32) for term in terms])).astype(bf16)
+
+
+def result_call(grads, out_part, arrived, residual):
+    parts = 4
+    rows, width = residual.shape
+    pair = out_part.shape[0] - 1
+
+    def cut(v):
+        return pl.BlockSpec((v.shape[0] // parts, v.shape[1]), lambda i: (i, 0))
+
+    own = pl.BlockSpec((1, rows // parts, width), lambda i: (pair, parts + i, 0))
+    return pl.pallas_call(
+        functools.partial(result_kernel, len(arrived)),
+        grid=(parts,),
+        out_shape=[jax.ShapeDtypeStruct(v.shape, f32) for v in grads]
+        + [jax.ShapeDtypeStruct(residual.shape, bf16)],
+        in_specs=[cut(v) for v in grads] + [own] + [cut(v) for v in arrived] + [cut(residual)],
+        out_specs=[cut(v) for v in grads] + [cut(residual)],
+        compiler_params=pltpu.CompilerParams(vmem_limit_bytes=60 * 2**20),
+    )(*grads, out_part, *arrived, residual)
+
+
 def passed_along(value, axis, steps):
     count = lax.axis_size(axis)
     first, last = (max(0, -steps), min(count, count - steps))
@@ -1368,7 +1395,14 @@
         return jnp.pad(rows, ((0, 0),) * (rows.ndim - 1) + ((0, LINE - rows.shape[-1]),))
 
     vectors = [norm1_gain, norm2_gain, conv_w, conv_bias, rgate_bias, igate_bias, decay_param]
-    small = jnp.concatenate([lanes(v.reshape(-1, v.shape[-1])) for v in vectors], 0)
+    small_rows = 6 + taps
+    small, at_row = None, 0
+    for v in vectors:
+        v = v.reshape(-1, v.shape[-1])
+        below = small_rows - at_row - v.shape[0]
+        placed = lax.pad(v, jnp.zeros((), bf16), ((at_row, below, 0), (0, LINE - v.shape[1], 0)))
+        small = placed if small is None else small + placed
+        at_row += v.shape[0]
     rim_inputs = inputs.reshape(rows_here, width)[rows_here - rim_rows :]
     full_in, full_gate, full_out, small_all, full_both, start_state, rims, flags = gather_call(
         net,
@@ -1489,7 +1523,7 @@
     )
     out_flow = Flow(net.seq.scatter_steps(block_rows(out_part)))
     grad_ffgate, grad_ffup, grad_ffdown = (
-        lax.psum_scatter(part, "dp", scatter_dimension=axis, tiled=True).astype(f32)
+        lax.psum_scatter(part, "dp", scatter_dimension=axis, tiled=True)
         for part, axis in ((gate_part, 0), (up_part, 0), (down_part, 1))
     )
 
@@ -1497,7 +1531,7 @@
     d_residual = cotan_rows.astype(f32) + d_resid_norm
     d_residual_low = d_residual.astype(bf16)
     d_mixed = dot_t(d_residual_low, full_out)
-    d_state = (d_mixed * gate_act).astype(bf16)
+    d_state = (d_mixed * gate_act).astype(bf16).astype(f32)
     d_gate_pre = gate_back(d_mixed * state_f)[0].astype(bf16)
     d_state, d_gate_pre = beside((d_state, d_gate_pre), out_flow)
 
@@ -1509,7 +1543,7 @@
         scan_back_kernel,
         1,
         seq_count,
-        (decay_rows, d_state.astype(f32), prev_states),
+        (decay_rows, d_state, prev_states),
         [row_shape, row_shape],
     )
     d_drive, d_decay, gate_terms = beside((d_drive, d_decay, gate_terms), out_flow)
@@ -1551,8 +1585,7 @@
     input_grad = (d_residual + d_token_norm).reshape(seqs_here, len_here, width)
 
     grad_norm1, input_grad = beside((grad_norm1, input_grad), out_flow)
-    ff_out = out_flow.finish()
-    output = (residual + ff_out).astype(bf16).reshape(seqs_here, len_here, width)
+    arrived = out_flow.finish()
 
     small_grads = [
         lanes(v.reshape(-1, devices, v.shape[-1] // devices).transpose(1, 0, 2)).astype(bf16)
@@ -1580,6 +1613,11 @@
             (0, 0, wide_here, CHIP_FIRST),
         ],
     )
+    ff_grads, arrived, grad_in = lax.optimization_barrier(
+        ((grad_ffgate, grad_ffup, grad_ffdown), arrived, grad_in)
+    )
+    grad_ffgate, grad_ffup, grad_ffdown, output = result_call(ff_grads, out_part, arrived, residual)
+    output = output.reshape(seqs_here, len_here, width)
     mine = [small_mine[i, :wide_here] for i in range(2)]
     mine += [small_mine[2 : 2 + taps, :chan_here]]
     mine += [small_mine[i, :chan_here] for i in range(2 + taps, 6 + taps)]

time: 721 us -> 711 us (0.986)
  other arithmetic: 47.5 us -> 35.7 us
    convert_element_type x4 -> x0, other arithmetic: 9.42 us -> none  [the longest x3 7.43 us: per_device(): lax.psum_scatter(part, 'dp', scatter_dimension=axis, tiled=True).astype(f32)]
  transfers between devices with their start and end apart: 23 -> 23, of which waited for: 7 -> 7; matrix products, arithmetic and copies ran while one was open for 16% -> 15% of each run, Pallas kernels for 26% -> 26%
where the time goes in v6:
time: 711 us; the launch traced here: 703 us
  Pallas kernels  501 us (70%)
  matrix products  61.4 us (9%)
  other arithmetic  35.7 us (5%)
  waiting for transfers between devices  34.7 us (5%)
  starting transfers between devices  30 us (4%)
  local copies, waits for them, and re-layouts  25 us (4%)
  between operations  15.4 us (2%)
    pallas_call x1, Pallas kernels, ff_call(): pl.pallas_call(functools.partial(ff_kernel, net.order, net.cores), out_sh...  178 us
    pallas_call x1, Pallas kernels, gather_call(): pl.pallas_call(functools.partial(gather_kernel, net.order, chips, cores,...  135 us
    pallas_call x1, Pallas kernels, reduce_call(): pl.pallas_call(functools.partial(reduce_kernel, net.order, chips, cores,...  127 us
    pallas_call x2, Pallas kernels, scan_call(): pl.pallas_call(functools.partial(kernel, count), out_shape=out_shapes, in...  40.6 us
    ppermute x16, waiting for transfers between devices, shift(): return lax.ppermute(value, self.axis, pairs)  33.4 us
    ppermute x16, starting transfers between devices, shift(): return lax.ppermute(value, self.axis, pairs)  28.4 us
    dot_general x3, matrix products, dot_t(): lax.dot_general(left, right, (((1,), (1,)), ((), ())), preferred_element_...  28 us
    dot_general x3, matrix products, t_dot(): lax.dot_general(left, right, (((0,), (0,)), ((), ())), preferred_element_...  16.9 us
  transfers between devices with their start and end apart: 23, of which 7 were waited for; matrix products, arithmetic and copies ran while one was open for 15% of the time, Pallas kernels for 26%

profile of v6, /device:TPU:0, one launch (start us, length us, event | category | flops | bytes accessed | tf_op | source)
XLA Modules:
  0.0 702.8 jit_solution(11716834730429537687)
XLA Ops:
  12.8 135.1 %shard_map.322 = (bf16[4,8,64,2560]{3,2,1,0:T(8,128)(2,1)}, bf16[4,8,64,2560]{3,2,1,0:T(8,128)(2,1)}, bf16[4,8,80,2048]{3,2,1,0:T(8,128)(2,1)}, bf16[4,8,10,128]...) custom-call(bf16[64,2560]{1,0:T(8,128)(2,1)} %refs_0_.1, ...), custom_call_target="tpu_custom_call" | custom-call | bytes 69181440 | tf_op jit(solution)/shard_map/pallas_call | solution.py:385
  154.8 6.9 fusion.41
  162.6 3.0 convolution_convert_fusion.3
  165.8 9.0 %collective-permute-done.1.refs_2_ = bf16[256,2048]{1,0:T(8,128)(2,1)} collective-permute-done((bf16[256,2048]{1,0:T(8,128)(2,1)}, bf16[256,2048]{1,0:T(8,128)(2,1)}, u32[]{:S(2)}, u32[]{:S(2)}) %collective-permute-start.1) | collective-permute-done | bytes 1048608 | tf_op jit(solution)/shard_map/ppermute | solution.py:44
  180.5 4.9 shard_map.323
  185.4 22.0 %shard_map.324 = (f32[256,2560]{1,0:T(8,128)S(1)}, f32[256,2560]{1,0:T(8,128)S(1)}, f32[1,2560]{1,0:T(1,128)S(1)}) custom-call(f32[256,2560]{1,0:T(8,128)S(1)} %get-tuple-element.99.decay_ref, f32[256,2560]{1,0:T(8,128)S(1)} %get-tuple-element.100.drive_ref, f32[1,2560]{1,0:T(1,128)S(1)} %reshape.355.start_ref), custom_call_target="tpu_custom_call" | custom-call | flops 5242880 | bytes 13107200 | tf_op jit(solution)/shard_map/pallas_call | solution.py:796
  210.8 6.6 multiply_reduce_fusion.6
  217.4 12.6 %collective-permute-done.4.refs_5_ = bf16[256,2048]{1,0:T(8,128)(2,1)S(1)} collective-permute-done((bf16[256,2048]{1,0:T(8,128)(2,1)S(1)}, bf16[256,2048]{1,0:T(8,128)(2,1)S(1)}, u32[]{:S(2)}, u32[]{:S(2)}) %collective-permute-start.4) | collective-permute-done | bytes 1048608 | tf_op jit(solution)/shard_map/ppermute | solution.py:44
  233.5 6.9 collective-permute-done.6.refs_7_
  241.6 177.9 %shard_map.325 = (bf16[8,256,2048]{2,1,0:T(8,128)(2,1)}, bf16[4,512,2048]{2,1,0:T(8,128)(2,1)}, bf16[4,512,2048]{2,1,0:T(8,128)(2,1)}, bf16[2048,768]{1,0:T(8,12...) custom-call(bf16[256,2048]{1,0:T(8,128)(2,1)} %multiply_convert_fusion.1.own_ref, ...), custom_call_target="tpu_custom_call" | custom-call | flops 57982058496 | bytes 83886080 | tf_op jit(solution)/shard_map/pallas_call | solution.py:1237
  425.2 11.5 %collective-permute-start.8 = (bf16[128,2048]{1,0:T(8,128)(2,1)}, bf16[128,2048]{1,0:T(8,128)(2,1)}, u32[]{:S(2)}, u32[]{:S(2)}) collective-permute-start(bf16[128,2048]{1,0:T(8,128)(2,1)} %get-tuple-element.190), channel_id=1, source_target_pairs={{1,3},{3,5},{5,7},{7,6},{6,4},{4,2},{2,0},{0,1},{9,11},{11,13},{13... | collective-permute-start | bytes 1572872 | tf_op jit(solution)/shard_map/ppermute | solution.py:44
  442.4 11.1 %fusion.14 = (bf16[256,2560]{1,0:T(8,128)(2,1)}, f32[256,2560]{1,0:T(8,128)}) fusion(f32[256,2560]{1,0:T(8,128)S(1)} %copy-done.27, f32[256,2560]{1,0:T(8,128)S(1)} %copy-done.4, bf16[2560,2048]{1,0:T(8,128)(2,1)} %bitcast.177, f32[256,2048]{1,0:T(8,128)S(1)} %multiply_add_fusion), kind=kOutput, calls=%fused_computation.24 | convolution fusion | flops 2702573568 | bytes 21757952 | tf_op jit(solution)/shard_map/dot_general | solution.py:1355
  459.6 5.6 convolution_convert_fusion.1
  471.2 18.6 %shard_map.326 = (f32[256,2560]{1,0:T(8,128)S(1)}, f32[256,2560]{1,0:T(8,128)S(1)}) custom-call(f32[256,2560]{1,0:T(8,128)S(1)} %copy-done.1, f32[256,2560]{1,0:T(8,128)S(1)} %copy-done.7, f32[256,2560]{1,0:T(8,128)S(1)} %copy-done.6), custom_call_target="tpu_custom_call" | custom-call | flops 5242880 | bytes 13107200 | tf_op jit(solution)/shard_map/pallas_call | solution.py:796
  489.8 5.7 convolution_convert_fusion.2
  495.4 4.5 fusion.32
  501.9 9.1 %fusion.70 = f32[256,2048]{1,0:T(8,128)} fusion(bf16[256,2560]{1,0:T(8,128)(2,1)S(1)} %copy-done.29, bf16[2048,2560]{1,0:T(8,128)(2,1)} %bitcast.175), kind=kOutput, calls=%fused_computation.169 | convolution fusion | flops 2684354560 | bytes 13893632 | tf_op jit(solution)/shard_map/dot_general | solution.py:1355
  511.0 9.2 %shard_map.327 = (bf16[256,2560]{1,0:T(8,128)(2,1)S(1)}, bf16[2560,512]{1,0:T(8,128)(2,1)S(1)}, f32[4,2560]{1,0:T(4,128)S(1)}) custom-call(bf16[256,2560]{1,0:T(8,128)(2,1)S(1)} %copy-done.9, bf16[2560,512]{1,0:T(8,128)(2,1)S(1)} %bitcast.150, f32[3,2560]{1,0:T(4,128)S(1)} %pad_maximum_fusion.3.vectors_ref, f32[256,1]{1,0:T(8,128)S(1)} %copy.44.reset_ref, ...), custom_call_target="tpu_custom_call" | custom-call | flops 3355443200 | bytes 15728640 | tf_op jit(solution)/shard_map/pallas_call | solution.py:871
  524.7 4.0 fusion.30
  532.2 3.6 multiply_reduce_fusion.3
  536.1 7.8 %fusion.22 = (f32[256]{0:T(256)S(1)}, bf16[2048]{0:T(1024)(128)(2,1)S(1)}, f32[256,2048]{1,0:T(8,128)S(1)}) fusion(bf16[1,256,2048]{2,1,0:T(8,128)(2,1)S(1)} %copy-done.22, f32[2048]{0:T(1024)S(1)} %reshape.368, f32[256]{0:T(256)S(1)} %add_rsqrt_fusion.1, f32[256,2048]{1,0:T(8,128)} %fusion.70, bf16[256,2560]{1,0:T(8,128)(2,1)S(1)} %get-tuple-element.195, ...), kind=kOutput, calls=%fused_computation.43 | convolution fusion | flops 2688546560 | bytes 17053696 | tf_op jit(solution)/shard_map/dot_general | solution.py:1355
  546.1 5.6 convolution_convert_fusion
  554.5 127.0 %shard_map.328 = (f32[64,2560]{1,0:T(8,128)}, f32[64,2560]{1,0:T(8,128)}, f32[80,2048]{1,0:T(8,128)}, f32[10,128]{1,0:T(8,128)}, f32[80,512]{1,0:T(8,128)}) custom-call(bf16[4,8,64,2560]{3,2,1,0:T(8,128)(2,1)} %bitcast.153, bf16[4,8,64,2560]{3,2,1,0:T(8,128)(2,1)} %bitcast.152, bf16[4,8,80,2048]{3,2,1,0:T(8,128)(2,1)} %bitcast.151, ...), custom_call_target="tpu_custom_call" | custom-call | bytes 68321280 | tf_op jit(solution)/shard_map/pallas_call | solution.py:615
  687.0 6.0 shard_map.329
  (231 shorter events, 73.4 us)
Async XLA Ops:
  7.2 143.7 %copy-start.21 = (bf16[1,256,2048]{2,1,0:T(8,128)(2,1)S(1)}, bf16[1,256,2048]{2,1,0:T(8,128)(2,1)}, u32[]{:S(2)}) copy-start(bf16[1,256,2048]{2,1,0:T(8,128)(2,1)} %param.19) | copy-start | bytes 3145732
  7.2 234.3 %all-gather.4.cloned.1.call-start = ((), (), s32[]{:S(2)}) async-start(), calls=%async_computation.3 | async-start | bytes 3932160 | tf_op jit(solution)/shard_map/all_gather | solution.py:1457
  147.9 93.6 %all-gather.6.cloned.1.call-start = ((), (), s32[]{:S(2)}) async-start(), calls=%async_computation.4 | async-start | bytes 3932160 | tf_op jit(solution)/shard_map/all_gather | solution.py:1458
  148.7 92.9 %all-gather.8.cloned.1.call-start = ((), (), s32[]{:S(2)}) async-start(), calls=%async_computation.5 | async-start | bytes 3932160 | tf_op jit(solution)/shard_map/all_gather | solution.py:1459
  148.7 26.1 %collective-permute-start.1 = (bf16[256,2048]{1,0:T(8,128)(2,1)}, bf16[256,2048]{1,0:T(8,128)(2,1)}, u32[]{:S(2)}, u32[]{:S(2)}) collective-permute-start(bf16[256,2048]{1,0:T(8,128)(2,1)} %bitcast.15.refs_0_), channel_id=1, source_target_pairs={{1,0},{3,1},{5,3},{7,5},{6,7},{4,6},{2,4},{0,2},{9,8},{11,9},{13,1... | collective-permute-start | bytes 3145736 | tf_op jit(solution)/shard_map/ppermute | solution.py:44
  149.6 25.8 %collective-permute-start = (bf16[256,2048]{1,0:T(8,128)(2,1)}, bf16[256,2048]{1,0:T(8,128)(2,1)}, u32[]{:S(2)}, u32[]{:S(2)}) collective-permute-start(bf16[256,2048]{1,0:T(8,128)(2,1)} %bitcast.15.refs_0_), channel_id=1, source_target_pairs={{1,3},{3,5},{5,7},{7,6},{6,4},{4,2},{2,0},{0,1},{9,11},{11,13},{13... | collective-permute-start | bytes 3145736 | tf_op jit(solution)/shard_map/ppermute | solution.py:44
  150.8 536.2 %reduce-scatter.4.cloned.1.call-start = ((), (), s32[]{:S(2)}) async-start(), calls=%async_computation.6 | async-start | bytes 3932160 | tf_op jit(solution)/shard_map/reduce_scatter | solution.py:1526
  175.3 32.1 %collective-permute-start.2 = (bf16[256,2048]{1,0:T(8,128)(2,1)}, bf16[256,2048]{1,0:T(8,128)(2,1)S(1)}, u32[]{:S(2)}, u32[]{:S(2)}) collective-permute-start(bf16[256,2048]{1,0:T(8,128)(2,1)} %collective-permute-done.refs_1_), channel_id=1, source_target_pairs={{1,3},{3,5},{5,7},{7,6},{6,4},{4,2},{2,0},{0,1},{9,11},{11,13},{13... | collective-permute-start | bytes 3145736 | tf_op jit(solution)/shard_map/ppermute | solution.py:44
  176.5 30.9 %collective-permute-start.3 = (bf16[256,2048]{1,0:T(8,128)(2,1)}, bf16[256,2048]{1,0:T(8,128)(2,1)S(1)}, u32[]{:S(2)}, u32[]{:S(2)}) collective-permute-start(bf16[256,2048]{1,0:T(8,128)(2,1)} %collective-permute-done.1.refs_2_), channel_id=1, source_target_pairs={{1,0},{3,1},{5,3},{7,5},{6,7},{4,6},{2,4},{0,2},{9,8},{11,9},{13,1... | collective-permute-start | bytes 3145736 | tf_op jit(solution)/shard_map/ppermute | solution.py:44
  207.5 22.4 %collective-permute-start.4 = (bf16[256,2048]{1,0:T(8,128)(2,1)S(1)}, bf16[256,2048]{1,0:T(8,128)(2,1)S(1)}, u32[]{:S(2)}, u32[]{:S(2)}) collective-permute-start(bf16[256,2048]{1,0:T(8,128)(2,1)S(1)} %collective-permute-done.2.refs_3_), channel_id=1, source_target_pairs={{1,3},{3,5},{5,7},{7,6},{6,4},{4,2},{2,0},{0,1},{9,11},{11,13},{13... | collective-permute-start | bytes 3145736 | tf_op jit(solution)/shard_map/ppermute | solution.py:44
  208.3 23.0 %collective-permute-start.5 = (bf16[256,2048]{1,0:T(8,128)(2,1)S(1)}, bf16[256,2048]{1,0:T(8,128)(2,1)S(1)}, u32[]{:S(2)}, u32[]{:S(2)}) collective-permute-start(bf16[256,2048]{1,0:T(8,128)(2,1)S(1)} %collective-permute-done.3.refs_4_), channel_id=1, source_target_pairs={{1,0},{3,1},{5,3},{7,5},{6,7},{4,6},{2,4},{0,2},{9,8},{11,9},{13,1... | collective-permute-start | bytes 3145736 | tf_op jit(solution)/shard_map/ppermute | solution.py:44
  230.0 10.4 %collective-permute-start.6 = (bf16[128,2048]{1,0:T(8,128)(2,1)S(1)}, bf16[128,2048]{1,0:T(8,128)(2,1)S(1)}, u32[]{:S(2)}, u32[]{:S(2)}) collective-permute-start(bf16[128,2048]{1,0:T(8,128)(2,1)S(1)} %slice.287), channel_id=1, source_target_pairs={{1,3},{3,5},{5,7},{7,6},{6,4},{4,2},{2,0},{0,1},{9,11},{11,13},{13... | collective-permute-start | bytes 1572872 | tf_op jit(solution)/shard_map/ppermute | solution.py:44
  231.4 10.1 %collective-permute-start.7 = (bf16[128,2048]{1,0:T(8,128)(2,1)S(1)}, bf16[128,2048]{1,0:T(8,128)(2,1)}, u32[]{:S(2)}, u32[]{:S(2)}) collective-permute-start(bf16[128,2048]{1,0:T(8,128)(2,1)S(1)} %slice.288), channel_id=1, source_target_pairs={{1,0},{3,1},{5,3},{7,5},{6,7},{4,6},{2,4},{0,2},{9,8},{11,9},{13,1... | collective-permute-start | bytes 1572872 | tf_op jit(solution)/shard_map/ppermute | solution.py:44
  419.5 267.5 %reduce-scatter.6.cloned.1.call-start = ((), (), s32[]{:S(2)}) async-start(), calls=%async_computation.7 | async-start | bytes 3932160 | tf_op jit(solution)/shard_map/reduce_scatter | solution.py:1526
  420.1 267.0 %reduce-scatter.8.cloned.1.call-start = ((), (), s32[]{:S(2)}) async-start(), calls=%async_computation.8 | async-start | bytes 3932160 | tf_op jit(solution)/shard_map/reduce_scatter | solution.py:1526
  424.1 29.4 %collective-permute-start.9 = (bf16[128,2048]{1,0:T(8,128)(2,1)}, bf16[128,2048]{1,0:T(8,128)(2,1)}, u32[]{:S(2)}, u32[]{:S(2)}) collective-permute-start(bf16[128,2048]{1,0:T(8,128)(2,1)} %get-tuple-element.189), channel_id=1, source_target_pairs={{1,0},{3,1},{5,3},{7,5},{6,7},{4,6},{2,4},{0,2},{9,8},{11,9},{13,1... | collective-permute-start | bytes 1572872 | tf_op jit(solution)/shard_map/ppermute | solution.py:44
  425.2 28.3 %collective-permute-start.8 = (bf16[128,2048]{1,0:T(8,128)(2,1)}, bf16[128,2048]{1,0:T(8,128)(2,1)}, u32[]{:S(2)}, u32[]{:S(2)}) collective-permute-start(bf16[128,2048]{1,0:T(8,128)(2,1)} %get-tuple-element.190), channel_id=1, source_target_pairs={{1,3},{3,5},{5,7},{7,6},{6,4},{4,2},{2,0},{0,1},{9,11},{11,13},{13... | collective-permute-start | bytes 1572872 | tf_op jit(solution)/shard_map/ppermute | solution.py:44
  456.5 38.9 %collective-permute-start.10 = (bf16[256,2048]{1,0:T(8,128)(2,1)}, bf16[256,2048]{1,0:T(8,128)(2,1)}, u32[]{:S(2)}, u32[]{:S(2)}) collective-permute-start(bf16[256,2048]{1,0:T(8,128)(2,1)} %pad_maximum_fusion), channel_id=1, source_target_pairs={{1,3},{3,5},{5,7},{7,6},{6,4},{4,2},{2,0},{0,1},{9,11},{11,13},{13... | collective-permute-start | bytes 3145736 | tf_op jit(solution)/shard_map/ppermute | solution.py:44
  458.8 36.7 %collective-permute-start.11 = (bf16[256,2048]{1,0:T(8,128)(2,1)}, bf16[256,2048]{1,0:T(8,128)(2,1)}, u32[]{:S(2)}, u32[]{:S(2)}) collective-permute-start(bf16[256,2048]{1,0:T(8,128)(2,1)} %pad_maximum_fusion.1), channel_id=1, source_target_pairs={{1,0},{3,1},{5,3},{7,5},{6,7},{4,6},{2,4},{0,2},{9,8},{11,9},{13,1... | collective-permute-start | bytes 3145736 | tf_op jit(solution)/shard_map/ppermute | solution.py:44
  499.9 22.3 %collective-permute-start.13 = (bf16[256,2048]{1,0:T(8,128)(2,1)}, bf16[256,2048]{1,0:T(8,128)(2,1)S(1)}, u32[]{:S(2)}, u32[]{:S(2)}) collective-permute-start(bf16[256,2048]{1,0:T(8,128)(2,1)} %get-tuple-element.185), channel_id=1, source_target_pairs={{1,0},{3,1},{5,3},{7,5},{6,7},{4,6},{2,4},{0,2},{9,8},{11,9},{13,1... | collective-permute-start | bytes 3145736 | tf_op jit(solution)/shard_map/ppermute | solution.py:44
  500.9 22.5 %collective-permute-start.12 = (bf16[256,2048]{1,0:T(8,128)(2,1)}, bf16[256,2048]{1,0:T(8,128)(2,1)}, u32[]{:S(2)}, u32[]{:S(2)}) collective-permute-start(bf16[256,2048]{1,0:T(8,128)(2,1)} %get-tuple-element.186), channel_id=1, source_target_pairs={{1,3},{3,5},{5,7},{7,6},{6,4},{4,2},{2,0},{0,1},{9,11},{11,13},{13... | collective-permute-start | bytes 3145736 | tf_op jit(solution)/shard_map/ppermute | solution.py:44
  523.4 8.4 %collective-permute-start.14 = (bf16[3,2560]{1,0:T(4,128)(2,1)S(1)}, bf16[3,2560]{1,0:T(4,128)(2,1)S(1)}, u32[]{:S(2)}, u32[]{:S(2)}) collective-permute-start(bf16[3,2560]{1,0:T(4,128)(2,1)S(1)} %slice.249), channel_id=1, source_target_pairs={{1,0},{2,1},{3,2},{4,3},{5,4},{6,5},{7,6},{9,8},{10,9},{11,10},{12... | collective-permute-start | bytes 46088 | tf_op jit(solution)/shard_map/ppermute | solution.py:1324
  528.7 23.0 %collective-permute-start.16 = (bf16[256,2048]{1,0:T(8,128)(2,1)}, bf16[256,2048]{1,0:T(8,128)(2,1)}, u32[]{:S(2)}, u32[]{:S(2)}) collective-permute-start(bf16[256,2048]{1,0:T(8,128)(2,1)} %get-tuple-element.183), channel_id=1, source_target_pairs={{1,0},{3,1},{5,3},{7,5},{6,7},{4,6},{2,4},{0,2},{9,8},{11,9},{13,1... | collective-permute-start | bytes 3145736 | tf_op jit(solution)/shard_map/ppermute | solution.py:44
  531.6 22.1 %collective-permute-start.15 = (bf16[256,2048]{1,0:T(8,128)(2,1)S(1)}, bf16[256,2048]{1,0:T(8,128)(2,1)}, u32[]{:S(2)}, u32[]{:S(2)}) collective-permute-start(bf16[256,2048]{1,0:T(8,128)(2,1)S(1)} %get-tuple-element.184), channel_id=1, source_target_pairs={{1,3},{3,5},{5,7},{7,6},{6,4},{4,2},{2,0},{0,1},{9,11},{11,13},{13... | collective-permute-start | bytes 3145736 | tf_op jit(solution)/shard_map/ppermute | solution.py:44
  (47 other events, 356.1 us)
Sparse Core Ops, SparseCore 0:
  148.0 28.2 all-gather.3
  177.8 28.5 all-gather.5
  208.0 28.5 all-gather.7
  419.6 36.1 reduce-scatter.3
  458.3 37.9 reduce-scatter.5
  498.7 37.9 reduce-scatter.7
